TPU v7x, 512 devices: a whole 4x8x8 slice. The times are simulated.
512 devices in a mesh: sub: 8 (over z), row: 4 (over x_lo, core), col: 16 (over y, x_hi).
Axes of the slice: x: 4 (x_hi: 2, x_lo: 2; x = x_hi * 2 + x_lo), y: 8, z: 8, core: 2. Of those that a mesh axis runs over, the one named last changes fastest.
Arguments:
- parent_front: float32 [16, 16, 32, 8192], P(None, 'col', None, ('sub', 'row')), as said below
- child_schur: float32 [8192, 4096], P(('sub', 'row', 'col')), as said below
- index_map: int32 [2, 256], replicated, may hold values from 0 to 511, as said below
Outputs:
- factored_front: float32 [16, 16, 32, 8192], P(None, 'col', None, ('sub', 'row'))
Inputs may be any that keep to these rules, and one draw needn't show every extreme that they name: parent_front is symmetric, and the front assembled with both children is positive definite. `child_schur`: each child's block is symmetric. index_map[c] holds distinct blocks for each c; with g = c * 256 + j and h = (g // 1) % 16, block f = index_map[c, j] satisfies (f * 16 // 32) % 16 == h; every front block receives a block of at least one child.
All inputs are finite; a program needn't handle non-finite values.
Results may differ from a plain program's by a relative error of at most 0.0001.
Values sent between devices are 32-bit elements; how exact they have to be, the bound alone decides.
No kernel may reach another device: no remote copies, remote signals or barrier semaphores. Data moves between devices by JAX's collectives and lax.ppermute only.
A program may use at most 64 MiB of HBM per device.

v0:
```python
import jax
import jax.numpy as jnp
from jax import lax
from jax.sharding import PartitionSpec as P

PANELS = 2
BLK = 16


highest = lax.Precision.HIGHEST


def spread_2(block, axis, owner):
    block = jnp.where(lax.axis_index(axis) == owner, block, jnp.zeros_like(block))
    return lax.psum(block, axis)


def panel_gather(front, number, panel_width, rows_dev):
    piece = front[number]
    gathered = lax.all_gather(piece, "col", axis=0, tiled=True)
    return gathered.reshape(panel_width, rows_dev)


def panel_blocks(front, slab, number, panel_width, rows_dev):
    panel_low = number * panel_width
    panel_high = panel_low + panel_width
    diag_parts = []
    rest_parts = []
    for source_shard in range(panel_low // rows_dev, (panel_high - 1) // rows_dev + 1):
        row_low = max(panel_low, source_shard * rows_dev) - source_shard * rows_dev
        row_high = min(panel_high, (source_shard + 1) * rows_dev) - source_shard * rows_dev
        sending = front[number + 1 :, 0, :, row_low:row_high].reshape(-1, row_high - row_low)
        diag_piece, rest_piece = (
            spread_2(slab, ("sub", "row"), source_shard),
            spread_2(sending, ("sub", "row"), source_shard),
        )
        diag_parts.append(diag_piece)
        rest_parts.append(rest_piece)
    return (jnp.concatenate(diag_parts, axis=1), jnp.concatenate(rest_parts, axis=1))


def subtract_update(solved_cols, lower_rows):
    return lax.dot_general(
        solved_cols,
        lower_rows,
        (((0,), (0,)), ((), ())),
        precision=highest,
        preferred_element_type=jnp.float32,
    )


def local(parent_front, child_schur, index_map):
    col_count = lax.axis_size("col")
    shard_count = lax.axis_size("sub") * lax.axis_size("row")
    col_groups, _, stripe, rows_dev = parent_front.shape
    front_order = rows_dev * shard_count
    panel_width = stripe * col_count
    child_rows, child_order = child_schur.shape
    col_index = lax.axis_index("col")
    device_index = lax.axis_index(("sub", "row", "col"))
    child_id = device_index * child_rows // child_order
    mapping = lax.dynamic_index_in_dim(index_map, child_id, 0, keepdims=False)
    front_blocks = front_order // BLK
    inverse = (
        jnp.full((front_blocks,), -1, jnp.int32)
        .at[mapping]
        .set(jnp.arange(child_order // BLK, dtype=jnp.int32))
    )
    positions = jnp.arange(front_order, dtype=jnp.int32)
    source_block = inverse[positions // BLK]
    present = source_block >= 0
    source_col = jnp.maximum(source_block, 0) * BLK + positions % BLK
    spread = jnp.take(child_schur, source_col, axis=1)
    spread = jnp.where(present[None, :], spread, jnp.float32(0.0))
    received = lax.all_to_all(spread, ("sub", "row"), split_axis=1, concat_axis=0, tiled=True)
    recv_blocks = received.shape[0] // BLK
    first_row = jnp.arange(recv_blocks, dtype=jnp.int32) * BLK
    source_shard = first_row // child_rows
    stacked = (source_shard * col_count + col_index) * child_rows + first_row % child_rows
    owner_child = stacked // child_order
    owner_block = stacked % child_order // BLK
    target = index_map[owner_child, owner_block] * BLK
    slot_block = (target // panel_width * stripe + target % stripe) // BLK
    local_blocks = col_groups * stripe // BLK
    placing = (jnp.arange(local_blocks, dtype=jnp.int32)[:, None] == slot_block[None, :]).astype(
        jnp.float32
    )
    added = jnp.dot(
        placing,
        received.reshape(recv_blocks, BLK * rows_dev),
        precision=highest,
        preferred_element_type=jnp.float32,
    )
    front = parent_front + added.reshape(col_groups, 1, stripe, rows_dev)
    row_pos = lax.axis_index(("sub", "row")) * rows_dev + jnp.arange(rows_dev)
    factored = jnp.zeros_like(parent_front)
    slab = panel_gather(front, 0, panel_width, rows_dev)
    for number in range(PANELS):
        begin_col = number * panel_width
        end_col = begin_col + panel_width
        diag_block, rest_block = panel_blocks(front, slab, number, panel_width, rows_dev)
        factor = jnp.linalg.cholesky(diag_block)
        solved_rows = lax.linalg.triangular_solve(factor, slab, left_side=True, lower=True)
        solved_rows = jnp.where(row_pos[None, :] >= begin_col, solved_rows, jnp.float32(0.0))
        solved_cols = lax.linalg.triangular_solve(factor, rest_block.T, left_side=True, lower=True)
        lower_rows = jnp.where(row_pos[None, :] >= end_col, solved_rows, jnp.float32(0.0))
        mine = lax.dynamic_slice_in_dim(solved_rows, col_index * stripe, stripe, 0)
        factored = factored.at[number].set(mine[None])
        whole = subtract_update(solved_cols, lower_rows)
        front = front.at[number + 1 :].add(-whole.reshape(-1, 1, stripe, rows_dev))
        if number + 1 < PANELS:
            slab = panel_gather(front, number + 1, panel_width, rows_dev)
    live = row_pos >= PANELS * panel_width
    tail = jnp.where(live[None, None, None, :], front[PANELS:], jnp.float32(0.0))
    factored = factored.at[PANELS:].set(tail)
    return factored


def solution(mesh):
    in_specs = (P(None, "col", None, ("sub", "row")), P(("sub", "row", "col"), None), P())
    out_specs = P(None, "col", None, ("sub", "row"))
    return jax.shard_map(local, mesh=mesh, in_specs=in_specs, out_specs=out_specs, check_vma=False)
```

profile of v0, /device:TPU:1, one launch (start us, length us, event | category | flops | bytes accessed | tf_op | source)
XLA Modules:
  0.0 978.9 jit_solution(1345012483278971323)
XLA Ops:
  8.7 51.2 %gather_fusion.1 = s32[8192]{0:T(1024)S(1)} fusion(s32[512]{0:T(512)S(1)} %scatter_custom_fusion, s32[8192]{0:T(1024)S(1)} %broadcast_clamp_fusion.1), kind=kCustom, calls=%fused_computation.1 | custom fusion | bytes 98304 | tf_op jit(solution)/shard_map/gather | solution.py:70
  60.7 27.7 %gather_fusion.2 = f32[8192,16]{1,0:T(8,128)} fusion(f32[16,4096]{0,1:T(8,128)S(1)} %copy.40, s32[8192]{0:T(1024)S(1)} %broadcast_clamp_fusion), kind=kCustom, calls=%fused_computation.2 | custom fusion | bytes 1081344 | tf_op jit(solution)/shard_map/jit(_take)/gather | solution.py:73
  92.2 12.9 %all-to-all-start = ((f32[16,32,256]{2,0,1:T(8,128)}), f32[16,32,256]{2,0,1:T(8,128)S(1)}, u32[]{:S(2)}, u32[]{:S(2)}) async-start(f32[16,32,256]{2,0,1:T(8,128)} %select_select_fusion.2), calls=%async_computation | async-start | bytes 1048576 | tf_op jit(solution)/shard_map/all_to_all | solution.py:75
  106.0 15.8 %all-to-all-done = f32[16,32,256]{2,0,1:T(8,128)S(1)} async-done(((f32[16,32,256]{2,0,1:T(8,128)}), f32[16,32,256]{2,0,1:T(8,128)S(1)}, u32[]{:S(2)}, u32[]{:S(2)}) %all-to-all-start) | async-done | bytes 524320 | tf_op jit(solution)/shard_map/all_to_all | solution.py:75
  122.7 36.7 %all-gather = f32[16,1,32,256]{3,2,1,0:T(8,128)S(1)} all-gather(f32[1,1,32,256]{3,2,1,0:T(8,128)S(1)} %slice.361), channel_id=2, replica_groups=mesh['sub'=8,'row'=4,'col'=16] {'col'}, dimensions={0}, use_global_device_ids=true | all-gather | bytes 557056 | tf_op jit(solution)/shard_map/all_gather | solution.py:20
  162.5 233.5 %all-reduce.9.cloned.1.call-done = (f32[512,256]{0,1:T(8,128)}, f32[512,256]{0,1:T(8,128)}, f32[480,256]{1,0:T(8,128)}, f32[480,256]{1,0:T(8,128)}) async-done(((f32[512,256]{0,1:T(8,128)}, f32[512,256]{0,1:T(8,128)}, f32[480,256]{1,0:T(8,128)}, f32[480,256]{1,0:T(8,128)}), (f32[512,256]{0,1:T(8,128)}, f32[512,256]{0,1:T(8,128)}, f32[480,256]{1,0:T(8,128)}, ...) | async-done | bytes 2031632 | tf_op jit(solution)/shard_map/psum | solution.py:15
  400.5 11.7 %cholesky.286 = f32[128,128]{1,0:T(8,128)S(1)} custom-call(f32[128,128]{1,0:T(8,128)S(1)} %cholesky.426), custom_call_target="Cholesky" | custom-call | tf_op jit(solution)/shard_map/jit(cholesky)/cholesky | solution.py:102
  412.4 9.8 %custom-call.37 = f32[1,128,128]{1,2,0:T(8,128)S(1)} custom-call(f32[1,128,128]{2,1,0:T(8,128)S(1)} %get-tuple-element.154), custom_call_target="InvertDiagBlocksLowerTriangular" | custom-call | tf_op jit(solution)/shard_map/jit(cholesky)/cholesky | solution.py:102
  424.8 11.7 %cholesky.305 = f32[128,128]{1,0:T(8,128)S(1)} custom-call(f32[128,128]{1,0:T(8,128)S(1)} %cholesky.430), custom_call_target="Cholesky" | custom-call | tf_op jit(solution)/shard_map/jit(cholesky)/cholesky | solution.py:102
  436.5 10.0 %custom-call.38 = f32[1,128,128]{1,2,0:T(8,128)S(1)} custom-call(f32[1,128,128]{2,1,0:T(8,128)S(1)} %get-tuple-element.151), custom_call_target="InvertDiagBlocksLowerTriangular" | custom-call | tf_op jit(solution)/shard_map/jit(cholesky)/cholesky | solution.py:102
  448.0 11.7 %cholesky.326 = f32[128,128]{1,0:T(8,128)S(1)} custom-call(f32[128,128]{1,0:T(8,128)S(1)} %cholesky.435), custom_call_target="Cholesky" | custom-call | tf_op jit(solution)/shard_map/jit(cholesky)/cholesky | solution.py:102
  460.5 9.8 %custom-call.39 = f32[1,128,128]{1,2,0:T(8,128)S(1)} custom-call(f32[1,128,128]{2,1,0:T(8,128)S(1)} %get-tuple-element.148), custom_call_target="InvertDiagBlocksLowerTriangular" | custom-call | tf_op jit(solution)/shard_map/jit(cholesky)/cholesky | solution.py:102
  471.8 11.7 %cholesky.343 = f32[128,128]{1,0:T(8,128)S(1)} custom-call(f32[128,128]{1,0:T(8,128)S(1)} %convolution_subtract_fusion.17), custom_call_target="Cholesky" | custom-call | tf_op jit(solution)/shard_map/jit(cholesky)/cholesky | solution.py:102
  495.2 39.3 %custom-call.40 = f32[4,128,128]{1,2,0:T(8,128)S(1)} custom-call(f32[4,128,128]{2,1,0:T(8,128)S(1)} %get-tuple-element.97), custom_call_target="InvertDiagBlocksLowerTriangular" | custom-call | tf_op jit(solution)/shard_map/triangular_solve/custom-call.3 | solution.py:103
  542.8 37.6 %all-gather.1 = f32[16,1,32,256]{3,2,1,0:T(8,128)S(1)} all-gather(f32[1,1,32,256]{3,2,1,0:T(8,128)S(1)} %slice.374), channel_id=3, replica_groups=mesh['sub'=8,'row'=4,'col'=16] {'col'}, dimensions={0}, use_global_device_ids=true | all-gather | bytes 557056 | tf_op jit(solution)/shard_map/all_gather | solution.py:20
  583.9 237.8 %all-reduce.7.cloned.1.call-done = (f32[512,256]{0,1:T(8,128)}, f32[512,256]{0,1:T(8,128)}, f32[448,256]{1,0:T(8,128)}, f32[448,256]{1,0:T(8,128)}) async-done(((f32[512,256]{0,1:T(8,128)}, f32[512,256]{0,1:T(8,128)}, f32[448,256]{1,0:T(8,128)}, f32[448,256]{1,0:T(8,128)}), (f32[512,256]{0,1:T(8,128)}, f32[512,256]{0,1:T(8,128)}, f32[448,256]{1,0:T(8,128)}, ...) | async-done | bytes 1966096 | tf_op jit(solution)/shard_map/psum | solution.py:15
  826.3 11.7 %cholesky.358 = f32[128,128]{1,0:T(8,128)S(1)} custom-call(f32[128,128]{1,0:T(8,128)S(1)} %cholesky.439), custom_call_target="Cholesky" | custom-call | tf_op jit(solution)/shard_map/jit(cholesky)/cholesky | solution.py:102
  838.1 9.8 %custom-call.41 = f32[1,128,128]{1,2,0:T(8,128)S(1)} custom-call(f32[1,128,128]{2,1,0:T(8,128)S(1)} %get-tuple-element.144), custom_call_target="InvertDiagBlocksLowerTriangular" | custom-call | tf_op jit(solution)/shard_map/jit(cholesky)/cholesky | solution.py:102
  850.5 11.7 %cholesky.377 = f32[128,128]{1,0:T(8,128)S(1)} custom-call(f32[128,128]{1,0:T(8,128)S(1)} %cholesky.443), custom_call_target="Cholesky" | custom-call | tf_op jit(solution)/shard_map/jit(cholesky)/cholesky | solution.py:102
  863.6 10.0 %custom-call.42 = f32[1,128,128]{1,2,0:T(8,128)S(1)} custom-call(f32[1,128,128]{2,1,0:T(8,128)S(1)} %get-tuple-element.141), custom_call_target="InvertDiagBlocksLowerTriangular" | custom-call | tf_op jit(solution)/shard_map/jit(cholesky)/cholesky | solution.py:102
  875.1 11.7 %cholesky.398 = f32[128,128]{1,0:T(8,128)S(1)} custom-call(f32[128,128]{1,0:T(8,128)S(1)} %cholesky.448), custom_call_target="Cholesky" | custom-call | tf_op jit(solution)/shard_map/jit(cholesky)/cholesky | solution.py:102
  887.5 9.8 %custom-call.43 = f32[1,128,128]{1,2,0:T(8,128)S(1)} custom-call(f32[1,128,128]{2,1,0:T(8,128)S(1)} %get-tuple-element.138), custom_call_target="InvertDiagBlocksLowerTriangular" | custom-call | tf_op jit(solution)/shard_map/jit(cholesky)/cholesky | solution.py:102
  898.8 11.9 %cholesky.415 = f32[128,128]{1,0:T(8,128)S(1)} custom-call(f32[128,128]{1,0:T(8,128)S(1)} %convolution_subtract_fusion.16), custom_call_target="Cholesky" | custom-call | tf_op jit(solution)/shard_map/jit(cholesky)/cholesky | solution.py:102
  922.1 39.3 %custom-call.44 = f32[4,128,128]{1,2,0:T(8,128)S(1)} custom-call(f32[4,128,128]{2,1,0:T(8,128)S(1)} %get-tuple-element.98), custom_call_target="InvertDiagBlocksLowerTriangular" | custom-call | tf_op jit(solution)/shard_map/triangular_solve/custom-call.3 | solution.py:103
  (167 shorter events, 89.9 us)
Async XLA Ops:
  8.7 51.4 %copy-start.3 = (f32[16,4096]{1,0:T(8,128)S(1)}, f32[16,4096]{1,0:T(8,128)}, u32[]{:S(2)}) copy-start(f32[16,4096]{1,0:T(8,128)} %param.17) | copy-start | bytes 786436
  88.4 16.8 %copy-start = (s32[2,256]{1,0:T(2,128)S(1)}, s32[2,256]{1,0:T(2,128)}, u32[]{:S(2)}) copy-start(s32[2,256]{1,0:T(2,128)} %param.18) | copy-start | bytes 6148
  88.4 34.2 %copy-start.1 = (f32[16,1,32,256]{3,2,1,0:T(8,128)S(1)}, f32[16,1,32,256]{3,2,1,0:T(8,128)}, u32[]{:S(2)}) copy-start(f32[16,1,32,256]{3,2,1,0:T(8,128)} %param.16) | copy-start | bytes 1572868
  92.2 29.6 %all-to-all-start = ((f32[16,32,256]{2,0,1:T(8,128)}), f32[16,32,256]{2,0,1:T(8,128)S(1)}, u32[]{:S(2)}, u32[]{:S(2)}) async-start(f32[16,32,256]{2,0,1:T(8,128)} %select_select_fusion.2), calls=%async_computation | async-start | bytes 1048576 | tf_op jit(solution)/shard_map/all_to_all | solution.py:75
  105.1 290.9 %all-reduce.9.cloned.1.call-start = ((), (), s32[]{:S(2)}) async-start(), calls=%async_computation.2 | async-start | bytes 4063232 | tf_op jit(solution)/shard_map/psum | solution.py:15
  161.9 659.8 %all-reduce.7.cloned.1.call-start = ((), (), s32[]{:S(2)}) async-start(), calls=%async_computation.1 | async-start | bytes 3932160 | tf_op jit(solution)/shard_map/psum | solution.py:15
  964.3 4.7 copy-start.2
Sparse Core Ops, SparseCore 0:
  162.0 233.9 all-reduce.8
  583.0 238.6 all-reduce.6
where the time goes:
time: 984 us; the launch traced here: 979 us
  waiting for transfers between devices  487 us (49%)
  other arithmetic  249 us (25%)
  local copies, waits for them, and re-layouts  111 us (11%)
  blocking collectives  74.3 us (8%)
  matrix products  23.9 us (2%)
  between operations  19.6 us (2%)
  starting transfers between devices  13.4 us (1%)
    psum x2, waiting for transfers between devices, spread_2(): return lax.psum(block, axis)  471 us
    another operation x29, other arithmetic, local(): factor = jnp.linalg.cholesky(diag_block)  158 us
    another operation x5, other arithmetic, local(): lax.linalg.triangular_solve(factor, slab, left_side=True, lower=True)  78.9 us
    all_gather x2, blocking collectives, panel_gather(): gathered = lax.all_gather(piece, 'col', axis=0, tiled=True)  74.3 us
    gather x1, local copies, waits for them, and re-layouts, local(): source_block = inverse[positions // BLK]  51.2 us
    gather x2, local copies, waits for them, and re-layouts, local(): spread = jnp.take(child_schur, source_col, axis=1)  30.5 us
  transfers between devices with their start and end apart: 3, of which 3 were waited for; matrix products, arithmetic and copies ran while one was open for 0% of the time, Pallas kernels for 0%

commit v1 on v0

v1 whole, which is shorter than its diff:
```python
import functools

import jax
import jax.numpy as jnp
from jax import lax
from jax.experimental import pallas as pl
from jax.experimental.pallas import tpu as pltpu
from jax.sharding import PartitionSpec as P

BLK = 16
TILE = 128
STEP = 8
SUBS = 8
ROWS = 4
COLS = 16
SHARDS = SUBS * ROWS
WIDE = 256
PANEL = 512
HIGHEST = lax.Precision.HIGHEST

VMEM = pl.BlockSpec(memory_space=pltpu.VMEM)
SMEM = pl.BlockSpec(memory_space=pltpu.SMEM)
PARAMS = pltpu.CompilerParams(vmem_limit_bytes=40 << 20)


def contract(a, b, dims):
    return lax.dot_general(
        a, b, ((dims[:1], dims[1:]), ((), ())), precision=HIGHEST, preferred_element_type=jnp.float32
    )


def dot(a, b):
    return contract(a, b, (1, 0))


def dot_t(a, b):
    return contract(a, b, (1, 1))


def t_dot(a, b):
    return contract(a, b, (0, 0))


def spread_kernel(where_ref, map_ref, child_ref, out_ref):
    child = where_ref[0]
    out_ref[...] = jnp.zeros_like(out_ref)
    lane_block = lax.broadcasted_iota(jnp.int32, (BLK, TILE), 1) // BLK

    def body(tile, carry):
        rows = child_ref[:, pl.ds(pl.multiple_of(tile * TILE, TILE), TILE)]
        for part in range(TILE // BLK):
            block = map_ref[child, tile * (TILE // BLK) + part]
            place = block % (TILE // BLK)
            target = block // (TILE // BLK)
            shift = (place - part + TILE // BLK) % (TILE // BLK) * BLK
            moved = pltpu.roll(rows, shift, 1)
            out_ref[target] = jnp.where(lane_block == place, moved, out_ref[target])
        return carry

    lax.fori_loop(0, child_ref.shape[1] // TILE, body, 0)


def spread_rows(where, index_map, child):
    return pl.pallas_call(
        spread_kernel,
        out_shape=jax.ShapeDtypeStruct((2 * SHARDS, BLK, TILE), jnp.float32),
        in_specs=[SMEM, SMEM, VMEM],
        out_specs=VMEM,
        compiler_params=PARAMS,
        name="spread_rows",
    )(where, index_map, child)


def place_kernel(where_ref, map_ref, received_ref, parent_ref, out_ref):
    col = where_ref[1]

    def body(source, carry):
        child = source // (SHARDS // 2)
        block = map_ref[child, source % (SHARDS // 2) * COLS + col]
        slot = block // (2 * COLS) * 2 + block % 2
        for half in range(2):
            lanes = slice(half * TILE, (half + 1) * TILE)
            out_ref[slot, :, lanes] = parent_ref[slot, :, lanes] + received_ref[source, half]
        return carry

    lax.fori_loop(0, SHARDS, body, 0)


def place(where, index_map, received, parent):
    return pl.pallas_call(
        place_kernel,
        out_shape=jax.ShapeDtypeStruct((SHARDS, BLK, WIDE), jnp.float32),
        in_specs=[SMEM, SMEM, VMEM, VMEM],
        out_specs=VMEM,
        compiler_params=PARAMS,
        name="place",
    )(where, index_map, received, parent)


def tree_sum(terms):
    while len(terms) > 1:
        terms = [sum(terms[i : i + 2]) for i in range(0, len(terms), 2)]
    return terms[0]


def factor_tile(read, out_ref):
    full = (8, TILE)
    groups = TILE // 8
    sub = lax.broadcasted_iota(jnp.int32, full, 0)
    lane = lax.broadcasted_iota(jnp.int32, full, 1)
    a = [read(h) for h in range(groups)]
    e = [jnp.where(lane == sub + 8 * h, jnp.float32(1), jnp.float32(0)) for h in range(groups)]
    for j in range(0, TILE, STEP):
        g, r = divmod(j, 8)
        col = [
            [jnp.broadcast_to(a[h][:, j + t : j + t + 1], full) for t in range(STEP)]
            for h in range(g, groups)
        ]
        p = [
            [jnp.broadcast_to(col[0][t][r + s : r + s + 1, :], full) for t in range(s + 1)]
            for s in range(STEP)
        ]
        ua = [jnp.broadcast_to(a[g][r + s : r + s + 1, :], full) for s in range(STEP)]
        ue = [jnp.broadcast_to(e[g][r + s : r + s + 1, :], full) for s in range(STEP)]
        rd = [None] * STEP
        low = [[None] * STEP for _ in range(STEP)]
        for t in range(STEP):
            rd[t] = 1.0 / p[t][t]
            for s in range(t + 1, STEP):
                low[s][t] = p[s][t] * rd[t]
            for s in range(t + 1, STEP):
                for q in range(t + 1, s + 1):
                    p[s][q] = p[s][q] - low[s][t] * p[q][t]
            for s in range(t + 1, STEP):
                ua[s] = ua[s] - low[s][t] * ua[t]
                ue[s] = ue[s] - low[s][t] * ue[t]
        for s in range(STEP):
            out_ref[j + s : j + s + 1, :] = (ue[s] * lax.rsqrt(p[s][s]))[0:1, :]
        if j + STEP >= TILE:
            break
        za = [ua[s] * rd[s] for s in range(STEP)]
        ze = [ue[s] * rd[s] for s in range(STEP)]
        for t in range(STEP - 1, 0, -1):
            for s in range(t):
                za[s] = za[s] - low[t][s] * za[t]
                ze[s] = ze[s] - low[t][s] * ze[t]
        for h in range(g, groups):
            if h == g and r + STEP >= 8:
                continue
            c = col[h - g]
            da = tree_sum([c[t] * za[t] for t in range(STEP)])
            de = tree_sum([c[t] * ze[t] for t in range(STEP)])
            if h == g:
                da = jnp.where(sub >= r + STEP, da, 0.0)
                de = jnp.where(sub >= r + STEP, de, 0.0)
            a[h] = a[h] - da
            e[h] = e[h] - de


def invert_factor(m_ref, w_ref, t_ref):
    tiles = m_ref.shape[0] // TILE
    w_ref[...] = jnp.zeros_like(w_ref)

    def body(b, carry):
        low = pl.multiple_of(b * TILE, TILE)
        factor_tile(
            lambda h: m_ref[pl.ds(pl.multiple_of(low + 8 * h, 8), 8), pl.ds(low, TILE)], t_ref
        )
        for c in range(tiles):

            @pl.when(b == c)
            def _():
                lo, hi = c * TILE, (c + 1) * TILE
                t = t_ref[...]
                if c:
                    w_ref[lo:hi, :lo] = dot(t, w_ref[lo:hi, :lo])
                w_ref[lo:hi, lo:hi] = t
                if c + 1 < tiles:
                    x = dot(t, m_ref[lo:hi, hi:])
                    m_ref[hi:, hi:] = m_ref[hi:, hi:] - t_dot(x, x)
                    w_ref[hi:, :hi] = w_ref[hi:, :hi] - t_dot(x, w_ref[lo:hi, :hi])

        return carry

    lax.fori_loop(0, tiles, body, 0)


def fill(m_ref, core, own_ref, other_ref):
    own = pl.multiple_of(core * WIDE, WIDE)
    other = pl.multiple_of((1 - core) * WIDE, WIDE)
    for slot in range(SHARDS):
        rows = slice(slot * BLK, (slot + 1) * BLK)
        m_ref[rows, pl.ds(own, WIDE)] = own_ref[slot]
        m_ref[rows, pl.ds(other, WIDE)] = other_ref[slot]


def first_kernel(where_ref, own_ref, other_ref, w_ref, m_ref, t_ref):
    fill(m_ref, where_ref[2] % 2, own_ref, other_ref)
    invert_factor(m_ref, w_ref, t_ref)


def first_factor(where, own, other):
    return pl.pallas_call(
        first_kernel,
        out_shape=jax.ShapeDtypeStruct((PANEL, PANEL), jnp.float32),
        in_specs=[SMEM, VMEM, VMEM],
        out_specs=VMEM,
        scratch_shapes=[
            pltpu.VMEM((PANEL, PANEL), jnp.float32),
            pltpu.VMEM((TILE, TILE), jnp.float32),
        ],
        compiler_params=PARAMS,
        cost_estimate=pl.CostEstimate(flops=60_000_000_000, bytes_accessed=4 << 20, transcendentals=0),
        name="first_factor",
    )(where, own, other)


def second_kernel(where_ref, inv_ref, up_own, up_other, low_own, low_other, w_ref, x_ref, m_ref, t_ref):
    core = where_ref[2] % 2
    fill(m_ref, core, up_own, up_other)
    x_ref[...] = dot(inv_ref[...], m_ref[...])
    fill(m_ref, core, low_own, low_other)
    m_ref[...] = m_ref[...] - t_dot(x_ref[...], x_ref[...])
    invert_factor(m_ref, w_ref, t_ref)


def second_factor(where, inv, up_own, up_other, low_own, low_other):
    shape = jax.ShapeDtypeStruct((PANEL, PANEL), jnp.float32)
    return pl.pallas_call(
        second_kernel,
        out_shape=(shape, shape),
        in_specs=[SMEM] + [VMEM] * 5,
        out_specs=(VMEM, VMEM),
        scratch_shapes=[
            pltpu.VMEM((PANEL, PANEL), jnp.float32),
            pltpu.VMEM((TILE, TILE), jnp.float32),
        ],
        compiler_params=PARAMS,
        cost_estimate=pl.CostEstimate(flops=60_000_000_000, bytes_accessed=8 << 20, transcendentals=0),
        name="second_factor",
    )(where, inv, up_own, up_other, low_own, low_other)


def finish_kernel(
    where_ref, inv0_ref, inv1_ref, x01_ref, cols_ref, row0, row1, row2, row3, front_ref, out_ref,
    rows_ref, cols0_ref, cols1_ref,
):
    col, row, shard = where_ref[1], where_ref[2], where_ref[3]
    for number, ref in enumerate((row0, row1, row2, row3)):
        chunk = (row // 2 ^ number // 2) * 2 + (row % 2 ^ number % 2)
        low = pl.multiple_of(chunk * WIDE, WIDE)
        for slot in range(SHARDS):
            rows_ref[slot * BLK : (slot + 1) * BLK, pl.ds(low, WIDE)] = ref[slot]
    for q in range(COLS):
        for half in range(2):
            at = slice(q * 2 * BLK + half * BLK, q * 2 * BLK + (half + 1) * BLK)
            cols0_ref[at, :] = cols_ref[q, half]
            cols1_ref[at, :] = cols_ref[q, 2 + half]
    r0 = dot_t(rows_ref[:, :PANEL], inv0_ref[...])
    c0 = dot(inv0_ref[...], cols0_ref[...])
    cols0_ref[...] = c0
    r1 = dot_t(rows_ref[:, PANEL:] - dot(r0, x01_ref[...]), inv1_ref[...])
    c1 = dot(inv1_ref[...], cols1_ref[...] - t_dot(x01_ref[...], c0))
    cols1_ref[...] = c1
    update = dot(r0, c0) + dot(r1, c1)
    live = (shard >= ROWS).astype(jnp.float32)
    for slot in range(4, SHARDS):
        rows = slice(slot * BLK, (slot + 1) * BLK)
        out_ref[slot] = (front_ref[slot] - update[rows]) * live
    mine = pl.multiple_of(col * 2 * BLK, 2 * BLK)
    past = (shard >= ROWS // 2).astype(jnp.float32)
    for half in range(2):
        out_ref[half] = cols0_ref[pl.ds(mine + half * BLK, BLK), :]
        out_ref[2 + half] = cols1_ref[pl.ds(mine + half * BLK, BLK), :] * past


def finish(where, inv0, inv1, x01, cols, rows, front):
    return pl.pallas_call(
        finish_kernel,
        out_shape=jax.ShapeDtypeStruct((SHARDS, BLK, WIDE), jnp.float32),
        in_specs=[SMEM] + [VMEM] * 9,
        out_specs=VMEM,
        scratch_shapes=[
            pltpu.VMEM((PANEL, 2 * PANEL), jnp.float32),
            pltpu.VMEM((PANEL, WIDE), jnp.float32),
            pltpu.VMEM((PANEL, WIDE), jnp.float32),
        ],
        compiler_params=PARAMS,
        name="finish",
    )(where, inv0, inv1, x01, cols, *rows, front)


def swap(x, axis, bit):
    return lax.ppermute(x, axis, [(i, i ^ bit) for i in range(ROWS)])


def to_all(x, axis, count):
    return lax.all_to_all(
        jnp.broadcast_to(x[None], (count, *x.shape)), axis, split_axis=0, concat_axis=0, tiled=True
    )


def exchange(x, axis):
    return lax.all_to_all(x, axis, split_axis=0, concat_axis=0, tiled=True)


def local(parent_front, child_schur, index_map):
    sub, row, col = (lax.axis_index(name) for name in ("sub", "row", "col"))
    shard = sub * ROWS + row
    where = jnp.stack([shard // (SHARDS // 2), col, row, shard]).astype(jnp.int32)
    parent = parent_front.reshape(SHARDS, BLK, WIDE)

    chunk = exchange(parent.reshape(SUBS, SHARDS // SUBS, BLK, WIDE), "sub")[0]
    parent_low = to_all(chunk, "sub", SUBS).reshape(SHARDS, BLK, WIDE)

    spread = spread_rows(where, index_map, child_schur).reshape(SHARDS, 2, BLK, TILE)
    low = jnp.broadcast_to(spread[None, :ROWS], (SUBS, ROWS, 2, BLK, TILE))
    low = exchange(low.reshape(SHARDS, 2, BLK, TILE), ("sub", "row"))
    rows = place(where, index_map, low, parent_low)
    pivots = to_all(rows[:4], "col", COLS)

    received = exchange(spread, ("sub", "row"))
    front = place(where, index_map, received, parent)
    cols = to_all(front[:4], "col", COLS)

    upper = pivots[:, :2].reshape(SHARDS, BLK, WIDE)
    lower = pivots[:, 2:].reshape(SHARDS, BLK, WIDE)
    left = row < 2
    crossed = swap(jnp.where(left, upper, lower), "row", 2)
    diag0 = jnp.where(left, upper, crossed)
    diag1 = jnp.where(left, crossed, lower)
    inv0 = first_factor(where, diag0, swap(diag0, "row", 1))
    above = jnp.where(left, swap(upper, "row", 2), upper)
    inv1, x01 = second_factor(
        where, inv0, above, swap(above, "row", 1), diag1, swap(diag1, "row", 1)
    )
    across = swap(rows, "row", 2)
    pieces = (rows, swap(rows, "row", 1), across, swap(across, "row", 1))
    out = finish(where, inv0, inv1, x01, cols, pieces, front)
    return out.reshape(parent_front.shape)


def solution(mesh):
    spec = P(None, "col", None, ("sub", "row"))
    in_specs = (spec, P(("sub", "row", "col"), None), P())
    return jax.shard_map(local, mesh=mesh, in_specs=in_specs, out_specs=spec, check_vma=False)
```

time: 984 us -> 243 us (0.25)
  waiting for transfers between devices: 487 us -> 62.1 us
  other arithmetic: 249 us -> 2.48 us
  local copies, waits for them, and re-layouts: 111 us -> 13.8 us
  Pallas kernels: 0 us -> 75.4 us
  blocking collectives: 74.3 us -> 19.1 us
  starting transfers between devices: 13.4 us -> 68.2 us
  matrix products: 23.9 us -> 0 us
  between operations: 19.6 us -> 0.29 us
    psum x2 -> x0, waiting for transfers between devices: 471 us -> none  [spread_2(): return lax.psum(block, axis)]
    another operation x34 -> x1, other arithmetic: 237 us -> 0.08 us  [local(): jnp.stack([shard // (SHARDS // 2), col, row, shard]).astype(jnp.int32)]
    gather x4 -> x0, local copies, waits for them, and re-layouts: 82.5 us -> none  [the longest x1 51.2 us: local(): source_block = inverse[positions // BLK]]
    pallas_call x0 -> x6, Pallas kernels: none -> 75.4 us  [the longest x1 28.2 us: second_factor(): pl.pallas_call(second_kernel, out_shape=(shape, shape), in_specs=[SMEM] +...]
    all_gather x2 -> x0, blocking collectives: 74.3 us -> none  [panel_gather(): gathered = lax.all_gather(piece, 'col', axis=0, tiled=True)]
    all_to_all x1 -> x5, waiting for transfers between devices: 15.8 us -> 54.2 us  [the longest x3 28.3 us: exchange(): return lax.all_to_all(x, axis, split_axis=0, concat_axis=0, tiled=True)]
    ppermute x0 -> x8, starting transfers between devices: none -> 31.6 us  [swap(): return lax.ppermute(x, axis, [(i, i ^ bit) for i in range(ROWS)])]
    all_to_all x1 -> x5, starting transfers between devices: 12.9 us -> 36.6 us  [the longest x3 23.5 us: exchange(): return lax.all_to_all(x, axis, split_axis=0, concat_axis=0, tiled=True)]
  transfers between devices with their start and end apart: 3 -> 13, of which waited for: 3 -> 4; matrix products, arithmetic and copies ran while one was open for 0% -> 2% of each run, Pallas kernels for 0% -> 24%
where the time goes in v1:
time: 243 us; the launch traced here: 241 us
  Pallas kernels  75.4 us (31%)
  starting transfers between devices  68.2 us (28%)
  waiting for transfers between devices  62.1 us (26%)
  blocking collectives  19.1 us (8%)
  local copies, waits for them, and re-layouts  13.8 us (6%)
  other arithmetic  2.48 us (1%)
    ppermute x8, starting transfers between devices, swap(): return lax.ppermute(x, axis, [(i, i ^ bit) for i in range(ROWS)])  31.6 us
    all_to_all x3, waiting for transfers between devices, exchange(): return lax.all_to_all(x, axis, split_axis=0, concat_axis=0, tiled=True)  28.3 us
    pallas_call x1, Pallas kernels, second_factor(): pl.pallas_call(second_kernel, out_shape=(shape, shape), in_specs=[SMEM] +...  28.2 us
    all_to_all x2, waiting for transfers between devices, to_all(): lax.all_to_all(jnp.broadcast_to(x[None], (count, *x.shape)), axis, split_...  25.9 us
    pallas_call x1, Pallas kernels, first_factor(): pl.pallas_call(first_kernel, out_shape=jax.ShapeDtypeStruct((PANEL, PANEL...  23.6 us
    all_to_all x3, starting transfers between devices, exchange(): return lax.all_to_all(x, axis, split_axis=0, concat_axis=0, tiled=True)  23.5 us
    all_to_all x1, blocking collectives, to_all(): lax.all_to_all(jnp.broadcast_to(x[None], (count, *x.shape)), axis, split_...  19.1 us
    pallas_call x1, Pallas kernels, finish(): pl.pallas_call(finish_kernel, out_shape=jax.ShapeDtypeStruct((SHARDS, BLK...  15.7 us
  transfers between devices with their start and end apart: 13, of which 4 were waited for; matrix products, arithmetic and copies ran while one was open for 2% of the time, Pallas kernels for 24%

profile of v1, /device:TPU:1, one launch (start us, length us, event | category | flops | bytes accessed | tf_op | source)
XLA Modules:
  0.0 241.3 jit_solution(8711185164946219007)
XLA Ops:
  0.0 11.0 %all-to-all-start.1 = ((f32[8,4,16,256]{3,2,1,0:T(8,128)}), f32[8,4,16,256]{3,2,1,0:T(8,128)S(1)}, u32[]{:S(2)}, u32[]{:S(2)}) async-start(f32[8,4,16,256]{3,2,1,0:T(8,128)} %bitcast.22), calls=%async_computation.1 | async-start | bytes 1048576 | tf_op jit(solution)/shard_map/all_to_all | solution.py:304
  11.7 5.2 %spread_rows.1 = f32[64,16,128]{2,1,0:T(8,128)} custom-call(s32[4]{0:T(128)S(1)} %pad_add_fusion.where_ref, s32[2,256]{1,0:T(2,128)S(1)} %copy-done.12, f32[16,4096]{1,0:T(8,128)S(1)} %copy-done.11), custom_call_target="tpu_custom_call" | custom-call | tf_op jit(solution)/shard_map/spread_rows/pallas_call | solution.py:64
  17.7 11.2 %all-to-all-done.1 = f32[8,4,16,256]{3,2,1,0:T(8,128)S(1)} async-done(((f32[8,4,16,256]{3,2,1,0:T(8,128)}), f32[8,4,16,256]{3,2,1,0:T(8,128)S(1)}, u32[]{:S(2)}, u32[]{:S(2)}) %all-to-all-start.1) | async-done | bytes 524320 | tf_op jit(solution)/shard_map/all_to_all | solution.py:304
  29.8 4.0 %all-to-all-start = ((f32[32,2,16,128]{3,2,1,0:T(8,128)}), f32[32,2,16,128]{3,2,1,0:T(8,128)S(1)}, u32[]{:S(2)}, u32[]{:S(2)}) async-start(f32[32,2,16,128]{3,2,1,0:T(8,128)} %bitcast.5), calls=%async_computation | async-start | bytes 1048576 | tf_op jit(solution)/shard_map/all_to_all | solution.py:304
  33.9 17.1 %all-to-all-done.received_ref = f32[32,2,16,128]{3,2,1,0:T(8,128)S(1)} async-done(((f32[32,2,16,128]{3,2,1,0:T(8,128)}), f32[32,2,16,128]{3,2,1,0:T(8,128)S(1)}, u32[]{:S(2)}, u32[]{:S(2)}) %all-to-all-start) | async-done | bytes 524320 | tf_op jit(solution)/shard_map/all_to_all | solution.py:304
  51.0 19.1 %all_to_all.30 = f32[8,4,16,256]{3,2,1,0:T(8,128)S(1)} all-to-all(f32[8,4,16,256]{3,2,1,0:T(8,128)S(1)} %broadcast_in_dim.30), channel_id=1, replica_groups=mesh['sub'=8,'row'=4,'col'=16] {'sub'}, dimensions={0} | all-to-all | bytes 1048576 | tf_op jit(solution)/shard_map/all_to_all | solution.py:298
  72.6 9.4 %all-to-all-start.3 = ((f32[16,4,16,256]{3,2,1,0:T(8,128)}), f32[16,4,16,256]{3,2,1,0:T(8,128)S(1)}, u32[]{:S(2)}, u32[]{:S(2)}) async-start(f32[16,4,16,256]{3,2,1,0:T(8,128)} %broadcast_in_dim.31), calls=%async_computation.3 | async-start | bytes 2097152 | tf_op jit(solution)/shard_map/all_to_all | solution.py:298
  82.0 25.9 %all-to-all-done.3 = f32[16,4,16,256]{3,2,1,0:T(8,128)S(1)} async-done(((f32[16,4,16,256]{3,2,1,0:T(8,128)}), f32[16,4,16,256]{3,2,1,0:T(8,128)S(1)}, u32[]{:S(2)}, u32[]{:S(2)}) %all-to-all-start.3) | async-done | bytes 1048608 | tf_op jit(solution)/shard_map/all_to_all | solution.py:298
  108.1 1.9 collective-permute-start
  110.0 3.4 %collective-permute-start.2 = (f32[32,16,256]{2,1,0:T(8,128)S(1)}, f32[32,16,256]{2,1,0:T(8,128)}, u32[]{:S(2)}, u32[]{:S(2)}) collective-permute-start(f32[32,16,256]{2,1,0:T(8,128)S(1)} %bitcast.25), channel_id=1, source_target_pairs={{0,32},{16,48},{32,0},{48,16},{1,33},{17,49},{33,1},{49,17},{2,34}... | collective-permute-start | bytes 1572872 | tf_op jit(solution)/shard_map/ppermute | solution.py:294
  113.4 8.5 %all-to-all-start.4 = ((f32[32,2,16,128]{3,2,1,0:T(8,128)}), f32[32,2,16,128]{3,2,1,0:T(8,128)S(1)}, u32[]{:S(2)}, u32[]{:S(2)}) async-start(f32[32,2,16,128]{3,2,1,0:T(8,128)} %bitcast.11), calls=%async_computation.4 | async-start | bytes 1048576 | tf_op jit(solution)/shard_map/all_to_all | solution.py:304
  121.9 3.4 %collective-permute-start.6 = (f32[32,16,256]{2,1,0:T(8,128)S(1)}, f32[32,16,256]{2,1,0:T(8,128)}, u32[]{:S(2)}, u32[]{:S(2)}) collective-permute-start(f32[32,16,256]{2,1,0:T(8,128)S(1)} %place.2.row0), channel_id=1, source_target_pairs={{0,32},{16,48},{32,0},{48,16},{1,33},{17,49},{33,1},{49,17},{2,34}... | collective-permute-start | bytes 1572872 | tf_op jit(solution)/shard_map/ppermute | solution.py:294
  125.3 7.8 %collective-permute-done.2 = f32[32,16,256]{2,1,0:T(8,128)} collective-permute-done((f32[32,16,256]{2,1,0:T(8,128)S(1)}, f32[32,16,256]{2,1,0:T(8,128)}, u32[]{:S(2)}, u32[]{:S(2)}) %collective-permute-start.2) | collective-permute-done | bytes 524320 | tf_op jit(solution)/shard_map/ppermute | solution.py:294
  133.2 2.3 bitcast_select_fusion
  135.5 14.1 %collective-permute-start.1 = (f32[32,16,256]{2,1,0:T(8,128)S(1)}, f32[32,16,256]{2,1,0:T(8,128)}, u32[]{:S(2)}, u32[]{:S(2)}) collective-permute-start(f32[32,16,256]{2,1,0:T(8,128)S(1)} %get-tuple-element.12.own_ref), channel_id=1, source_target_pairs={{0,16},{16,0},{32,48},{48,32},{1,17},{17,1},{33,49},{49,33},{2,18}... | collective-permute-start | bytes 1572872 | tf_op jit(solution)/shard_map/ppermute | solution.py:294
  149.6 1.3 place.3.front_ref
  152.1 3.7 %all-to-all-start.5 = ((f32[16,4,16,256]{3,2,1,0:T(8,128)}), f32[16,4,16,256]{3,2,1,0:T(8,128)S(1)}, u32[]{:S(2)}, u32[]{:S(2)}) async-start(f32[16,4,16,256]{3,2,1,0:T(8,128)} %broadcast_in_dim.32), calls=%async_computation.5 | async-start | bytes 2097152 | tf_op jit(solution)/shard_map/all_to_all | solution.py:298
  155.8 2.0 collective-permute-start.5
  157.8 2.3 collective-permute-start.7
  160.1 2.0 collective-permute-start.3
  162.1 2.5 %collective-permute-start.4 = (f32[32,16,256]{2,1,0:T(8,128)}, f32[32,16,256]{2,1,0:T(8,128)S(1)}, u32[]{:S(2)}, u32[]{:S(2)}) collective-permute-start(f32[32,16,256]{2,1,0:T(8,128)} %get-tuple-element.11.low_own), channel_id=1, source_target_pairs={{0,16},{16,0},{32,48},{48,32},{1,17},{17,1},{33,49},{49,33},{2,18}... | collective-permute-start | bytes 1572872 | tf_op jit(solution)/shard_map/ppermute | solution.py:294
  165.7 23.6 %first_factor.1.inv_ref.inv0_ref = f32[512,512]{1,0:T(8,128)S(1)} custom-call(s32[4]{0:T(128)S(1)} %pad_add_fusion.where_ref, f32[32,16,256]{2,1,0:T(8,128)S(1)} %copy-done.6, f32[32,16,256]{2,1,0:T(8,128)} %collective-permute-done.1.other_ref), custom_call_target="tpu_custom_call" | custom-call | flops 60000002048 | bytes 4194304 | tf_op jit(solution)/shard_map/first_factor/pallas_call | solution.py:203
  189.4 28.2 %second_factor.1 = (f32[512,512]{1,0:T(8,128)S(1)}, f32[512,512]{1,0:T(8,128)S(1)}) custom-call(s32[4]{0:T(128)S(1)} %pad_add_fusion.where_ref, f32[512,512]{1,0:T(8,128)S(1)} %first_factor.1.inv_ref.inv0_ref, f32[32,16,256]{2,1,0:T(8,128)} %get-tuple-element.13.up_own, f32[32,16,256]{2,1,0:T(8,128)S(1)} %collective-permute-done.3.up_other, ...), custom_call_target="tpu_custom_call" | custom-call | flops 60000002048 | bytes 8388608 | tf_op jit(solution)/shard_map/second_factor/pallas_call | solution.py:229
  225.6 15.7 %finish.1 = f32[32,16,256]{2,1,0:T(8,128)} custom-call(s32[4]{0:T(128)S(1)} %pad_add_fusion.where_ref, f32[512,512]{1,0:T(8,128)S(1)} %first_factor.1.inv_ref.inv0_ref, f32[512,512]{1,0:T(8,128)S(1)} %copy-done.2, f32[512,512]{1,0:T(8,128)S(1)} %copy-done.4, f32[16,4,16,256]{3,2,1,0:T(8,128)S(1)} %all-to-all-done.5.cols_ref, f32[32,16,256]{2,1,0:T(8,128)S(1)} %place.2.row0, ...), custom_call_target="tpu_custom_call" | custom-call | tf_op jit(solution)/shard_map/finish/pallas_call | solution.py:278
  (47 shorter events, 15.3 us)
Async XLA Ops:
  0.0 11.1 %copy-start.11 = (f32[16,4096]{1,0:T(8,128)S(1)}, f32[16,4096]{1,0:T(8,128)}, u32[]{:S(2)}) copy-start(f32[16,4096]{1,0:T(8,128)} %child_ref.1) | copy-start | bytes 786436
  0.0 29.0 %all-to-all-start.1 = ((f32[8,4,16,256]{3,2,1,0:T(8,128)}), f32[8,4,16,256]{3,2,1,0:T(8,128)S(1)}, u32[]{:S(2)}, u32[]{:S(2)}) async-start(f32[8,4,16,256]{3,2,1,0:T(8,128)} %bitcast.22), calls=%async_computation.1 | async-start | bytes 1048576 | tf_op jit(solution)/shard_map/all_to_all | solution.py:304
  29.8 21.1 %all-to-all-start = ((f32[32,2,16,128]{3,2,1,0:T(8,128)}), f32[32,2,16,128]{3,2,1,0:T(8,128)S(1)}, u32[]{:S(2)}, u32[]{:S(2)}) async-start(f32[32,2,16,128]{3,2,1,0:T(8,128)} %bitcast.5), calls=%async_computation | async-start | bytes 1048576 | tf_op jit(solution)/shard_map/all_to_all | solution.py:304
  72.6 35.3 %all-to-all-start.3 = ((f32[16,4,16,256]{3,2,1,0:T(8,128)}), f32[16,4,16,256]{3,2,1,0:T(8,128)S(1)}, u32[]{:S(2)}, u32[]{:S(2)}) async-start(f32[16,4,16,256]{3,2,1,0:T(8,128)} %broadcast_in_dim.31), calls=%async_computation.3 | async-start | bytes 2097152 | tf_op jit(solution)/shard_map/all_to_all | solution.py:298
  108.1 17.3 %collective-permute-start = (f32[32,16,256]{2,1,0:T(8,128)S(1)}, f32[32,16,256]{2,1,0:T(8,128)}, u32[]{:S(2)}, u32[]{:S(2)}) collective-permute-start(f32[32,16,256]{2,1,0:T(8,128)S(1)} %bitcast_select_fusion.1), channel_id=1, source_target_pairs={{0,32},{16,48},{32,0},{48,16},{1,33},{17,49},{33,1},{49,17},{2,34}... | collective-permute-start | bytes 1572872 | tf_op jit(solution)/shard_map/ppermute | solution.py:294
  110.0 23.2 %collective-permute-start.2 = (f32[32,16,256]{2,1,0:T(8,128)S(1)}, f32[32,16,256]{2,1,0:T(8,128)}, u32[]{:S(2)}, u32[]{:S(2)}) collective-permute-start(f32[32,16,256]{2,1,0:T(8,128)S(1)} %bitcast.25), channel_id=1, source_target_pairs={{0,32},{16,48},{32,0},{48,16},{1,33},{17,49},{33,1},{49,17},{2,34}... | collective-permute-start | bytes 1572872 | tf_op jit(solution)/shard_map/ppermute | solution.py:294
  113.4 36.3 %all-to-all-start.4 = ((f32[32,2,16,128]{3,2,1,0:T(8,128)}), f32[32,2,16,128]{3,2,1,0:T(8,128)S(1)}, u32[]{:S(2)}, u32[]{:S(2)}) async-start(f32[32,2,16,128]{3,2,1,0:T(8,128)} %bitcast.11), calls=%async_computation.4 | async-start | bytes 1048576 | tf_op jit(solution)/shard_map/all_to_all | solution.py:304
  121.9 27.7 %copy-start = (f32[16,1,32,256]{3,2,1,0:T(8,128)S(1)}, f32[16,1,32,256]{3,2,1,0:T(8,128)}, u32[]{:S(2)}) copy-start(f32[16,1,32,256]{3,2,1,0:T(8,128)} %param.3) | copy-start | bytes 1572868
  121.9 35.9 %collective-permute-start.6 = (f32[32,16,256]{2,1,0:T(8,128)S(1)}, f32[32,16,256]{2,1,0:T(8,128)}, u32[]{:S(2)}, u32[]{:S(2)}) collective-permute-start(f32[32,16,256]{2,1,0:T(8,128)S(1)} %place.2.row0), channel_id=1, source_target_pairs={{0,32},{16,48},{32,0},{48,16},{1,33},{17,49},{33,1},{49,17},{2,34}... | collective-permute-start | bytes 1572872 | tf_op jit(solution)/shard_map/ppermute | solution.py:294
  135.5 15.5 %copy-start.5 = (f32[32,16,256]{2,1,0:T(8,128)}, f32[32,16,256]{2,1,0:T(8,128)S(1)}, u32[]{:S(2)}) copy-start(f32[32,16,256]{2,1,0:T(8,128)S(1)} %get-tuple-element.12.own_ref) | copy-start | bytes 1572868
  135.5 29.1 %collective-permute-start.1 = (f32[32,16,256]{2,1,0:T(8,128)S(1)}, f32[32,16,256]{2,1,0:T(8,128)}, u32[]{:S(2)}, u32[]{:S(2)}) collective-permute-start(f32[32,16,256]{2,1,0:T(8,128)S(1)} %get-tuple-element.12.own_ref), channel_id=1, source_target_pairs={{0,16},{16,0},{32,48},{48,32},{1,17},{17,1},{33,49},{49,33},{2,18}... | collective-permute-start | bytes 1572872 | tf_op jit(solution)/shard_map/ppermute | solution.py:294
  152.1 69.0 %all-to-all-start.5 = ((f32[16,4,16,256]{3,2,1,0:T(8,128)}), f32[16,4,16,256]{3,2,1,0:T(8,128)S(1)}, u32[]{:S(2)}, u32[]{:S(2)}) async-start(f32[16,4,16,256]{3,2,1,0:T(8,128)} %broadcast_in_dim.32), calls=%async_computation.5 | async-start | bytes 2097152 | tf_op jit(solution)/shard_map/all_to_all | solution.py:298
  155.8 63.7 %collective-permute-start.5 = (f32[32,16,256]{2,1,0:T(8,128)S(1)}, f32[32,16,256]{2,1,0:T(8,128)S(1)}, u32[]{:S(2)}, u32[]{:S(2)}) collective-permute-start(f32[32,16,256]{2,1,0:T(8,128)S(1)} %place.2.row0), channel_id=1, source_target_pairs={{0,16},{16,0},{32,48},{48,32},{1,17},{17,1},{33,49},{49,33},{2,18}... | collective-permute-start | bytes 1572872 | tf_op jit(solution)/shard_map/ppermute | solution.py:294
  157.8 62.5 %collective-permute-start.7 = (f32[32,16,256]{2,1,0:T(8,128)}, f32[32,16,256]{2,1,0:T(8,128)S(1)}, u32[]{:S(2)}, u32[]{:S(2)}) collective-permute-start(f32[32,16,256]{2,1,0:T(8,128)} %collective-permute-done.6.row2), channel_id=1, source_target_pairs={{0,16},{16,0},{32,48},{48,32},{1,17},{17,1},{33,49},{49,33},{2,18}... | collective-permute-start | bytes 1572872 | tf_op jit(solution)/shard_map/ppermute | solution.py:294
  160.1 29.2 %collective-permute-start.3 = (f32[32,16,256]{2,1,0:T(8,128)}, f32[32,16,256]{2,1,0:T(8,128)S(1)}, u32[]{:S(2)}, u32[]{:S(2)}) collective-permute-start(f32[32,16,256]{2,1,0:T(8,128)} %get-tuple-element.13.up_own), channel_id=1, source_target_pairs={{0,16},{16,0},{32,48},{48,32},{1,17},{17,1},{33,49},{49,33},{2,18}... | collective-permute-start | bytes 1572872 | tf_op jit(solution)/shard_map/ppermute | solution.py:294
  162.1 27.2 %collective-permute-start.4 = (f32[32,16,256]{2,1,0:T(8,128)}, f32[32,16,256]{2,1,0:T(8,128)S(1)}, u32[]{:S(2)}, u32[]{:S(2)}) collective-permute-start(f32[32,16,256]{2,1,0:T(8,128)} %get-tuple-element.11.low_own), channel_id=1, source_target_pairs={{0,16},{16,0},{32,48},{48,32},{1,17},{17,1},{33,49},{49,33},{2,18}... | collective-permute-start | bytes 1572872 | tf_op jit(solution)/shard_map/ppermute | solution.py:294
  164.6 1.0 copy-start.6
  217.5 1.0 copy-start.1
  218.5 1.0 copy-start.3
  220.3 0.8 copy-start.9
  221.1 1.2 copy-start.2
  222.3 1.2 copy-start.4
  223.5 1.0 copy-start.8
  224.6 1.0 copy-start.10
  (2 other events, 1.5 us)

commit v2 on v1

--- a/solution.py
+++ b/solution.py
@@ -20,7 +20,10 @@
 
 VMEM = pl.BlockSpec(memory_space=pltpu.VMEM)
 SMEM = pl.BlockSpec(memory_space=pltpu.SMEM)
-PARAMS = pltpu.CompilerParams(vmem_limit_bytes=40 << 20)
+
+
+def params(mib):
+    return pltpu.CompilerParams(vmem_limit_bytes=mib << 20)
 
 
 def contract(a, b, dims):
@@ -66,7 +69,7 @@
         out_shape=jax.ShapeDtypeStruct((2 * SHARDS, BLK, TILE), jnp.float32),
         in_specs=[SMEM, SMEM, VMEM],
         out_specs=VMEM,
-        compiler_params=PARAMS,
+        compiler_params=params(4),
         name="spread_rows",
     )(where, index_map, child)
 
@@ -92,8 +95,36 @@
         out_shape=jax.ShapeDtypeStruct((SHARDS, BLK, WIDE), jnp.float32),
         in_specs=[SMEM, SMEM, VMEM, VMEM],
         out_specs=VMEM,
-        compiler_params=PARAMS,
+        compiler_params=params(6),
         name="place",
+    )(where, index_map, received, parent)
+
+
+def corner_kernel(where_ref, map_ref, received_ref, parent_ref, out_ref):
+    col = where_ref[1]
+
+    def body(source, carry):
+        child = source // (SHARDS // 2)
+        block = map_ref[child, source % (SHARDS // 2) * COLS + col]
+        slot = block // (2 * COLS) * 2 + block % 2
+
+        @pl.when(slot < 2)
+        def _():
+            out_ref[slot] = parent_ref[slot] + received_ref[source]
+
+        return carry
+
+    lax.fori_loop(0, SHARDS, body, 0)
+
+
+def place_corner(where, index_map, received, parent):
+    return pl.pallas_call(
+        corner_kernel,
+        out_shape=jax.ShapeDtypeStruct((2, BLK, TILE), jnp.float32),
+        in_specs=[SMEM, SMEM, VMEM, VMEM],
+        out_specs=VMEM,
+        compiler_params=params(4),
+        name="place_corner",
     )(where, index_map, received, parent)
 
 
@@ -185,46 +216,49 @@
     lax.fori_loop(0, tiles, body, 0)
 
 
-def fill(m_ref, core, own_ref, other_ref):
-    own = pl.multiple_of(core * WIDE, WIDE)
-    other = pl.multiple_of((1 - core) * WIDE, WIDE)
-    for slot in range(SHARDS):
-        rows = slice(slot * BLK, (slot + 1) * BLK)
-        m_ref[rows, pl.ds(own, WIDE)] = own_ref[slot]
-        m_ref[rows, pl.ds(other, WIDE)] = other_ref[slot]
-
-
-def first_kernel(where_ref, own_ref, other_ref, w_ref, m_ref, t_ref):
-    fill(m_ref, where_ref[2] % 2, own_ref, other_ref)
+def corner_tile(row):
+    return row % 2 * 2 + row // 2
+
+
+def first_kernel(corner_ref, w_ref, m_ref, t_ref):
+    for row in range(ROWS):
+        low = corner_tile(row) * TILE
+        m_ref[:, low : low + TILE] = corner_ref[row]
     invert_factor(m_ref, w_ref, t_ref)
 
 
-def first_factor(where, own, other):
+def first_factor(corner):
     return pl.pallas_call(
         first_kernel,
         out_shape=jax.ShapeDtypeStruct((PANEL, PANEL), jnp.float32),
-        in_specs=[SMEM, VMEM, VMEM],
+        in_specs=[VMEM],
         out_specs=VMEM,
         scratch_shapes=[
             pltpu.VMEM((PANEL, PANEL), jnp.float32),
             pltpu.VMEM((TILE, TILE), jnp.float32),
         ],
-        compiler_params=PARAMS,
+        compiler_params=params(8),
         cost_estimate=pl.CostEstimate(flops=60_000_000_000, bytes_accessed=4 << 20, transcendentals=0),
         name="first_factor",
-    )(where, own, other)
-
-
-def second_kernel(where_ref, inv_ref, up_own, up_other, low_own, low_other, w_ref, x_ref, m_ref, t_ref):
-    core = where_ref[2] % 2
-    fill(m_ref, core, up_own, up_other)
-    x_ref[...] = dot(inv_ref[...], m_ref[...])
-    fill(m_ref, core, low_own, low_other)
-    m_ref[...] = m_ref[...] - t_dot(x_ref[...], x_ref[...])
+    )(corner)
+
+
+def fill(row, refs, into):
+    for number, ref in enumerate(refs):
+        chunk = (row // 2 ^ number // 2) * 2 + (row % 2 ^ number % 2)
+        low = pl.multiple_of(chunk * WIDE, WIDE)
+        for slot in range(SHARDS):
+            into[slot * BLK : (slot + 1) * BLK, pl.ds(low, WIDE)] = ref[slot]
+
+
+def second_kernel(where_ref, inv_ref, own, core, across, both, w_ref, x_ref, a_ref, m_ref, t_ref):
+    fill(where_ref[2], (own, core, across, both), a_ref)
+    x_ref[...] = dot_t(inv_ref[...], a_ref[:, :PANEL])
+    m_ref[...] = a_ref[:, PANEL:] - t_dot(x_ref[...], x_ref[...])
     invert_factor(m_ref, w_ref, t_ref)
 
 
-def second_factor(where, inv, up_own, up_other, low_own, low_other):
+def second_factor(where, inv, pieces):
     shape = jax.ShapeDtypeStruct((PANEL, PANEL), jnp.float32)
     return pl.pallas_call(
         second_kernel,
@@ -232,13 +266,14 @@
         in_specs=[SMEM] + [VMEM] * 5,
         out_specs=(VMEM, VMEM),
         scratch_shapes=[
+            pltpu.VMEM((PANEL, 2 * PANEL), jnp.float32),
             pltpu.VMEM((PANEL, PANEL), jnp.float32),
             pltpu.VMEM((TILE, TILE), jnp.float32),
         ],
-        compiler_params=PARAMS,
+        compiler_params=params(16),
         cost_estimate=pl.CostEstimate(flops=60_000_000_000, bytes_accessed=8 << 20, transcendentals=0),
         name="second_factor",
-    )(where, inv, up_own, up_other, low_own, low_other)
+    )(where, inv, *pieces)
 
 
 def finish_kernel(
@@ -246,11 +281,7 @@
     rows_ref, cols0_ref, cols1_ref,
 ):
     col, row, shard = where_ref[1], where_ref[2], where_ref[3]
-    for number, ref in enumerate((row0, row1, row2, row3)):
-        chunk = (row // 2 ^ number // 2) * 2 + (row % 2 ^ number % 2)
-        low = pl.multiple_of(chunk * WIDE, WIDE)
-        for slot in range(SHARDS):
-            rows_ref[slot * BLK : (slot + 1) * BLK, pl.ds(low, WIDE)] = ref[slot]
+    fill(row, (row0, row1, row2, row3), rows_ref)
     for q in range(COLS):
         for half in range(2):
             at = slice(q * 2 * BLK + half * BLK, q * 2 * BLK + (half + 1) * BLK)
@@ -285,7 +316,7 @@
             pltpu.VMEM((PANEL, WIDE), jnp.float32),
             pltpu.VMEM((PANEL, WIDE), jnp.float32),
         ],
-        compiler_params=PARAMS,
+        compiler_params=params(24),
         name="finish",
     )(where, inv0, inv1, x01, cols, *rows, front)
 
@@ -302,6 +333,11 @@
 
 def exchange(x, axis):
     return lax.all_to_all(x, axis, split_axis=0, concat_axis=0, tiled=True)
+
+
+def over_rows(x):
+    across = swap(x, "row", 2)
+    return x, swap(x, "row", 1), across, swap(across, "row", 1)
 
 
 def local(parent_front, child_schur, index_map):
@@ -310,33 +346,28 @@
     where = jnp.stack([shard // (SHARDS // 2), col, row, shard]).astype(jnp.int32)
     parent = parent_front.reshape(SHARDS, BLK, WIDE)
 
+    crossed = swap(parent[:2, :, TILE:], "row", 2)
+    corner = to_all(jnp.where(row < 2, parent[:2, :, :TILE], crossed), "sub", SUBS)[0]
+    spread = spread_rows(where, index_map, child_schur)
+    tiles = jnp.stack([spread[corner_tile(i)] for i in range(ROWS)])
+    tiles = jnp.broadcast_to(tiles[None], (SUBS, ROWS, BLK, TILE)).reshape(SHARDS, BLK, TILE)
+    corner = place_corner(where, index_map, exchange(tiles, ("sub", "row")), corner)
+    corner = to_all(corner, "col", COLS).reshape(PANEL, TILE)
+    inv0 = first_factor(to_all(corner, "row", ROWS))
+
     chunk = exchange(parent.reshape(SUBS, SHARDS // SUBS, BLK, WIDE), "sub")[0]
     parent_low = to_all(chunk, "sub", SUBS).reshape(SHARDS, BLK, WIDE)
-
-    spread = spread_rows(where, index_map, child_schur).reshape(SHARDS, 2, BLK, TILE)
+    spread = spread.reshape(SHARDS, 2, BLK, TILE)
     low = jnp.broadcast_to(spread[None, :ROWS], (SUBS, ROWS, 2, BLK, TILE))
     low = exchange(low.reshape(SHARDS, 2, BLK, TILE), ("sub", "row"))
     rows = place(where, index_map, low, parent_low)
-    pivots = to_all(rows[:4], "col", COLS)
+    pivots = to_all(rows[2:4], "col", COLS).reshape(SHARDS, BLK, WIDE)
+    inv1, x01 = second_factor(where, inv0, over_rows(pivots))
 
     received = exchange(spread, ("sub", "row"))
     front = place(where, index_map, received, parent)
     cols = to_all(front[:4], "col", COLS)
-
-    upper = pivots[:, :2].reshape(SHARDS, BLK, WIDE)
-    lower = pivots[:, 2:].reshape(SHARDS, BLK, WIDE)
-    left = row < 2
-    crossed = swap(jnp.where(left, upper, lower), "row", 2)
-    diag0 = jnp.where(left, upper, crossed)
-    diag1 = jnp.where(left, crossed, lower)
-    inv0 = first_factor(where, diag0, swap(diag0, "row", 1))
-    above = jnp.where(left, swap(upper, "row", 2), upper)
-    inv1, x01 = second_factor(
-        where, inv0, above, swap(above, "row", 1), diag1, swap(diag1, "row", 1)
-    )
-    across = swap(rows, "row", 2)
-    pieces = (rows, swap(rows, "row", 1), across, swap(across, "row", 1))
-    out = finish(where, inv0, inv1, x01, cols, pieces, front)
+    out = finish(where, inv0, inv1, x01, cols, over_rows(rows), front)
     return out.reshape(parent_front.shape)
 
 

time: 243 us -> 296 us (1.22)
  blocking collectives: 19.1 us -> 56.1 us
  waiting for transfers between devices: 62.1 us -> 81.1 us
  starting transfers between devices: 68.2 us -> 64.8 us
    all_to_all x1 -> x2, blocking collectives: 19.1 us -> 39.6 us  [to_all(): lax.all_to_all(jnp.broadcast_to(x[None], (count, *x.shape)), axis, split_...]
    all_to_all x3, waiting for transfers between devices: 28.3 us -> 48.2 us  [exchange(): return lax.all_to_all(x, axis, split_axis=0, concat_axis=0, tiled=True)]
    all_to_all x0 -> x1, blocking collectives: none -> 16.5 us  [exchange(): return lax.all_to_all(x, axis, split_axis=0, concat_axis=0, tiled=True)]
    all_to_all x2 -> x4, starting transfers between devices: 13 us -> 29.2 us  [to_all(): lax.all_to_all(jnp.broadcast_to(x[None], (count, *x.shape)), axis, split_...]
    ppermute x8 -> x7, starting transfers between devices: 31.6 us -> 19.5 us  [swap(): return lax.ppermute(x, axis, [(i, i ^ bit) for i in range(ROWS)])]
    all_to_all x2 -> x4, waiting for transfers between devices: 25.9 us -> 17.6 us  [to_all(): lax.all_to_all(jnp.broadcast_to(x[None], (count, *x.shape)), axis, split_...]
    ppermute x8 -> x7, waiting for transfers between devices: 7.84 us -> 15.3 us  [swap(): return lax.ppermute(x, axis, [(i, i ^ bit) for i in range(ROWS)])]
    all_to_all x3, starting transfers between devices: 23.5 us -> 16.1 us  [exchange(): return lax.all_to_all(x, axis, split_axis=0, concat_axis=0, tiled=True)]
  transfers between devices with their start and end apart: 13 -> 14, of which waited for: 4 -> 6; matrix products, arithmetic and copies ran while one was open for 2% -> 1% of each run, Pallas kernels for 24% -> 21%
where the time goes in v2:
time: 296 us; the launch traced here: 295 us
  waiting for transfers between devices  81.1 us (27%)
  Pallas kernels  76.2 us (26%)
  starting transfers between devices  64.8 us (22%)
  blocking collectives  56.1 us (19%)
  local copies, waits for them, and re-layouts  15.5 us (5%)
    all_to_all x3, waiting for transfers between devices, exchange(): return lax.all_to_all(x, axis, split_axis=0, concat_axis=0, tiled=True)  48.2 us
    all_to_all x2, blocking collectives, to_all(): lax.all_to_all(jnp.broadcast_to(x[None], (count, *x.shape)), axis, split_...  39.6 us
    all_to_all x4, starting transfers between devices, to_all(): lax.all_to_all(jnp.broadcast_to(x[None], (count, *x.shape)), axis, split_...  29.2 us
    pallas_call x1, Pallas kernels, second_factor(): pl.pallas_call(second_kernel, out_shape=(shape, shape), in_specs=[SMEM] +...  28 us
    pallas_call x1, Pallas kernels, first_factor(): pl.pallas_call(first_kernel, out_shape=jax.ShapeDtypeStruct((PANEL, PANEL...  22.6 us
    ppermute x7, starting transfers between devices, swap(): return lax.ppermute(x, axis, [(i, i ^ bit) for i in range(ROWS)])  19.5 us
    all_to_all x4, waiting for transfers between devices, to_all(): lax.all_to_all(jnp.broadcast_to(x[None], (count, *x.shape)), axis, split_...  17.6 us
    all_to_all x1, blocking collectives, exchange(): return lax.all_to_all(x, axis, split_axis=0, concat_axis=0, tiled=True)  16.5 us
  transfers between devices with their start and end apart: 14, of which 6 were waited for; matrix products, arithmetic and copies ran while one was open for 1% of the time, Pallas kernels for 21%

profile of v2, /device:TPU:1, one launch (start us, length us, event | category | flops | bytes accessed | tf_op | source)
XLA Modules:
  0.0 294.8 jit_solution(14378241686432900087)
XLA Ops:
  0.7 3.9 %collective-permute-start = (f32[2,16,128]{2,1,0:T(8,128)S(1)}, f32[2,16,128]{2,1,0:T(8,128)S(1)}, u32[]{:S(2)}, u32[]{:S(2)}) collective-permute-start(f32[2,16,128]{2,1,0:T(8,128)S(1)} %slice.50), channel_id=1, source_target_pairs={{0,32},{16,48},{32,0},{48,16},{1,33},{17,49},{33,1},{49,17},{2,34}... | collective-permute-start | bytes 49160 | tf_op jit(solution)/shard_map/ppermute | solution.py:325
  6.3 5.2 %spread_rows.1 = f32[64,16,128]{2,1,0:T(8,128)} custom-call(s32[4]{0:T(128)S(1)} %pad_add_fusion.where_ref, s32[2,256]{1,0:T(2,128)S(1)} %copy-done.9, f32[16,4096]{1,0:T(8,128)S(1)} %copy-done.8), custom_call_target="tpu_custom_call" | custom-call | tf_op jit(solution)/shard_map/spread_rows/pallas_call | solution.py:67
  12.9 10.0 %all-to-all-start.1 = ((f32[8,2,16,128]{3,2,1,0:T(8,128)}), f32[8,2,16,128]{3,2,1,0:T(8,128)S(1)}, u32[]{:S(2)}, u32[]{:S(2)}) async-start(f32[8,2,16,128]{3,2,1,0:T(8,128)} %broadcast_in_dim.23), calls=%async_computation.1 | async-start | bytes 262144 | tf_op jit(solution)/shard_map/all_to_all | solution.py:329
  23.7 7.2 %all-to-all-done.1 = f32[8,2,16,128]{3,2,1,0:T(8,128)S(1)} async-done(((f32[8,2,16,128]{3,2,1,0:T(8,128)}), f32[8,2,16,128]{3,2,1,0:T(8,128)S(1)}, u32[]{:S(2)}, u32[]{:S(2)}) %all-to-all-start.1) | async-done | bytes 131104 | tf_op jit(solution)/shard_map/all_to_all | solution.py:329
  30.9 16.5 %all_to_all.50.received_ref = f32[32,16,128]{2,1,0:T(8,128)S(1)} all-to-all(f32[32,16,128]{2,1,0:T(8,128)S(1)} %bitcast.22), channel_id=1, replica_groups=mesh['sub'=8,'row'=4,'col'=16] {'sub','row'}, dimensions={0} | all-to-all | bytes 524288 | tf_op jit(solution)/shard_map/all_to_all | solution.py:335
  47.4 3.5 %all-to-all-start.5 = ((f32[8,4,16,256]{3,2,1,0:T(8,128)}), f32[8,4,16,256]{3,2,1,0:T(8,128)S(1)}, u32[]{:S(2)}, u32[]{:S(2)}) async-start(f32[8,4,16,256]{3,2,1,0:T(8,128)} %bitcast.10), calls=%async_computation.5 | async-start | bytes 1048576 | tf_op jit(solution)/shard_map/all_to_all | solution.py:335
  52.5 15.4 %all-to-all-done.5 = f32[8,4,16,256]{3,2,1,0:T(8,128)S(1)} async-done(((f32[8,4,16,256]{3,2,1,0:T(8,128)}), f32[8,4,16,256]{3,2,1,0:T(8,128)S(1)}, u32[]{:S(2)}, u32[]{:S(2)}) %all-to-all-start.5) | async-done | bytes 524320 | tf_op jit(solution)/shard_map/all_to_all | solution.py:335
  68.6 9.1 %all-to-all-start.2 = ((f32[16,2,16,128]{3,2,1,0:T(8,128)}), f32[16,2,16,128]{3,2,1,0:T(8,128)S(1)}, u32[]{:S(2)}, u32[]{:S(2)}) async-start(f32[16,2,16,128]{3,2,1,0:T(8,128)} %broadcast_in_dim.24), calls=%async_computation.2 | async-start | bytes 524288 | tf_op jit(solution)/shard_map/all_to_all | solution.py:329
  78.5 10.4 %all-to-all-done.2 = f32[16,2,16,128]{3,2,1,0:T(8,128)S(1)} async-done(((f32[16,2,16,128]{3,2,1,0:T(8,128)}), f32[16,2,16,128]{3,2,1,0:T(8,128)S(1)}, u32[]{:S(2)}, u32[]{:S(2)}) %all-to-all-start.2) | async-done | bytes 262176 | tf_op jit(solution)/shard_map/all_to_all | solution.py:329
  89.8 6.9 %all-to-all-start.4 = ((f32[32,2,16,128]{3,2,1,0:T(8,128)}), f32[32,2,16,128]{3,2,1,0:T(8,128)S(1)}, u32[]{:S(2)}, u32[]{:S(2)}) async-start(f32[32,2,16,128]{3,2,1,0:T(8,128)} %bitcast.9), calls=%async_computation.4 | async-start | bytes 1048576 | tf_op jit(solution)/shard_map/all_to_all | solution.py:335
  96.7 17.1 %all-to-all-done.4.received_ref = f32[32,2,16,128]{3,2,1,0:T(8,128)S(1)} async-done(((f32[32,2,16,128]{3,2,1,0:T(8,128)}), f32[32,2,16,128]{3,2,1,0:T(8,128)S(1)}, u32[]{:S(2)}, u32[]{:S(2)}) %all-to-all-start.4) | async-done | bytes 524320 | tf_op jit(solution)/shard_map/all_to_all | solution.py:335
  113.8 19.1 %all_to_all.51 = f32[8,4,16,256]{3,2,1,0:T(8,128)S(1)} all-to-all(f32[8,4,16,256]{3,2,1,0:T(8,128)S(1)} %broadcast_in_dim.60), channel_id=1, replica_groups=mesh['sub'=8,'row'=4,'col'=16] {'sub'}, dimensions={0} | all-to-all | bytes 1048576 | tf_op jit(solution)/shard_map/all_to_all | solution.py:329
  133.0 5.7 %all-to-all-start.8 = ((f32[32,2,16,128]{3,2,1,0:T(8,128)}), f32[32,2,16,128]{3,2,1,0:T(8,128)S(1)}, u32[]{:S(2)}, u32[]{:S(2)}) async-start(f32[32,2,16,128]{3,2,1,0:T(8,128)} %bitcast.14), calls=%async_computation.8 | async-start | bytes 1048576 | tf_op jit(solution)/shard_map/all_to_all | solution.py:335
  140.1 15.7 %all-to-all-done.8.received_ref = f32[32,2,16,128]{3,2,1,0:T(8,128)S(1)} async-done(((f32[32,2,16,128]{3,2,1,0:T(8,128)}), f32[32,2,16,128]{3,2,1,0:T(8,128)S(1)}, u32[]{:S(2)}, u32[]{:S(2)}) %all-to-all-start.8) | async-done | bytes 524320 | tf_op jit(solution)/shard_map/all_to_all | solution.py:335
  155.8 20.5 %all_to_all.52 = f32[16,2,16,256]{3,2,1,0:T(8,128)} all-to-all(f32[16,2,16,256]{3,2,1,0:T(8,128)S(1)} %broadcast_in_dim.61), channel_id=1, replica_groups=mesh['sub'=8,'row'=4,'col'=16] {'col'}, dimensions={0} | all-to-all | bytes 1048576 | tf_op jit(solution)/shard_map/all_to_all | solution.py:329
  177.4 6.4 %all-to-all-start.3 = ((f32[4,512,128]{2,1,0:T(8,128)}), f32[4,512,128]{2,1,0:T(8,128)S(1)}, u32[]{:S(2)}, u32[]{:S(2)}) async-start(f32[4,512,128]{2,1,0:T(8,128)} %broadcast_in_dim.26), calls=%async_computation.3 | async-start | bytes 2097152 | tf_op jit(solution)/shard_map/all_to_all | solution.py:329
  183.8 3.3 %collective-permute-start.2 = (f32[32,16,256]{2,1,0:T(8,128)}, f32[32,16,256]{2,1,0:T(8,128)}, u32[]{:S(2)}, u32[]{:S(2)}) collective-permute-start(f32[32,16,256]{2,1,0:T(8,128)} %bitcast.13.own), channel_id=1, source_target_pairs={{0,32},{16,48},{32,0},{48,16},{1,33},{17,49},{33,1},{49,17},{2,34}... | collective-permute-start | bytes 1572872 | tf_op jit(solution)/shard_map/ppermute | solution.py:325
  193.4 15.3 %collective-permute-done.2.across = f32[32,16,256]{2,1,0:T(8,128)} collective-permute-done((f32[32,16,256]{2,1,0:T(8,128)}, f32[32,16,256]{2,1,0:T(8,128)}, u32[]{:S(2)}, u32[]{:S(2)}) %collective-permute-start.2) | collective-permute-done | bytes 524320 | tf_op jit(solution)/shard_map/ppermute | solution.py:325
  208.7 3.2 %collective-permute-start.3 = (f32[32,16,256]{2,1,0:T(8,128)}, f32[32,16,256]{2,1,0:T(8,128)}, u32[]{:S(2)}, u32[]{:S(2)}) collective-permute-start(f32[32,16,256]{2,1,0:T(8,128)} %collective-permute-done.2.across), channel_id=1, source_target_pairs={{0,16},{16,0},{32,48},{48,32},{1,17},{17,1},{33,49},{49,33},{2,18}... | collective-permute-start | bytes 1572872 | tf_op jit(solution)/shard_map/ppermute | solution.py:325
  213.1 3.7 %all-to-all-start.9 = ((f32[16,4,16,256]{3,2,1,0:T(8,128)}), f32[16,4,16,256]{3,2,1,0:T(8,128)S(1)}, u32[]{:S(2)}, u32[]{:S(2)}) async-start(f32[16,4,16,256]{3,2,1,0:T(8,128)} %broadcast_in_dim.62), calls=%async_computation.9 | async-start | bytes 2097152 | tf_op jit(solution)/shard_map/all_to_all | solution.py:329
  216.7 22.6 %first_factor.1.inv_ref.inv0_ref = f32[512,512]{1,0:T(8,128)S(1)} custom-call(f32[4,512,128]{2,1,0:T(8,128)S(1)} %all-to-all-done.3.corner_ref), custom_call_target="tpu_custom_call" | custom-call | flops 60000002048 | bytes 4194304 | tf_op jit(solution)/shard_map/first_factor/pallas_call | solution.py:231
  241.3 2.6 collective-permute-start.6
  244.0 28.0 %second_factor.1 = (f32[512,512]{1,0:T(8,128)S(1)}, f32[512,512]{1,0:T(8,128)S(1)}) custom-call(s32[4]{0:T(128)S(1)} %pad_add_fusion.where_ref, f32[512,512]{1,0:T(8,128)S(1)} %first_factor.1.inv_ref.inv0_ref, f32[32,16,256]{2,1,0:T(8,128)} %bitcast.13.own, f32[32,16,256]{2,1,0:T(8,128)} %collective-permute-done.1.core, ...), custom_call_target="tpu_custom_call" | custom-call | flops 60000002048 | bytes 8388608 | tf_op jit(solution)/shard_map/second_factor/pallas_call | solution.py:263
  279.1 15.7 %finish.1 = f32[32,16,256]{2,1,0:T(8,128)} custom-call(s32[4]{0:T(128)S(1)} %pad_add_fusion.where_ref, f32[512,512]{1,0:T(8,128)S(1)} %copy-done.1, f32[512,512]{1,0:T(8,128)S(1)} %get-tuple-element.7.inv1_ref, f32[512,512]{1,0:T(8,128)S(1)} %copy-done.3, f32[16,4,16,256]{3,2,1,0:T(8,128)S(1)} %all-to-all-done.9.cols_ref, f32[32,16,256]{2,1,0:T(8,128)S(1)} %place.2.row0, ...), custom_call_target="tpu_custom_call" | custom-call | tf_op jit(solution)/shard_map/finish/pallas_call | solution.py:309
  (52 shorter events, 27.5 us)
Async XLA Ops:
  0.7 10.8 %collective-permute-start = (f32[2,16,128]{2,1,0:T(8,128)S(1)}, f32[2,16,128]{2,1,0:T(8,128)S(1)}, u32[]{:S(2)}, u32[]{:S(2)}) collective-permute-start(f32[2,16,128]{2,1,0:T(8,128)S(1)} %slice.50), channel_id=1, source_target_pairs={{0,32},{16,48},{32,0},{48,16},{1,33},{17,49},{33,1},{49,17},{2,34}... | collective-permute-start | bytes 49160 | tf_op jit(solution)/shard_map/ppermute | solution.py:325
  4.7 0.7 copy-start.9
  5.4 0.9 copy-start.8
  12.9 18.0 %all-to-all-start.1 = ((f32[8,2,16,128]{3,2,1,0:T(8,128)}), f32[8,2,16,128]{3,2,1,0:T(8,128)S(1)}, u32[]{:S(2)}, u32[]{:S(2)}) async-start(f32[8,2,16,128]{3,2,1,0:T(8,128)} %broadcast_in_dim.23), calls=%async_computation.1 | async-start | bytes 262144 | tf_op jit(solution)/shard_map/all_to_all | solution.py:329
  47.4 20.5 %all-to-all-start.5 = ((f32[8,4,16,256]{3,2,1,0:T(8,128)}), f32[8,4,16,256]{3,2,1,0:T(8,128)S(1)}, u32[]{:S(2)}, u32[]{:S(2)}) async-start(f32[8,4,16,256]{3,2,1,0:T(8,128)} %bitcast.10), calls=%async_computation.5 | async-start | bytes 1048576 | tf_op jit(solution)/shard_map/all_to_all | solution.py:335
  68.6 20.3 %all-to-all-start.2 = ((f32[16,2,16,128]{3,2,1,0:T(8,128)}), f32[16,2,16,128]{3,2,1,0:T(8,128)S(1)}, u32[]{:S(2)}, u32[]{:S(2)}) async-start(f32[16,2,16,128]{3,2,1,0:T(8,128)} %broadcast_in_dim.24), calls=%async_computation.2 | async-start | bytes 524288 | tf_op jit(solution)/shard_map/all_to_all | solution.py:329
  89.8 24.0 %all-to-all-start.4 = ((f32[32,2,16,128]{3,2,1,0:T(8,128)}), f32[32,2,16,128]{3,2,1,0:T(8,128)S(1)}, u32[]{:S(2)}, u32[]{:S(2)}) async-start(f32[32,2,16,128]{3,2,1,0:T(8,128)} %bitcast.9), calls=%async_computation.4 | async-start | bytes 1048576 | tf_op jit(solution)/shard_map/all_to_all | solution.py:335
  133.0 22.8 %all-to-all-start.8 = ((f32[32,2,16,128]{3,2,1,0:T(8,128)}), f32[32,2,16,128]{3,2,1,0:T(8,128)S(1)}, u32[]{:S(2)}, u32[]{:S(2)}) async-start(f32[32,2,16,128]{3,2,1,0:T(8,128)} %bitcast.14), calls=%async_computation.8 | async-start | bytes 1048576 | tf_op jit(solution)/shard_map/all_to_all | solution.py:335
  177.4 34.6 %all-to-all-start.3 = ((f32[4,512,128]{2,1,0:T(8,128)}), f32[4,512,128]{2,1,0:T(8,128)S(1)}, u32[]{:S(2)}, u32[]{:S(2)}) async-start(f32[4,512,128]{2,1,0:T(8,128)} %broadcast_in_dim.26), calls=%async_computation.3 | async-start | bytes 2097152 | tf_op jit(solution)/shard_map/all_to_all | solution.py:329
  183.8 24.9 %collective-permute-start.2 = (f32[32,16,256]{2,1,0:T(8,128)}, f32[32,16,256]{2,1,0:T(8,128)}, u32[]{:S(2)}, u32[]{:S(2)}) collective-permute-start(f32[32,16,256]{2,1,0:T(8,128)} %bitcast.13.own), channel_id=1, source_target_pairs={{0,32},{16,48},{32,0},{48,16},{1,33},{17,49},{33,1},{49,17},{2,34}... | collective-permute-start | bytes 1572872 | tf_op jit(solution)/shard_map/ppermute | solution.py:325
  188.9 52.4 %collective-permute-start.5 = (f32[32,16,256]{2,1,0:T(8,128)S(1)}, f32[32,16,256]{2,1,0:T(8,128)}, u32[]{:S(2)}, u32[]{:S(2)}) collective-permute-start(f32[32,16,256]{2,1,0:T(8,128)S(1)} %place.2.row0), channel_id=1, source_target_pairs={{0,32},{16,48},{32,0},{48,16},{1,33},{17,49},{33,1},{49,17},{2,34}... | collective-permute-start | bytes 1572872 | tf_op jit(solution)/shard_map/ppermute | solution.py:325
  190.9 53.0 %collective-permute-start.1 = (f32[32,16,256]{2,1,0:T(8,128)}, f32[32,16,256]{2,1,0:T(8,128)}, u32[]{:S(2)}, u32[]{:S(2)}) collective-permute-start(f32[32,16,256]{2,1,0:T(8,128)} %bitcast.13.own), channel_id=1, source_target_pairs={{0,16},{16,0},{32,48},{48,32},{1,17},{17,1},{33,49},{49,33},{2,18}... | collective-permute-start | bytes 1572872 | tf_op jit(solution)/shard_map/ppermute | solution.py:325
  208.7 35.2 %collective-permute-start.3 = (f32[32,16,256]{2,1,0:T(8,128)}, f32[32,16,256]{2,1,0:T(8,128)}, u32[]{:S(2)}, u32[]{:S(2)}) collective-permute-start(f32[32,16,256]{2,1,0:T(8,128)} %collective-permute-done.2.across), channel_id=1, source_target_pairs={{0,16},{16,0},{32,48},{48,32},{1,17},{17,1},{33,49},{49,33},{2,18}... | collective-permute-start | bytes 1572872 | tf_op jit(solution)/shard_map/ppermute | solution.py:325
  213.1 61.5 %all-to-all-start.9 = ((f32[16,4,16,256]{3,2,1,0:T(8,128)}), f32[16,4,16,256]{3,2,1,0:T(8,128)S(1)}, u32[]{:S(2)}, u32[]{:S(2)}) async-start(f32[16,4,16,256]{3,2,1,0:T(8,128)} %broadcast_in_dim.62), calls=%async_computation.9 | async-start | bytes 2097152 | tf_op jit(solution)/shard_map/all_to_all | solution.py:329
  239.4 32.6 %copy-start = (f32[512,512]{1,0:T(8,128)}, f32[512,512]{1,0:T(8,128)S(1)}, u32[]{:S(2)}) copy-start(f32[512,512]{1,0:T(8,128)S(1)} %first_factor.1.inv_ref.inv0_ref) | copy-start | bytes 3145732
  239.4 33.6 %collective-permute-start.4 = (f32[32,16,256]{2,1,0:T(8,128)S(1)}, f32[32,16,256]{2,1,0:T(8,128)S(1)}, u32[]{:S(2)}, u32[]{:S(2)}) collective-permute-start(f32[32,16,256]{2,1,0:T(8,128)S(1)} %place.2.row0), channel_id=1, source_target_pairs={{0,16},{16,0},{32,48},{48,32},{1,17},{17,1},{33,49},{49,33},{2,18}... | collective-permute-start | bytes 1572872 | tf_op jit(solution)/shard_map/ppermute | solution.py:325
  241.3 32.4 %collective-permute-start.6 = (f32[32,16,256]{2,1,0:T(8,128)}, f32[32,16,256]{2,1,0:T(8,128)S(1)}, u32[]{:S(2)}, u32[]{:S(2)}) collective-permute-start(f32[32,16,256]{2,1,0:T(8,128)} %collective-permute-done.5.row2), channel_id=1, source_target_pairs={{0,16},{16,0},{32,48},{48,32},{1,17},{17,1},{33,49},{49,33},{2,18}... | collective-permute-start | bytes 1572872 | tf_op jit(solution)/shard_map/ppermute | solution.py:325
  272.0 1.0 copy-start.2
  273.0 0.8 copy-start.4
  273.8 0.8 copy-start.6
  274.6 1.2 copy-start.1
  275.8 1.2 copy-start.3
  277.0 1.0 copy-start.5
  278.1 1.0 copy-start.7

commit v3 on v1

--- a/solution.py
+++ b/solution.py
@@ -20,7 +20,10 @@
 
 VMEM = pl.BlockSpec(memory_space=pltpu.VMEM)
 SMEM = pl.BlockSpec(memory_space=pltpu.SMEM)
-PARAMS = pltpu.CompilerParams(vmem_limit_bytes=40 << 20)
+
+
+def params(mib):
+    return pltpu.CompilerParams(vmem_limit_bytes=mib << 20)
 
 
 def contract(a, b, dims):
@@ -66,12 +69,17 @@
         out_shape=jax.ShapeDtypeStruct((2 * SHARDS, BLK, TILE), jnp.float32),
         in_specs=[SMEM, SMEM, VMEM],
         out_specs=VMEM,
-        compiler_params=PARAMS,
+        compiler_params=params(4),
         name="spread_rows",
     )(where, index_map, child)
 
 
-def place_kernel(where_ref, map_ref, received_ref, parent_ref, out_ref):
+def home(group):
+    far = group - SUBS
+    return (group, 0) if group < SUBS else (far // (SUBS - 1), far % (SUBS - 1) + 1)
+
+
+def place_kernel(where_ref, map_ref, received_ref, parent_ref, out_ref, dealt_ref):
     col = where_ref[1]
 
     def body(source, carry):
@@ -84,15 +92,22 @@
         return carry
 
     lax.fori_loop(0, SHARDS, body, 0)
+    for group in range(2 * SHARDS):
+        owner, number = home(group)
+        low = group % 2 * 8
+        dealt_ref[owner, number] = out_ref[group // 2, low : low + 8, :]
 
 
 def place(where, index_map, received, parent):
     return pl.pallas_call(
         place_kernel,
-        out_shape=jax.ShapeDtypeStruct((SHARDS, BLK, WIDE), jnp.float32),
+        out_shape=(
+            jax.ShapeDtypeStruct((SHARDS, BLK, WIDE), jnp.float32),
+            jax.ShapeDtypeStruct((SUBS, 8, 8, WIDE), jnp.float32),
+        ),
         in_specs=[SMEM, SMEM, VMEM, VMEM],
-        out_specs=VMEM,
-        compiler_params=PARAMS,
+        out_specs=(VMEM, VMEM),
+        compiler_params=params(6),
         name="place",
     )(where, index_map, received, parent)
 
@@ -185,60 +200,65 @@
     lax.fori_loop(0, tiles, body, 0)
 
 
-def fill(m_ref, core, own_ref, other_ref):
-    own = pl.multiple_of(core * WIDE, WIDE)
-    other = pl.multiple_of((1 - core) * WIDE, WIDE)
-    for slot in range(SHARDS):
-        rows = slice(slot * BLK, (slot + 1) * BLK)
-        m_ref[rows, pl.ds(own, WIDE)] = own_ref[slot]
-        m_ref[rows, pl.ds(other, WIDE)] = other_ref[slot]
-
-
-def first_kernel(where_ref, own_ref, other_ref, w_ref, m_ref, t_ref):
-    fill(m_ref, where_ref[2] % 2, own_ref, other_ref)
+def fill(row, refs, into, first, last):
+    for number, ref in enumerate(refs):
+        chunk = (row // 2 ^ number // 2) * 2 + (row % 2 ^ number % 2)
+
+        @pl.when((chunk >= first) & (chunk < last))
+        def _():
+            low = pl.multiple_of((chunk - first) * WIDE, WIDE)
+            for part in range(4):
+                for q in range(COLS):
+                    at = q * 2 * BLK + part * 8
+                    into[at : at + 8, pl.ds(low, WIDE)] = ref[part, q]
+
+
+def first_kernel(where_ref, own, core, across, both, w_ref, m_ref, t_ref):
+    fill(where_ref[2], (own, core, across, both), m_ref, 0, 2)
     invert_factor(m_ref, w_ref, t_ref)
 
 
-def first_factor(where, own, other):
+def first_factor(where, pieces):
     return pl.pallas_call(
         first_kernel,
         out_shape=jax.ShapeDtypeStruct((PANEL, PANEL), jnp.float32),
-        in_specs=[SMEM, VMEM, VMEM],
+        in_specs=[SMEM] + [VMEM] * 4,
         out_specs=VMEM,
         scratch_shapes=[
             pltpu.VMEM((PANEL, PANEL), jnp.float32),
             pltpu.VMEM((TILE, TILE), jnp.float32),
         ],
-        compiler_params=PARAMS,
+        compiler_params=params(10),
         cost_estimate=pl.CostEstimate(flops=60_000_000_000, bytes_accessed=4 << 20, transcendentals=0),
         name="first_factor",
-    )(where, own, other)
-
-
-def second_kernel(where_ref, inv_ref, up_own, up_other, low_own, low_other, w_ref, x_ref, m_ref, t_ref):
-    core = where_ref[2] % 2
-    fill(m_ref, core, up_own, up_other)
-    x_ref[...] = dot(inv_ref[...], m_ref[...])
-    fill(m_ref, core, low_own, low_other)
-    m_ref[...] = m_ref[...] - t_dot(x_ref[...], x_ref[...])
+    )(where, *pieces)
+
+
+def second_kernel(where_ref, inv_ref, *refs):
+    upper, lower, (w_ref, x_ref, a_ref, m_ref, t_ref) = refs[:4], refs[4:8], refs[8:]
+    fill(where_ref[2], upper, a_ref, 2, 4)
+    x_ref[...] = dot(inv_ref[...], a_ref[...])
+    fill(where_ref[2], lower, a_ref, 2, 4)
+    m_ref[...] = a_ref[...] - t_dot(x_ref[...], x_ref[...])
     invert_factor(m_ref, w_ref, t_ref)
 
 
-def second_factor(where, inv, up_own, up_other, low_own, low_other):
+def second_factor(where, inv, upper, lower):
     shape = jax.ShapeDtypeStruct((PANEL, PANEL), jnp.float32)
     return pl.pallas_call(
         second_kernel,
         out_shape=(shape, shape),
-        in_specs=[SMEM] + [VMEM] * 5,
+        in_specs=[SMEM] + [VMEM] * 9,
         out_specs=(VMEM, VMEM),
         scratch_shapes=[
             pltpu.VMEM((PANEL, PANEL), jnp.float32),
+            pltpu.VMEM((PANEL, PANEL), jnp.float32),
             pltpu.VMEM((TILE, TILE), jnp.float32),
         ],
-        compiler_params=PARAMS,
+        compiler_params=params(16),
         cost_estimate=pl.CostEstimate(flops=60_000_000_000, bytes_accessed=8 << 20, transcendentals=0),
         name="second_factor",
-    )(where, inv, up_own, up_other, low_own, low_other)
+    )(where, inv, *upper, *lower)
 
 
 def finish_kernel(
@@ -249,8 +269,8 @@
     for number, ref in enumerate((row0, row1, row2, row3)):
         chunk = (row // 2 ^ number // 2) * 2 + (row % 2 ^ number % 2)
         low = pl.multiple_of(chunk * WIDE, WIDE)
-        for slot in range(SHARDS):
-            rows_ref[slot * BLK : (slot + 1) * BLK, pl.ds(low, WIDE)] = ref[slot]
+        for group in range(2 * SHARDS):
+            rows_ref[group * 8 : (group + 1) * 8, pl.ds(low, WIDE)] = ref[home(group)]
     for q in range(COLS):
         for half in range(2):
             at = slice(q * 2 * BLK + half * BLK, q * 2 * BLK + (half + 1) * BLK)
@@ -285,7 +305,7 @@
             pltpu.VMEM((PANEL, WIDE), jnp.float32),
             pltpu.VMEM((PANEL, WIDE), jnp.float32),
         ],
-        compiler_params=PARAMS,
+        compiler_params=params(24),
         name="finish",
     )(where, inv0, inv1, x01, cols, *rows, front)
 
@@ -302,6 +322,11 @@
 
 def exchange(x, axis):
     return lax.all_to_all(x, axis, split_axis=0, concat_axis=0, tiled=True)
+
+
+def over_rows(x):
+    across = swap(x, "row", 2)
+    return x, swap(x, "row", 1), across, swap(across, "row", 1)
 
 
 def local(parent_front, child_schur, index_map):
@@ -310,33 +335,22 @@
     where = jnp.stack([shard // (SHARDS // 2), col, row, shard]).astype(jnp.int32)
     parent = parent_front.reshape(SHARDS, BLK, WIDE)
 
-    chunk = exchange(parent.reshape(SUBS, SHARDS // SUBS, BLK, WIDE), "sub")[0]
-    parent_low = to_all(chunk, "sub", SUBS).reshape(SHARDS, BLK, WIDE)
-
     spread = spread_rows(where, index_map, child_schur).reshape(SHARDS, 2, BLK, TILE)
-    low = jnp.broadcast_to(spread[None, :ROWS], (SUBS, ROWS, 2, BLK, TILE))
-    low = exchange(low.reshape(SHARDS, 2, BLK, TILE), ("sub", "row"))
-    rows = place(where, index_map, low, parent_low)
-    pivots = to_all(rows[:4], "col", COLS)
-
-    received = exchange(spread, ("sub", "row"))
-    front = place(where, index_map, received, parent)
-    cols = to_all(front[:4], "col", COLS)
-
-    upper = pivots[:, :2].reshape(SHARDS, BLK, WIDE)
-    lower = pivots[:, 2:].reshape(SHARDS, BLK, WIDE)
-    left = row < 2
-    crossed = swap(jnp.where(left, upper, lower), "row", 2)
-    diag0 = jnp.where(left, upper, crossed)
-    diag1 = jnp.where(left, crossed, lower)
-    inv0 = first_factor(where, diag0, swap(diag0, "row", 1))
-    above = jnp.where(left, swap(upper, "row", 2), upper)
-    inv1, x01 = second_factor(
-        where, inv0, above, swap(above, "row", 1), diag1, swap(diag1, "row", 1)
-    )
-    across = swap(rows, "row", 2)
-    pieces = (rows, swap(rows, "row", 1), across, swap(across, "row", 1))
-    out = finish(where, inv0, inv1, x01, cols, pieces, front)
+    front, dealt = place(where, index_map, exchange(spread, ("sub", "row")), parent)
+
+    chunk = exchange(dealt, "sub")[0]
+    pivots = to_all(chunk[0], ("sub", "col"), SUBS * COLS).reshape(2, 4, COLS, 8, WIDE)
+    upper = over_rows(pivots[0])
+    inv0 = first_factor(where, upper)
+
+    chunk, _ = lax.optimization_barrier((chunk, pivots))
+    rows, _ = lax.optimization_barrier((to_all(chunk, "sub", SUBS), inv0))
+    rows = over_rows(rows)
+    inv1, x01 = second_factor(where, inv0, upper, over_rows(pivots[1]))
+
+    top, _ = lax.optimization_barrier((front[:4], inv0))
+    cols = to_all(top, "col", COLS)
+    out = finish(where, inv0, inv1, x01, cols, rows, front)
     return out.reshape(parent_front.shape)
 
 

time: 243 us -> 225 us (0.926)
  blocking collectives: 19.1 us -> 88.3 us
  waiting for transfers between devices: 62.1 us -> 1.75 us
  starting transfers between devices: 68.2 us -> 41.7 us
  local copies, waits for them, and re-layouts: 13.8 us -> 18.5 us
    all_to_all x0 -> x2, blocking collectives: none -> 48.9 us  [exchange(): return lax.all_to_all(x, axis, split_axis=0, concat_axis=0, tiled=True)]
    all_to_all x3 -> x0, waiting for transfers between devices: 28.3 us -> none  [exchange(): return lax.all_to_all(x, axis, split_axis=0, concat_axis=0, tiled=True)]
    all_to_all x2, waiting for transfers between devices: 25.9 us -> 0.01 us  [to_all(): lax.all_to_all(jnp.broadcast_to(x[None], (count, *x.shape)), axis, split_...]
    all_to_all x3 -> x0, starting transfers between devices: 23.5 us -> none  [exchange(): return lax.all_to_all(x, axis, split_axis=0, concat_axis=0, tiled=True)]
    all_to_all x1, blocking collectives: 19.1 us -> 39.4 us  [to_all(): lax.all_to_all(jnp.broadcast_to(x[None], (count, *x.shape)), axis, split_...]
    ppermute x8 -> x9, waiting for transfers between devices: 7.84 us -> 1.75 us  [swap(): return lax.ppermute(x, axis, [(i, i ^ bit) for i in range(ROWS)])]
    unnamed x26 -> x38, local copies, waits for them, and re-layouts: 9.71 us -> 15.6 us
    ppermute x8 -> x9, starting transfers between devices: 31.6 us -> 30.9 us  [swap(): return lax.ppermute(x, axis, [(i, i ^ bit) for i in range(ROWS)])]
  transfers between devices with their start and end apart: 13 -> 11, of which waited for: 4 -> 1; matrix products, arithmetic and copies ran while one was open for 2% -> 1% of each run, Pallas kernels for 24% -> 23%
where the time goes in v3:
time: 225 us; the launch traced here: 224 us
  blocking collectives  88.3 us (39%)
  Pallas kernels  73.1 us (32%)
  starting transfers between devices  41.7 us (19%)
  local copies, waits for them, and re-layouts  18.5 us (8%)
    all_to_all x2, blocking collectives, exchange(): return lax.all_to_all(x, axis, split_axis=0, concat_axis=0, tiled=True)  48.9 us
    all_to_all x1, blocking collectives, to_all(): lax.all_to_all(jnp.broadcast_to(x[None], (count, *x.shape)), axis, split_...  39.4 us
    ppermute x9, starting transfers between devices, swap(): return lax.ppermute(x, axis, [(i, i ^ bit) for i in range(ROWS)])  30.9 us
    pallas_call x1, Pallas kernels, second_factor(): pl.pallas_call(second_kernel, out_shape=(shape, shape), in_specs=[SMEM] +...  28.3 us
    pallas_call x1, Pallas kernels, first_factor(): pl.pallas_call(first_kernel, out_shape=jax.ShapeDtypeStruct((PANEL, PANEL...  23.1 us
    pallas_call x1, Pallas kernels, finish(): pl.pallas_call(finish_kernel, out_shape=jax.ShapeDtypeStruct((SHARDS, BLK...  15.9 us
    unnamed x38, local copies, waits for them, and re-layouts  15.6 us
    all_to_all x2, starting transfers between devices, to_all(): lax.all_to_all(jnp.broadcast_to(x[None], (count, *x.shape)), axis, split_...  10.8 us
  transfers between devices with their start and end apart: 11, of which 1 were waited for; matrix products, arithmetic and copies ran while one was open for 1% of the time, Pallas kernels for 23%

profile of v3, /device:TPU:1, one launch (start us, length us, event | category | flops | bytes accessed | tf_op | source)
XLA Modules:
  0.0 223.7 jit_solution(11230880820219038241)
XLA Ops:
  1.6 4.4 %spread_rows.1 = f32[64,16,128]{2,1,0:T(8,128)S(1)} custom-call(s32[4]{0:T(128)S(1)} %pad_add_fusion.where_ref, s32[2,256]{1,0:T(2,128)S(1)} %copy-done.10, f32[16,4096]{1,0:T(8,128)S(1)} %copy-done.9), custom_call_target="tpu_custom_call" | custom-call | tf_op jit(solution)/shard_map/spread_rows/pallas_call | solution.py:67
  6.1 29.5 %all_to_all.25.received_ref = f32[32,2,16,128]{3,2,1,0:T(8,128)S(1)} all-to-all(f32[32,2,16,128]{3,2,1,0:T(8,128)S(1)} %bitcast.15), channel_id=1, replica_groups=mesh['sub'=8,'row'=4,'col'=16] {'sub','row'}, dimensions={0} | all-to-all | bytes 1048576 | tf_op jit(solution)/shard_map/all_to_all | solution.py:324
  35.6 1.4 place.1
  37.0 19.4 %all_to_all.26 = f32[8,8,8,256]{3,2,1,0:T(8,128)S(1)} all-to-all(f32[8,8,8,256]{3,2,1,0:T(8,128)S(1)} %get-tuple-element.11), channel_id=1, replica_groups=mesh['sub'=8,'row'=4,'col'=16] {'sub'}, dimensions={0} | all-to-all | bytes 1048576 | tf_op jit(solution)/shard_map/all_to_all | solution.py:324
  56.4 39.4 %all_to_all.27 = f32[128,8,256]{2,1,0:T(8,128)S(1)} all-to-all(f32[128,8,256]{2,1,0:T(8,128)S(1)} %broadcast_in_dim.9), channel_id=1, replica_groups=mesh['sub'=8,'row'=4,'col'=16] {'sub','col'}, dimensions={0} | all-to-all | bytes 2097152 | tf_op jit(solution)/shard_map/all_to_all | solution.py:318
  96.6 1.9 collective-permute-start.1
  98.6 6.8 %collective-permute-start = (f32[4,16,8,256]{3,2,1,0:T(8,128)S(1)}, f32[4,16,8,256]{3,2,1,0:T(8,128)S(1)}, u32[]{:S(2)}, u32[]{:S(2)}) collective-permute-start(f32[4,16,8,256]{3,2,1,0:T(8,128)S(1)} %bitcast.18), channel_id=1, source_target_pairs={{0,16},{16,0},{32,48},{48,32},{1,17},{17,1},{33,49},{49,33},{2,18}... | collective-permute-start | bytes 1572872 | tf_op jit(solution)/shard_map/ppermute | solution.py:314
  105.4 1.7 collective-permute-done.1.across.refs_2_
  107.1 7.6 %collective-permute-start.2 = (f32[4,16,8,256]{3,2,1,0:T(8,128)S(1)}, f32[4,16,8,256]{3,2,1,0:T(8,128)S(1)}, u32[]{:S(2)}, u32[]{:S(2)}) collective-permute-start(f32[4,16,8,256]{3,2,1,0:T(8,128)S(1)} %collective-permute-done.1.across.refs_2_), channel_id=1, source_target_pairs={{0,16},{16,0},{32,48},{48,32},{1,17},{17,1},{33,49},{49,33},{2,18}... | collective-permute-start | bytes 1572872 | tf_op jit(solution)/shard_map/ppermute | solution.py:314
  115.6 4.3 %all-to-all-start.4 = ((f32[8,8,8,256]{3,2,1,0:T(8,128)}), f32[8,8,8,256]{3,2,1,0:T(8,128)S(1)}, u32[]{:S(2)}, u32[]{:S(2)}) async-start(f32[8,8,8,256]{3,2,1,0:T(8,128)} %broadcast_in_dim.22), calls=%async_computation.4 | async-start | bytes 1048576 | tf_op jit(solution)/shard_map/all_to_all | solution.py:318
  119.9 1.9 collective-permute-start.4
  123.5 1.0 copy-done.14
  125.5 23.1 %first_factor.1.inv_ref.inv0_ref = f32[512,512]{1,0:T(8,128)S(1)} custom-call(s32[4]{0:T(128)S(1)} %pad_add_fusion.where_ref, f32[4,16,8,256]{3,2,1,0:T(8,128)S(1)} %bitcast.19, f32[4,16,8,256]{3,2,1,0:T(8,128)S(1)} %copy-done.14, f32[4,16,8,256]{3,2,1,0:T(8,128)S(1)} %collective-permute-done.1.across.refs_2_, f32[4,16,8,256]{3,2,1,0:T(8,128)S(1)} %copy-done.17), custom_call_target="tpu_custom_call" | custom-call | flops 60000002048 | bytes 4194304 | tf_op jit(solution)/shard_map/first_factor/pallas_call | solution.py:222
  148.7 3.4 %collective-permute-start.7 = (f32[8,8,8,256]{3,2,1,0:T(8,128)S(1)}, f32[8,8,8,256]{3,2,1,0:T(8,128)}, u32[]{:S(2)}, u32[]{:S(2)}) collective-permute-start(f32[8,8,8,256]{3,2,1,0:T(8,128)S(1)} %all-to-all-done.4.row0), channel_id=1, source_target_pairs={{0,32},{16,48},{32,0},{48,16},{1,33},{17,49},{33,1},{49,17},{2,34}... | collective-permute-start | bytes 1572872 | tf_op jit(solution)/shard_map/ppermute | solution.py:314
  152.1 2.8 %collective-permute-start.3 = (f32[4,16,8,256]{3,2,1,0:T(8,128)}, f32[4,16,8,256]{3,2,1,0:T(8,128)}, u32[]{:S(2)}, u32[]{:S(2)}) collective-permute-start(f32[4,16,8,256]{3,2,1,0:T(8,128)} %bitcast.8.refs_4_), channel_id=1, source_target_pairs={{0,16},{16,0},{32,48},{48,32},{1,17},{17,1},{33,49},{49,33},{2,18}... | collective-permute-start | bytes 1572872 | tf_op jit(solution)/shard_map/ppermute | solution.py:314
  154.9 1.9 collective-permute-start.5
  156.8 2.4 %collective-permute-start.6 = (f32[8,8,8,256]{3,2,1,0:T(8,128)S(1)}, f32[8,8,8,256]{3,2,1,0:T(8,128)}, u32[]{:S(2)}, u32[]{:S(2)}) collective-permute-start(f32[8,8,8,256]{3,2,1,0:T(8,128)S(1)} %all-to-all-done.4.row0), channel_id=1, source_target_pairs={{0,16},{16,0},{32,48},{48,32},{1,17},{17,1},{33,49},{49,33},{2,18}... | collective-permute-start | bytes 1572872 | tf_op jit(solution)/shard_map/ppermute | solution.py:314
  159.2 1.1 broadcast_in_dim.10
  160.3 6.5 %all-to-all-start.3 = ((f32[16,4,16,256]{3,2,1,0:T(8,128)}), f32[16,4,16,256]{3,2,1,0:T(8,128)S(1)}, u32[]{:S(2)}, u32[]{:S(2)}) async-start(f32[16,4,16,256]{3,2,1,0:T(8,128)} %broadcast_in_dim.10), calls=%async_computation.3 | async-start | bytes 2097152 | tf_op jit(solution)/shard_map/all_to_all | solution.py:318
  166.9 2.2 collective-permute-start.8
  173.3 28.3 %second_factor.1 = (f32[512,512]{1,0:T(8,128)S(1)}, f32[512,512]{1,0:T(8,128)S(1)}) custom-call(s32[4]{0:T(128)S(1)} %pad_add_fusion.where_ref, f32[512,512]{1,0:T(8,128)S(1)} %first_factor.1.inv_ref.inv0_ref, f32[4,16,8,256]{3,2,1,0:T(8,128)S(1)} %bitcast.20, f32[4,16,8,256]{3,2,1,0:T(8,128)S(1)} %copy-done.15, f32[4,16,8,256]{3,2,1,0:T(8,128)S(1)} %copy-done.12, ...), custom_call_target="tpu_custom_call" | custom-call | flops 60000002048 | bytes 8388608 | tf_op jit(solution)/shard_map/second_factor/pallas_call | solution.py:248
  204.4 1.2 copy-done.1
  205.6 1.2 copy-done.3
  207.8 15.9 %finish.1 = f32[32,16,256]{2,1,0:T(8,128)} custom-call(s32[4]{0:T(128)S(1)} %pad_add_fusion.where_ref, f32[512,512]{1,0:T(8,128)S(1)} %first_factor.1.inv_ref.inv0_ref, f32[512,512]{1,0:T(8,128)S(1)} %copy-done.1, f32[512,512]{1,0:T(8,128)S(1)} %copy-done.3, f32[16,4,16,256]{3,2,1,0:T(8,128)S(1)} %all-to-all-done.3.cols_ref, ...), custom_call_target="tpu_custom_call" | custom-call | tf_op jit(solution)/shard_map/finish/pallas_call | solution.py:298
  (52 shorter events, 14.0 us)
Async XLA Ops:
  6.1 29.5 %copy-start.4 = (f32[16,1,32,256]{3,2,1,0:T(8,128)S(1)}, f32[16,1,32,256]{3,2,1,0:T(8,128)}, u32[]{:S(2)}) copy-start(f32[16,1,32,256]{3,2,1,0:T(8,128)} %param.3) | copy-start | bytes 1572868
  96.6 26.0 %copy-start.5 = (f32[64,8,256]{2,1,0:T(8,128)}, f32[64,8,256]{2,1,0:T(8,128)S(1)}, u32[]{:S(2)}) copy-start(f32[64,8,256]{2,1,0:T(8,128)S(1)} %get-tuple-element.18) | copy-start | bytes 1572868
  96.6 10.5 %collective-permute-start.1 = (f32[4,16,8,256]{3,2,1,0:T(8,128)S(1)}, f32[4,16,8,256]{3,2,1,0:T(8,128)S(1)}, u32[]{:S(2)}, u32[]{:S(2)}) collective-permute-start(f32[4,16,8,256]{3,2,1,0:T(8,128)S(1)} %bitcast.17), channel_id=1, source_target_pairs={{0,32},{16,48},{32,0},{48,16},{1,33},{17,49},{33,1},{49,17},{2,34}... | collective-permute-start | bytes 1572872 | tf_op jit(solution)/shard_map/ppermute | solution.py:314
  98.6 23.3 %collective-permute-start = (f32[4,16,8,256]{3,2,1,0:T(8,128)S(1)}, f32[4,16,8,256]{3,2,1,0:T(8,128)S(1)}, u32[]{:S(2)}, u32[]{:S(2)}) collective-permute-start(f32[4,16,8,256]{3,2,1,0:T(8,128)S(1)} %bitcast.18), channel_id=1, source_target_pairs={{0,16},{16,0},{32,48},{48,32},{1,17},{17,1},{33,49},{49,33},{2,18}... | collective-permute-start | bytes 1572872 | tf_op jit(solution)/shard_map/ppermute | solution.py:314
  107.1 15.5 %copy-start.11 = (f32[4,16,8,256]{3,2,1,0:T(8,128)}, f32[4,16,8,256]{3,2,1,0:T(8,128)S(1)}, u32[]{:S(2)}) copy-start(f32[4,16,8,256]{3,2,1,0:T(8,128)S(1)} %collective-permute-done.1.across.refs_2_) | copy-start | bytes 1572868
  107.1 15.5 %collective-permute-start.2 = (f32[4,16,8,256]{3,2,1,0:T(8,128)S(1)}, f32[4,16,8,256]{3,2,1,0:T(8,128)S(1)}, u32[]{:S(2)}, u32[]{:S(2)}) collective-permute-start(f32[4,16,8,256]{3,2,1,0:T(8,128)S(1)} %collective-permute-done.1.across.refs_2_), channel_id=1, source_target_pairs={{0,16},{16,0},{32,48},{48,32},{1,17},{17,1},{33,49},{49,33},{2,18}... | collective-permute-start | bytes 1572872 | tf_op jit(solution)/shard_map/ppermute | solution.py:314
  115.6 33.1 %all-to-all-start.4 = ((f32[8,8,8,256]{3,2,1,0:T(8,128)}), f32[8,8,8,256]{3,2,1,0:T(8,128)S(1)}, u32[]{:S(2)}, u32[]{:S(2)}) async-start(f32[8,8,8,256]{3,2,1,0:T(8,128)} %broadcast_in_dim.22), calls=%async_computation.4 | async-start | bytes 1048576 | tf_op jit(solution)/shard_map/all_to_all | solution.py:318
  119.9 34.9 %collective-permute-start.4 = (f32[4,16,8,256]{3,2,1,0:T(8,128)}, f32[4,16,8,256]{3,2,1,0:T(8,128)}, u32[]{:S(2)}, u32[]{:S(2)}) collective-permute-start(f32[4,16,8,256]{3,2,1,0:T(8,128)} %bitcast.8.refs_4_), channel_id=1, source_target_pairs={{0,32},{16,48},{32,0},{48,16},{1,33},{17,49},{33,1},{49,17},{2,34}... | collective-permute-start | bytes 1572872 | tf_op jit(solution)/shard_map/ppermute | solution.py:314
  123.5 1.0 copy-start.14
  124.5 1.0 copy-start.17
  148.7 18.2 %collective-permute-start.7 = (f32[8,8,8,256]{3,2,1,0:T(8,128)S(1)}, f32[8,8,8,256]{3,2,1,0:T(8,128)}, u32[]{:S(2)}, u32[]{:S(2)}) collective-permute-start(f32[8,8,8,256]{3,2,1,0:T(8,128)S(1)} %all-to-all-done.4.row0), channel_id=1, source_target_pairs={{0,32},{16,48},{32,0},{48,16},{1,33},{17,49},{33,1},{49,17},{2,34}... | collective-permute-start | bytes 1572872 | tf_op jit(solution)/shard_map/ppermute | solution.py:314
  152.1 17.0 %collective-permute-start.3 = (f32[4,16,8,256]{3,2,1,0:T(8,128)}, f32[4,16,8,256]{3,2,1,0:T(8,128)}, u32[]{:S(2)}, u32[]{:S(2)}) collective-permute-start(f32[4,16,8,256]{3,2,1,0:T(8,128)} %bitcast.8.refs_4_), channel_id=1, source_target_pairs={{0,16},{16,0},{32,48},{48,32},{1,17},{17,1},{33,49},{49,33},{2,18}... | collective-permute-start | bytes 1572872 | tf_op jit(solution)/shard_map/ppermute | solution.py:314
  154.9 14.2 %collective-permute-start.5 = (f32[4,16,8,256]{3,2,1,0:T(8,128)}, f32[4,16,8,256]{3,2,1,0:T(8,128)}, u32[]{:S(2)}, u32[]{:S(2)}) collective-permute-start(f32[4,16,8,256]{3,2,1,0:T(8,128)} %collective-permute-done.4.refs_6_), channel_id=1, source_target_pairs={{0,16},{16,0},{32,48},{48,32},{1,17},{17,1},{33,49},{49,33},{2,18}... | collective-permute-start | bytes 1572872 | tf_op jit(solution)/shard_map/ppermute | solution.py:314
  156.8 46.8 %collective-permute-start.6 = (f32[8,8,8,256]{3,2,1,0:T(8,128)S(1)}, f32[8,8,8,256]{3,2,1,0:T(8,128)}, u32[]{:S(2)}, u32[]{:S(2)}) collective-permute-start(f32[8,8,8,256]{3,2,1,0:T(8,128)S(1)} %all-to-all-done.4.row0), channel_id=1, source_target_pairs={{0,16},{16,0},{32,48},{48,32},{1,17},{17,1},{33,49},{49,33},{2,18}... | collective-permute-start | bytes 1572872 | tf_op jit(solution)/shard_map/ppermute | solution.py:314
  160.3 44.0 %all-to-all-start.3 = ((f32[16,4,16,256]{3,2,1,0:T(8,128)}), f32[16,4,16,256]{3,2,1,0:T(8,128)S(1)}, u32[]{:S(2)}, u32[]{:S(2)}) async-start(f32[16,4,16,256]{3,2,1,0:T(8,128)} %broadcast_in_dim.10), calls=%async_computation.3 | async-start | bytes 2097152 | tf_op jit(solution)/shard_map/all_to_all | solution.py:318
  166.9 36.7 %collective-permute-start.8 = (f32[8,8,8,256]{3,2,1,0:T(8,128)}, f32[8,8,8,256]{3,2,1,0:T(8,128)S(1)}, u32[]{:S(2)}, u32[]{:S(2)}) collective-permute-start(f32[8,8,8,256]{3,2,1,0:T(8,128)} %collective-permute-done.7.row2), channel_id=1, source_target_pairs={{0,16},{16,0},{32,48},{48,32},{1,17},{17,1},{33,49},{49,33},{2,18}... | collective-permute-start | bytes 1572872 | tf_op jit(solution)/shard_map/ppermute | solution.py:314
  169.1 1.0 copy-start.6
  170.1 1.0 copy-start.12
  171.2 1.0 copy-start.15
  172.2 1.0 copy-start.18
  202.5 1.0 copy-start.2
  204.4 1.2 copy-start.1
  205.6 1.2 copy-start.3
  206.8 1.0 copy-start.8
  (6 other events, 5.0 us)

commit v4 on v3

--- a/solution.py
+++ b/solution.py
@@ -16,6 +16,7 @@
 SHARDS = SUBS * ROWS
 WIDE = 256
 PANEL = 512
+TOP = 4
 HIGHEST = lax.Precision.HIGHEST
 
 VMEM = pl.BlockSpec(memory_space=pltpu.VMEM)
@@ -32,6 +33,20 @@
     )
 
 
+def split(a):
+    high = a.astype(jnp.bfloat16)
+    return high, (a - high.astype(jnp.float32)).astype(jnp.bfloat16)
+
+
+def contract_split(a, b, dims):
+    def product(x, y):
+        return lax.dot_general(
+            x, y, ((dims[:1], dims[1:]), ((), ())), preferred_element_type=jnp.float32
+        )
+
+    return product(a[0], b[1]) + product(a[1], b[0]) + product(a[0], b[0])
+
+
 def dot(a, b):
     return contract(a, b, (1, 0))
 
@@ -44,7 +59,7 @@
     return contract(a, b, (0, 0))
 
 
-def spread_kernel(where_ref, map_ref, child_ref, out_ref):
+def spread_kernel(where_ref, map_ref, child_ref, out_ref, low_ref):
     child = where_ref[0]
     out_ref[...] = jnp.zeros_like(out_ref)
     lane_block = lax.broadcasted_iota(jnp.int32, (BLK, TILE), 1) // BLK
@@ -61,55 +76,88 @@
         return carry
 
     lax.fori_loop(0, child_ref.shape[1] // TILE, body, 0)
+    for sub in range(SUBS):
+        low_ref[sub] = out_ref[: 2 * ROWS]
 
 
 def spread_rows(where, index_map, child):
     return pl.pallas_call(
         spread_kernel,
-        out_shape=jax.ShapeDtypeStruct((2 * SHARDS, BLK, TILE), jnp.float32),
+        out_shape=(
+            jax.ShapeDtypeStruct((2 * SHARDS, BLK, TILE), jnp.float32),
+            jax.ShapeDtypeStruct((SUBS, 2 * ROWS, BLK, TILE), jnp.float32),
+        ),
         in_specs=[SMEM, SMEM, VMEM],
-        out_specs=VMEM,
+        out_specs=(VMEM, VMEM),
         compiler_params=params(4),
         name="spread_rows",
     )(where, index_map, child)
 
 
-def home(group):
-    far = group - SUBS
-    return (group, 0) if group < SUBS else (far // (SUBS - 1), far % (SUBS - 1) + 1)
-
-
-def place_kernel(where_ref, map_ref, received_ref, parent_ref, out_ref, dealt_ref):
+def each_source(where_ref, map_ref, use):
     col = where_ref[1]
 
     def body(source, carry):
         child = source // (SHARDS // 2)
         block = map_ref[child, source % (SHARDS // 2) * COLS + col]
-        slot = block // (2 * COLS) * 2 + block % 2
-        for half in range(2):
-            lanes = slice(half * TILE, (half + 1) * TILE)
-            out_ref[slot, :, lanes] = parent_ref[slot, :, lanes] + received_ref[source, half]
+        use(source, block // (2 * COLS) * 2 + block % 2)
         return carry
 
     lax.fori_loop(0, SHARDS, body, 0)
-    for group in range(2 * SHARDS):
-        owner, number = home(group)
-        low = group % 2 * 8
-        dealt_ref[owner, number] = out_ref[group // 2, low : low + 8, :]
-
-
-def place(where, index_map, received, parent):
+
+
+def add_block(out_ref, slot, parent, received_ref, source):
+    for half in range(2):
+        lanes = slice(half * TILE, (half + 1) * TILE)
+        out_ref[slot, :, lanes] = parent[:, lanes] + received_ref[source, half]
+
+
+def place_kernel(where_ref, map_ref, received_ref, parent_ref, out_ref, top_ref):
+    def use(source, slot):
+        add_block(out_ref, slot, parent_ref[slot], received_ref, source)
+
+    each_source(where_ref, map_ref, use)
+    for q in range(COLS):
+        top_ref[q] = out_ref[:TOP]
+
+
+def place_top_kernel(where_ref, map_ref, received_ref, parent_ref, top_ref, out_ref):
+    def use(source, slot):
+        @pl.when(slot < TOP)
+        def _():
+            add_block(out_ref, slot, parent_ref[slot], received_ref, source)
+
+    each_source(where_ref, map_ref, use)
+    for q in range(COLS):
+        top_ref[q] = out_ref[...]
+
+
+def place_rest_kernel(where_ref, map_ref, received_ref, parent_ref, top_ref, out_ref):
+    def use(source, slot):
+        @pl.when(slot >= TOP)
+        def _():
+            add_block(out_ref, slot, parent_ref[slot - TOP], received_ref, source)
+
+    each_source(where_ref, map_ref, use)
+    out_ref[:TOP] = top_ref[0]
+
+
+FRONT = jax.ShapeDtypeStruct((SHARDS, BLK, WIDE), jnp.float32)
+TOPS = jax.ShapeDtypeStruct((COLS, TOP, BLK, WIDE), jnp.float32)
+
+
+def call(kernel, out_shape, operands, mib, scratch=(), flops=None):
+    cost = flops and pl.CostEstimate(flops=flops, bytes_accessed=4 << 20, transcendentals=0)
     return pl.pallas_call(
-        place_kernel,
-        out_shape=(
-            jax.ShapeDtypeStruct((SHARDS, BLK, WIDE), jnp.float32),
-            jax.ShapeDtypeStruct((SUBS, 8, 8, WIDE), jnp.float32),
-        ),
-        in_specs=[SMEM, SMEM, VMEM, VMEM],
-        out_specs=(VMEM, VMEM),
-        compiler_params=params(6),
-        name="place",
-    )(where, index_map, received, parent)
+        kernel,
+        out_shape=out_shape,
+        in_specs=[SMEM, SMEM] + [VMEM] * (len(operands) - 2),
+        out_specs=jax.tree.map(lambda _: VMEM, out_shape),
+        scratch_shapes=list(scratch),
+        compiler_params=params(mib),
+        cost_estimate=cost,
+        name=kernel.__name__.removesuffix("_kernel"),
+    )(*operands)
 
 
 def tree_sum(terms):
@@ -207,10 +255,10 @@
         @pl.when((chunk >= first) & (chunk < last))
         def _():
             low = pl.multiple_of((chunk - first) * WIDE, WIDE)
-            for part in range(4):
-                for q in range(COLS):
-                    at = q * 2 * BLK + part * 8
-                    into[at : at + 8, pl.ds(low, WIDE)] = ref[part, q]
+            for q in range(COLS):
+                for half in range(2):
+                    at = (2 * q + half) * BLK
+                    into[at : at + BLK, pl.ds(low, WIDE)] = ref[q, half]
 
 
 def first_kernel(where_ref, own, core, across, both, w_ref, m_ref, t_ref):
@@ -269,20 +317,24 @@
     for number, ref in enumerate((row0, row1, row2, row3)):
         chunk = (row // 2 ^ number // 2) * 2 + (row % 2 ^ number % 2)
         low = pl.multiple_of(chunk * WIDE, WIDE)
-        for group in range(2 * SHARDS):
-            rows_ref[group * 8 : (group + 1) * 8, pl.ds(low, WIDE)] = ref[home(group)]
+        for slot in range(SHARDS):
+            rows_ref[slot * BLK : (slot + 1) * BLK, pl.ds(low, WIDE)] = ref[slot]
     for q in range(COLS):
         for half in range(2):
             at = slice(q * 2 * BLK + half * BLK, q * 2 * BLK + (half + 1) * BLK)
             cols0_ref[at, :] = cols_ref[q, half]
             cols1_ref[at, :] = cols_ref[q, 2 + half]
-    r0 = dot_t(rows_ref[:, :PANEL], inv0_ref[...])
-    c0 = dot(inv0_ref[...], cols0_ref[...])
+    inv0, inv1, x01 = split(inv0_ref[...]), split(inv1_ref[...]), split(x01_ref[...])
+    r0 = split(contract_split(split(rows_ref[:, :PANEL]), inv0, (1, 1)))
+    c0 = contract_split(inv0, split(cols0_ref[...]), (1, 0))
     cols0_ref[...] = c0
-    r1 = dot_t(rows_ref[:, PANEL:] - dot(r0, x01_ref[...]), inv1_ref[...])
-    c1 = dot(inv1_ref[...], cols1_ref[...] - t_dot(x01_ref[...], c0))
+    c0 = split(c0)
+    r1 = split(rows_ref[:, PANEL:] - contract_split(r0, x01, (1, 0)))
+    r1 = split(contract_split(r1, inv1, (1, 1)))
+    c1 = split(cols1_ref[...] - contract_split(x01, c0, (0, 0)))
+    c1 = contract_split(inv1, c1, (1, 0))
     cols1_ref[...] = c1
-    update = dot(r0, c0) + dot(r1, c1)
+    update = contract_split(r0, c0, (1, 0)) + contract_split(r1, split(c1), (1, 0))
     live = (shard >= ROWS).astype(jnp.float32)
     for slot in range(4, SHARDS):
         rows = slice(slot * BLK, (slot + 1) * BLK)
@@ -329,27 +381,42 @@
     return x, swap(x, "row", 1), across, swap(across, "row", 1)
 
 
+def from_first(x, sub):
+    for step in (4, 2, 1):
+        pairs = [(i, i + step) for i in range(0, SUBS, 2 * step)]
+        got = lax.ppermute(x, "sub", pairs)
+        x = jnp.where(sub % (2 * step) == step, got, x)
+    return x
+
+
 def local(parent_front, child_schur, index_map):
     sub, row, col = (lax.axis_index(name) for name in ("sub", "row", "col"))
     shard = sub * ROWS + row
     where = jnp.stack([shard // (SHARDS // 2), col, row, shard]).astype(jnp.int32)
     parent = parent_front.reshape(SHARDS, BLK, WIDE)
-
-    spread = spread_rows(where, index_map, child_schur).reshape(SHARDS, 2, BLK, TILE)
-    front, dealt = place(where, index_map, exchange(spread, ("sub", "row")), parent)
-
-    chunk = exchange(dealt, "sub")[0]
-    pivots = to_all(chunk[0], ("sub", "col"), SUBS * COLS).reshape(2, 4, COLS, 8, WIDE)
-    upper = over_rows(pivots[0])
+    parent_top = from_first(parent[:TOP], sub)
+    parent_rest = from_first(parent[TOP:], sub)
+
+    spread, low = spread_rows(where, index_map, child_schur)
+    low = exchange(low.reshape(SHARDS, 2, BLK, TILE), ("sub", "row"))
+    tops, _ = call(
+        place_top_kernel,
+        (TOPS, jax.ShapeDtypeStruct((TOP, BLK, WIDE), jnp.float32)),
+        (where, index_map, low, parent_top),
+        6,
+    )
+    pivots = exchange(tops, "col")
+    rows = call(place_rest_kernel, FRONT, (where, index_map, low, parent_rest, tops), 6)
+    rows = over_rows(rows)
+    upper = over_rows(pivots[:, :2])
+    lower = over_rows(pivots[:, 2:])
     inv0 = first_factor(where, upper)
 
-    chunk, _ = lax.optimization_barrier((chunk, pivots))
-    rows, _ = lax.optimization_barrier((to_all(chunk, "sub", SUBS), inv0))
-    rows = over_rows(rows)
-    inv1, x01 = second_factor(where, inv0, upper, over_rows(pivots[1]))
-
-    top, _ = lax.optimization_barrier((front[:4], inv0))
-    cols = to_all(top, "col", COLS)
+    spread, _ = lax.optimization_barrier((spread.reshape(SHARDS, 2, BLK, TILE), pivots))
+    received, _ = lax.optimization_barrier((exchange(spread, ("sub", "row")), inv0))
+    front, tops = call(place_kernel, (FRONT, TOPS), (where, index_map, received, parent), 6)
+    inv1, x01 = second_factor(where, inv0, upper, lower)
+    cols = exchange(tops, "col")
     out = finish(where, inv0, inv1, x01, cols, rows, front)
     return out.reshape(parent_front.shape)
 

time: 225 us -> 210 us (0.933)
  blocking collectives: 88.3 us -> 0 us
  starting transfers between devices: 41.7 us -> 96.5 us
  waiting for transfers between devices: 1.75 us -> 25.2 us
  local copies, waits for them, and re-layouts: 18.5 us -> 13.3 us
    all_to_all x3 -> x0, blocking collectives: 88.3 us -> none  [the longest x2 48.9 us: exchange(): return lax.all_to_all(x, axis, split_axis=0, concat_axis=0, tiled=True)]
    all_to_all x2 -> x4, starting transfers between devices: 10.8 us -> 42.7 us  [exchange(): return lax.all_to_all(x, axis, split_axis=0, concat_axis=0, tiled=True)]
    ppermute x0 -> x6, waiting for transfers between devices: none -> 25.2 us  [from_first(): got = lax.ppermute(x, 'sub', pairs)]
    ppermute x0 -> x6, starting transfers between devices: none -> 21.4 us  [from_first(): got = lax.ppermute(x, 'sub', pairs)]
    pallas_call x1, Pallas kernels: 15.9 us -> 8.52 us  [finish(): pl.pallas_call(finish_kernel, out_shape=jax.ShapeDtypeStruct((SHARDS, BLK...]
    pallas_call x2 -> x4, Pallas kernels: 5.78 us -> 12.6 us  [the longest x3 7.27 us: call(): pl.pallas_call(kernel, out_shape=out_shape, in_specs=[SMEM, SMEM] + [VMEM...]
    unnamed x38 -> x30, local copies, waits for them, and re-layouts: 15.6 us -> 12 us
  transfers between devices with their start and end apart: 11 -> 19, of which waited for: 1 -> 6; matrix products, arithmetic and copies ran while one was open for 1% -> 1% of each run, Pallas kernels for 23% -> 27%
where the time goes in v4:
time: 210 us; the launch traced here: 209 us
  starting transfers between devices  96.5 us (46%)
  Pallas kernels  73.2 us (35%)
  waiting for transfers between devices  25.2 us (12%)
  local copies, waits for them, and re-layouts  13.3 us (6%)
    all_to_all x4, starting transfers between devices, exchange(): return lax.all_to_all(x, axis, split_axis=0, concat_axis=0, tiled=True)  42.7 us
    ppermute x9, starting transfers between devices, swap(): return lax.ppermute(x, axis, [(i, i ^ bit) for i in range(ROWS)])  32.4 us
    pallas_call x1, Pallas kernels, second_factor(): pl.pallas_call(second_kernel, out_shape=(shape, shape), in_specs=[SMEM] +...  28.3 us
    ppermute x6, waiting for transfers between devices, from_first(): got = lax.ppermute(x, 'sub', pairs)  25.2 us
    pallas_call x1, Pallas kernels, first_factor(): pl.pallas_call(first_kernel, out_shape=jax.ShapeDtypeStruct((PANEL, PANEL...  23.8 us
    ppermute x6, starting transfers between devices, from_first(): got = lax.ppermute(x, 'sub', pairs)  21.4 us
    unnamed x30, local copies, waits for them, and re-layouts  12 us
    pallas_call x1, Pallas kernels, finish(): pl.pallas_call(finish_kernel, out_shape=jax.ShapeDtypeStruct((SHARDS, BLK...  8.52 us
  transfers between devices with their start and end apart: 19, of which 6 were waited for; matrix products, arithmetic and copies ran while one was open for 1% of the time, Pallas kernels for 27%

profile of v4, /device:TPU:1, one launch (start us, length us, event | category | flops | bytes accessed | tf_op | source)
XLA Modules:
  0.0 208.9 jit_solution(14501403608695452169)
XLA Ops:
  1.6 5.4 %spread_rows.1 = (f32[64,16,128]{2,1,0:T(8,128)}, f32[8,8,16,128]{3,2,1,0:T(8,128)}) custom-call(s32[4]{0:T(128)S(1)} %pad_add_fusion.where_ref, s32[2,256]{1,0:T(2,128)S(1)} %copy-done.11, f32[16,4096]{1,0:T(8,128)S(1)} %copy-done.10), custom_call_target="tpu_custom_call" | custom-call | tf_op jit(solution)/shard_map/spread_rows/pallas_call | solution.py:84
  7.0 13.0 %all-to-all-start = ((f32[32,2,16,128]{3,2,1,0:T(8,128)}), f32[32,2,16,128]{3,2,1,0:T(8,128)S(1)}, u32[]{:S(2)}, u32[]{:S(2)}) async-start(f32[32,2,16,128]{3,2,1,0:T(8,128)} %bitcast.4), calls=%async_computation | async-start | bytes 1048576 | tf_op jit(solution)/shard_map/all_to_all | solution.py:376
  20.1 7.2 %collective-permute-start = (f32[4,16,256]{2,1,0:T(8,128)S(1)}, f32[4,16,256]{2,1,0:T(8,128)S(1)}, u32[]{:S(2)}, u32[]{:S(2)}) collective-permute-start(f32[4,16,256]{2,1,0:T(8,128)S(1)} %bitcast.15), channel_id=1, source_target_pairs={{0,256},{1,257},{2,258},{3,259},{4,260},{5,261},{6,262},{7,263},{8... | collective-permute-start | bytes 196616 | tf_op jit(solution)/shard_map/ppermute | solution.py:387
  27.3 4.5 %collective-permute-done = f32[4,16,256]{2,1,0:T(8,128)S(1)} collective-permute-done((f32[4,16,256]{2,1,0:T(8,128)S(1)}, f32[4,16,256]{2,1,0:T(8,128)S(1)}, u32[]{:S(2)}, u32[]{:S(2)}) %collective-permute-start) | collective-permute-done | bytes 65568 | tf_op jit(solution)/shard_map/ppermute | solution.py:387
  37.1 2.6 %place_top.1 = (f32[16,4,16,256]{3,2,1,0:T(8,128)}, f32[4,16,256]{2,1,0:T(8,128)}) custom-call(s32[4]{0:T(128)S(1)} %pad_add_fusion.where_ref, s32[2,256]{1,0:T(2,128)S(1)} %copy-done.11, f32[32,2,16,128]{3,2,1,0:T(8,128)S(1)} %all-to-all-done.received_ref, f32[4,16,256]{2,1,0:T(8,128)S(1)} %broadcast_select_fusion.5.parent_ref), custom_call_target="tpu_custom_call" | custom-call | tf_op jit(solution)/shard_map/place_top/pallas_call | solution.py:151
  39.7 9.1 %all-to-all-start.1 = ((f32[16,4,16,256]{3,2,1,0:T(8,128)}), f32[16,4,16,256]{3,2,1,0:T(8,128)}, u32[]{:S(2)}, u32[]{:S(2)}) async-start(f32[16,4,16,256]{3,2,1,0:T(8,128)} %get-tuple-element.15.top_ref), calls=%async_computation.1 | async-start | bytes 2097152 | tf_op jit(solution)/shard_map/all_to_all | solution.py:376
  48.9 8.2 %collective-permute-start.9 = (f32[28,16,256]{2,1,0:T(8,128)S(1)}, f32[28,16,256]{2,1,0:T(8,128)S(1)}, u32[]{:S(2)}, u32[]{:S(2)}) collective-permute-start(f32[28,16,256]{2,1,0:T(8,128)S(1)} %bitcast.13), channel_id=1, source_target_pairs={{0,256},{1,257},{2,258},{3,259},{4,260},{5,261},{6,262},{7,263},{8... | collective-permute-start | bytes 1376264 | tf_op jit(solution)/shard_map/ppermute | solution.py:387
  57.1 7.3 %collective-permute-done.9 = f32[28,16,256]{2,1,0:T(8,128)S(1)} collective-permute-done((f32[28,16,256]{2,1,0:T(8,128)S(1)}, f32[28,16,256]{2,1,0:T(8,128)S(1)}, u32[]{:S(2)}, u32[]{:S(2)}) %collective-permute-start.9) | collective-permute-done | bytes 458784 | tf_op jit(solution)/shard_map/ppermute | solution.py:387
  65.8 7.9 %collective-permute-done.10 = f32[28,16,256]{2,1,0:T(8,128)S(1)} collective-permute-done((f32[28,16,256]{2,1,0:T(8,128)S(1)}, f32[28,16,256]{2,1,0:T(8,128)S(1)}, u32[]{:S(2)}, u32[]{:S(2)}) %collective-permute-start.10) | collective-permute-done | bytes 458784 | tf_op jit(solution)/shard_map/ppermute | solution.py:387
  77.1 2.9 %collective-permute-start.4 = (f32[16,2,16,256]{3,2,1,0:T(8,128)S(1)}, f32[16,2,16,256]{3,2,1,0:T(8,128)S(1)}, u32[]{:S(2)}, u32[]{:S(2)}) collective-permute-start(f32[16,2,16,256]{3,2,1,0:T(8,128)S(1)} %get-tuple-element.24.own.refs_0_), channel_id=1, source_target_pairs={{0,32},{16,48},{32,0},{48,16},{1,33},{17,49},{33,1},{49,17},{2,34}... | collective-permute-start | bytes 1572872 | tf_op jit(solution)/shard_map/ppermute | solution.py:366
  80.0 2.9 %collective-permute-done.11 = f32[28,16,256]{2,1,0:T(8,128)} collective-permute-done((f32[28,16,256]{2,1,0:T(8,128)S(1)}, f32[28,16,256]{2,1,0:T(8,128)}, u32[]{:S(2)}, u32[]{:S(2)}) %collective-permute-start.11) | collective-permute-done | bytes 458784 | tf_op jit(solution)/shard_map/ppermute | solution.py:387
  83.0 2.2 %place_rest.1.row0 = f32[32,16,256]{2,1,0:T(8,128)S(1)} custom-call(s32[4]{0:T(128)S(1)} %pad_add_fusion.where_ref, s32[2,256]{1,0:T(2,128)S(1)} %copy-done.11, f32[32,2,16,128]{3,2,1,0:T(8,128)S(1)} %all-to-all-done.received_ref, f32[28,16,256]{2,1,0:T(8,128)S(1)} %broadcast_select_fusion.2.parent_ref, f32[16,4,16,256]{3,2,1,0:T(8,128)} %get-tuple-element.15.top_ref), custom_call_target="tpu_custom_call" | custom-call | tf_op jit(solution)/shard_map/place_rest/pallas_call | solution.py:151
  85.2 2.9 %collective-permute-start.13 = (f32[32,16,256]{2,1,0:T(8,128)S(1)}, f32[32,16,256]{2,1,0:T(8,128)}, u32[]{:S(2)}, u32[]{:S(2)}) collective-permute-start(f32[32,16,256]{2,1,0:T(8,128)S(1)} %place_rest.1.row0), channel_id=1, source_target_pairs={{0,32},{16,48},{32,0},{48,16},{1,33},{17,49},{33,1},{49,17},{2,34}... | collective-permute-start | bytes 1572872 | tf_op jit(solution)/shard_map/ppermute | solution.py:366
  88.1 2.4 %collective-permute-start.7 = (f32[16,2,16,256]{3,2,1,0:T(8,128)S(1)}, f32[16,2,16,256]{3,2,1,0:T(8,128)}, u32[]{:S(2)}, u32[]{:S(2)}) collective-permute-start(f32[16,2,16,256]{3,2,1,0:T(8,128)S(1)} %get-tuple-element.23.refs_4_), channel_id=1, source_target_pairs={{0,32},{16,48},{32,0},{48,16},{1,33},{17,49},{33,1},{49,17},{2,34}... | collective-permute-start | bytes 1572872 | tf_op jit(solution)/shard_map/ppermute | solution.py:366
  90.5 7.0 %collective-permute-start.3 = (f32[16,2,16,256]{3,2,1,0:T(8,128)S(1)}, f32[16,2,16,256]{3,2,1,0:T(8,128)}, u32[]{:S(2)}, u32[]{:S(2)}) collective-permute-start(f32[16,2,16,256]{3,2,1,0:T(8,128)S(1)} %get-tuple-element.24.own.refs_0_), channel_id=1, source_target_pairs={{0,16},{16,0},{32,48},{48,32},{1,17},{17,1},{33,49},{49,33},{2,18}... | collective-permute-start | bytes 1572872 | tf_op jit(solution)/shard_map/ppermute | solution.py:366
  99.5 2.4 %collective-permute-start.12 = (f32[32,16,256]{2,1,0:T(8,128)S(1)}, f32[32,16,256]{2,1,0:T(8,128)}, u32[]{:S(2)}, u32[]{:S(2)}) collective-permute-start(f32[32,16,256]{2,1,0:T(8,128)S(1)} %place_rest.1.row0), channel_id=1, source_target_pairs={{0,16},{16,0},{32,48},{48,32},{1,17},{17,1},{33,49},{49,33},{2,18}... | collective-permute-start | bytes 1572872 | tf_op jit(solution)/shard_map/ppermute | solution.py:366
  101.9 8.6 %collective-permute-start.14 = (f32[32,16,256]{2,1,0:T(8,128)}, f32[32,16,256]{2,1,0:T(8,128)}, u32[]{:S(2)}, u32[]{:S(2)}) collective-permute-start(f32[32,16,256]{2,1,0:T(8,128)} %collective-permute-done.13.row2), channel_id=1, source_target_pairs={{0,16},{16,0},{32,48},{48,32},{1,17},{17,1},{33,49},{49,33},{2,18}... | collective-permute-start | bytes 1572872 | tf_op jit(solution)/shard_map/ppermute | solution.py:366
  110.5 10.9 %all-to-all-start.2 = ((f32[32,2,16,128]{3,2,1,0:T(8,128)}), f32[32,2,16,128]{3,2,1,0:T(8,128)S(1)}, u32[]{:S(2)}, u32[]{:S(2)}) async-start(f32[32,2,16,128]{3,2,1,0:T(8,128)} %bitcast.6), calls=%async_computation.2 | async-start | bytes 1048576 | tf_op jit(solution)/shard_map/all_to_all | solution.py:376
  123.6 2.2 %collective-permute-start.8 = (f32[16,2,16,256]{3,2,1,0:T(8,128)}, f32[16,2,16,256]{3,2,1,0:T(8,128)}, u32[]{:S(2)}, u32[]{:S(2)}) collective-permute-start(f32[16,2,16,256]{3,2,1,0:T(8,128)} %collective-permute-done.7.refs_6_), channel_id=1, source_target_pairs={{0,16},{16,0},{32,48},{48,32},{1,17},{17,1},{33,49},{49,33},{2,18}... | collective-permute-start | bytes 1572872 | tf_op jit(solution)/shard_map/ppermute | solution.py:366
  127.9 23.8 %first_factor.1.inv_ref.inv0_ref = f32[512,512]{1,0:T(8,128)S(1)} custom-call(s32[4]{0:T(128)S(1)} %pad_add_fusion.where_ref, f32[16,2,16,256]{3,2,1,0:T(8,128)S(1)} %copy-done.6, f32[16,2,16,256]{3,2,1,0:T(8,128)} %collective-permute-done.3.core.refs_1_, f32[16,2,16,256]{3,2,1,0:T(8,128)S(1)} %copy-done.13, ...), custom_call_target="tpu_custom_call" | custom-call | flops 60000002048 | bytes 4194304 | tf_op jit(solution)/shard_map/first_factor/pallas_call | solution.py:270
  151.7 2.4 %place.1 = (f32[32,16,256]{2,1,0:T(8,128)S(1)}, f32[16,4,16,256]{3,2,1,0:T(8,128)}) custom-call(s32[4]{0:T(128)S(1)} %pad_add_fusion.where_ref, s32[2,256]{1,0:T(2,128)S(1)} %copy-done.11, f32[32,2,16,128]{3,2,1,0:T(8,128)S(1)} %all-to-all-done.2.received_ref, f32[32,16,256]{2,1,0:T(8,128)S(1)} %bitcast.12), custom_call_target="tpu_custom_call" | custom-call | tf_op jit(solution)/shard_map/place/pallas_call | solution.py:151
  154.9 9.6 %all-to-all-start.3 = ((f32[16,4,16,256]{3,2,1,0:T(8,128)}), f32[16,4,16,256]{3,2,1,0:T(8,128)S(1)}, u32[]{:S(2)}, u32[]{:S(2)}) async-start(f32[16,4,16,256]{3,2,1,0:T(8,128)} %get-tuple-element.21), calls=%async_computation.3 | async-start | bytes 2097152 | tf_op jit(solution)/shard_map/all_to_all | solution.py:376
  166.6 28.3 %second_factor.1 = (f32[512,512]{1,0:T(8,128)S(1)}, f32[512,512]{1,0:T(8,128)S(1)}) custom-call(s32[4]{0:T(128)S(1)} %pad_add_fusion.where_ref, f32[512,512]{1,0:T(8,128)S(1)} %first_factor.1.inv_ref.inv0_ref, f32[16,2,16,256]{3,2,1,0:T(8,128)S(1)} %copy-done.7, f32[16,2,16,256]{3,2,1,0:T(8,128)} %collective-permute-done.3.core.refs_1_, ...), custom_call_target="tpu_custom_call" | custom-call | flops 60000002048 | bytes 8388608 | tf_op jit(solution)/shard_map/second_factor/pallas_call | solution.py:296
  200.4 8.5 %finish.1 = f32[32,16,256]{2,1,0:T(8,128)} custom-call(s32[4]{0:T(128)S(1)} %pad_add_fusion.where_ref, f32[512,512]{1,0:T(8,128)S(1)} %first_factor.1.inv_ref.inv0_ref, f32[512,512]{1,0:T(8,128)S(1)} %copy-done.2, f32[512,512]{1,0:T(8,128)S(1)} %copy-done.4, f32[16,4,16,256]{3,2,1,0:T(8,128)S(1)} %all-to-all-done.3.cols_ref, ...), custom_call_target="tpu_custom_call" | custom-call | tf_op jit(solution)/shard_map/finish/pallas_call | solution.py:350
  (61 shorter events, 26.3 us)
Async XLA Ops:
  7.0 13.0 %copy-start = (f32[16,1,32,256]{3,2,1,0:T(8,128)S(1)}, f32[16,1,32,256]{3,2,1,0:T(8,128)}, u32[]{:S(2)}) copy-start(f32[16,1,32,256]{3,2,1,0:T(8,128)} %param.3) | copy-start | bytes 1572868
  7.0 30.1 %all-to-all-start = ((f32[32,2,16,128]{3,2,1,0:T(8,128)}), f32[32,2,16,128]{3,2,1,0:T(8,128)S(1)}, u32[]{:S(2)}, u32[]{:S(2)}) async-start(f32[32,2,16,128]{3,2,1,0:T(8,128)} %bitcast.4), calls=%async_computation | async-start | bytes 1048576 | tf_op jit(solution)/shard_map/all_to_all | solution.py:376
  20.1 11.7 %collective-permute-start = (f32[4,16,256]{2,1,0:T(8,128)S(1)}, f32[4,16,256]{2,1,0:T(8,128)S(1)}, u32[]{:S(2)}, u32[]{:S(2)}) collective-permute-start(f32[4,16,256]{2,1,0:T(8,128)S(1)} %bitcast.15), channel_id=1, source_target_pairs={{0,256},{1,257},{2,258},{3,259},{4,260},{5,261},{6,262},{7,263},{8... | collective-permute-start | bytes 196616 | tf_op jit(solution)/shard_map/ppermute | solution.py:387
  31.8 2.6 %collective-permute-start.1 = (f32[4,16,256]{2,1,0:T(8,128)S(1)}, f32[4,16,256]{2,1,0:T(8,128)S(1)}, u32[]{:S(2)}, u32[]{:S(2)}) collective-permute-start(f32[4,16,256]{2,1,0:T(8,128)S(1)} %broadcast_select_fusion.3), channel_id=1, source_target_pairs={{0,128},{256,384},{1,129},{257,385},{2,130},{258,386},{3,131},{259... | collective-permute-start | bytes 196616 | tf_op jit(solution)/shard_map/ppermute | solution.py:387
  34.4 2.6 %collective-permute-start.2 = (f32[4,16,256]{2,1,0:T(8,128)S(1)}, f32[4,16,256]{2,1,0:T(8,128)S(1)}, u32[]{:S(2)}, u32[]{:S(2)}) collective-permute-start(f32[4,16,256]{2,1,0:T(8,128)S(1)} %broadcast_select_fusion.4), channel_id=1, source_target_pairs={{0,64},{128,192},{256,320},{384,448},{1,65},{129,193},{257,321},{3... | collective-permute-start | bytes 196616 | tf_op jit(solution)/shard_map/ppermute | solution.py:387
  39.7 36.1 %all-to-all-start.1 = ((f32[16,4,16,256]{3,2,1,0:T(8,128)}), f32[16,4,16,256]{3,2,1,0:T(8,128)}, u32[]{:S(2)}, u32[]{:S(2)}) async-start(f32[16,4,16,256]{3,2,1,0:T(8,128)} %get-tuple-element.15.top_ref), calls=%async_computation.1 | async-start | bytes 2097152 | tf_op jit(solution)/shard_map/all_to_all | solution.py:376
  48.9 15.5 %collective-permute-start.9 = (f32[28,16,256]{2,1,0:T(8,128)S(1)}, f32[28,16,256]{2,1,0:T(8,128)S(1)}, u32[]{:S(2)}, u32[]{:S(2)}) collective-permute-start(f32[28,16,256]{2,1,0:T(8,128)S(1)} %bitcast.13), channel_id=1, source_target_pairs={{0,256},{1,257},{2,258},{3,259},{4,260},{5,261},{6,262},{7,263},{8... | collective-permute-start | bytes 1376264 | tf_op jit(solution)/shard_map/ppermute | solution.py:387
  64.4 9.2 %collective-permute-start.10 = (f32[28,16,256]{2,1,0:T(8,128)S(1)}, f32[28,16,256]{2,1,0:T(8,128)S(1)}, u32[]{:S(2)}, u32[]{:S(2)}) collective-permute-start(f32[28,16,256]{2,1,0:T(8,128)S(1)} %broadcast_select_fusion), channel_id=1, source_target_pairs={{0,128},{256,384},{1,129},{257,385},{2,130},{258,386},{3,131},{259... | collective-permute-start | bytes 1376264 | tf_op jit(solution)/shard_map/ppermute | solution.py:387
  73.7 9.2 %collective-permute-start.11 = (f32[28,16,256]{2,1,0:T(8,128)S(1)}, f32[28,16,256]{2,1,0:T(8,128)}, u32[]{:S(2)}, u32[]{:S(2)}) collective-permute-start(f32[28,16,256]{2,1,0:T(8,128)S(1)} %broadcast_select_fusion.1), channel_id=1, source_target_pairs={{0,64},{128,192},{256,320},{384,448},{1,65},{129,193},{257,321},{3... | collective-permute-start | bytes 1376264 | tf_op jit(solution)/shard_map/ppermute | solution.py:387
  77.1 13.4 %copy-start.5 = (f32[16,2,16,256]{3,2,1,0:T(8,128)}, f32[16,2,16,256]{3,2,1,0:T(8,128)S(1)}, u32[]{:S(2)}) copy-start(f32[16,2,16,256]{3,2,1,0:T(8,128)S(1)} %get-tuple-element.24.own.refs_0_) | copy-start | bytes 1572868
  77.1 20.5 %collective-permute-start.4 = (f32[16,2,16,256]{3,2,1,0:T(8,128)S(1)}, f32[16,2,16,256]{3,2,1,0:T(8,128)S(1)}, u32[]{:S(2)}, u32[]{:S(2)}) collective-permute-start(f32[16,2,16,256]{3,2,1,0:T(8,128)S(1)} %get-tuple-element.24.own.refs_0_), channel_id=1, source_target_pairs={{0,32},{16,48},{32,0},{48,16},{1,33},{17,49},{33,1},{49,17},{2,34}... | collective-permute-start | bytes 1572872 | tf_op jit(solution)/shard_map/ppermute | solution.py:366
  85.2 16.7 %collective-permute-start.13 = (f32[32,16,256]{2,1,0:T(8,128)S(1)}, f32[32,16,256]{2,1,0:T(8,128)}, u32[]{:S(2)}, u32[]{:S(2)}) collective-permute-start(f32[32,16,256]{2,1,0:T(8,128)S(1)} %place_rest.1.row0), channel_id=1, source_target_pairs={{0,32},{16,48},{32,0},{48,16},{1,33},{17,49},{33,1},{49,17},{2,34}... | collective-permute-start | bytes 1572872 | tf_op jit(solution)/shard_map/ppermute | solution.py:366
  88.1 33.3 %collective-permute-start.7 = (f32[16,2,16,256]{3,2,1,0:T(8,128)S(1)}, f32[16,2,16,256]{3,2,1,0:T(8,128)}, u32[]{:S(2)}, u32[]{:S(2)}) collective-permute-start(f32[16,2,16,256]{3,2,1,0:T(8,128)S(1)} %get-tuple-element.23.refs_4_), channel_id=1, source_target_pairs={{0,32},{16,48},{32,0},{48,16},{1,33},{17,49},{33,1},{49,17},{2,34}... | collective-permute-start | bytes 1572872 | tf_op jit(solution)/shard_map/ppermute | solution.py:366
  90.5 33.1 %collective-permute-start.3 = (f32[16,2,16,256]{3,2,1,0:T(8,128)S(1)}, f32[16,2,16,256]{3,2,1,0:T(8,128)}, u32[]{:S(2)}, u32[]{:S(2)}) collective-permute-start(f32[16,2,16,256]{3,2,1,0:T(8,128)S(1)} %get-tuple-element.24.own.refs_0_), channel_id=1, source_target_pairs={{0,16},{16,0},{32,48},{48,32},{1,17},{17,1},{33,49},{49,33},{2,18}... | collective-permute-start | bytes 1572872 | tf_op jit(solution)/shard_map/ppermute | solution.py:366
  97.5 13.0 %copy-start.12 = (f32[16,2,16,256]{3,2,1,0:T(8,128)}, f32[16,2,16,256]{3,2,1,0:T(8,128)S(1)}, u32[]{:S(2)}) copy-start(f32[16,2,16,256]{3,2,1,0:T(8,128)S(1)} %collective-permute-done.4.across.refs_2_) | copy-start | bytes 1572868
  97.6 28.2 %collective-permute-start.5 = (f32[16,2,16,256]{3,2,1,0:T(8,128)S(1)}, f32[16,2,16,256]{3,2,1,0:T(8,128)}, u32[]{:S(2)}, u32[]{:S(2)}) collective-permute-start(f32[16,2,16,256]{3,2,1,0:T(8,128)S(1)} %collective-permute-done.4.across.refs_2_), channel_id=1, source_target_pairs={{0,16},{16,0},{32,48},{48,32},{1,17},{17,1},{33,49},{49,33},{2,18}... | collective-permute-start | bytes 1572872 | tf_op jit(solution)/shard_map/ppermute | solution.py:366
  99.5 97.4 %collective-permute-start.12 = (f32[32,16,256]{2,1,0:T(8,128)S(1)}, f32[32,16,256]{2,1,0:T(8,128)}, u32[]{:S(2)}, u32[]{:S(2)}) collective-permute-start(f32[32,16,256]{2,1,0:T(8,128)S(1)} %place_rest.1.row0), channel_id=1, source_target_pairs={{0,16},{16,0},{32,48},{48,32},{1,17},{17,1},{33,49},{49,33},{2,18}... | collective-permute-start | bytes 1572872 | tf_op jit(solution)/shard_map/ppermute | solution.py:366
  101.9 95.0 %collective-permute-start.14 = (f32[32,16,256]{2,1,0:T(8,128)}, f32[32,16,256]{2,1,0:T(8,128)}, u32[]{:S(2)}, u32[]{:S(2)}) collective-permute-start(f32[32,16,256]{2,1,0:T(8,128)} %collective-permute-done.13.row2), channel_id=1, source_target_pairs={{0,16},{16,0},{32,48},{48,32},{1,17},{17,1},{33,49},{49,33},{2,18}... | collective-permute-start | bytes 1572872 | tf_op jit(solution)/shard_map/ppermute | solution.py:366
  110.5 41.2 %all-to-all-start.2 = ((f32[32,2,16,128]{3,2,1,0:T(8,128)}), f32[32,2,16,128]{3,2,1,0:T(8,128)S(1)}, u32[]{:S(2)}, u32[]{:S(2)}) async-start(f32[32,2,16,128]{3,2,1,0:T(8,128)} %bitcast.6), calls=%async_computation.2 | async-start | bytes 1048576 | tf_op jit(solution)/shard_map/all_to_all | solution.py:376
  121.4 43.1 %collective-permute-start.6 = (f32[16,2,16,256]{3,2,1,0:T(8,128)S(1)}, f32[16,2,16,256]{3,2,1,0:T(8,128)}, u32[]{:S(2)}, u32[]{:S(2)}) collective-permute-start(f32[16,2,16,256]{3,2,1,0:T(8,128)S(1)} %get-tuple-element.23.refs_4_), channel_id=1, source_target_pairs={{0,16},{16,0},{32,48},{48,32},{1,17},{17,1},{33,49},{49,33},{2,18}... | collective-permute-start | bytes 1572872 | tf_op jit(solution)/shard_map/ppermute | solution.py:366
  123.6 40.9 %collective-permute-start.8 = (f32[16,2,16,256]{3,2,1,0:T(8,128)}, f32[16,2,16,256]{3,2,1,0:T(8,128)}, u32[]{:S(2)}, u32[]{:S(2)}) collective-permute-start(f32[16,2,16,256]{3,2,1,0:T(8,128)} %collective-permute-done.7.refs_6_), channel_id=1, source_target_pairs={{0,16},{16,0},{32,48},{48,32},{1,17},{17,1},{33,49},{49,33},{2,18}... | collective-permute-start | bytes 1572872 | tf_op jit(solution)/shard_map/ppermute | solution.py:366
  154.9 42.0 %all-to-all-start.3 = ((f32[16,4,16,256]{3,2,1,0:T(8,128)}), f32[16,4,16,256]{3,2,1,0:T(8,128)S(1)}, u32[]{:S(2)}, u32[]{:S(2)}) async-start(f32[16,4,16,256]{3,2,1,0:T(8,128)} %get-tuple-element.21), calls=%async_computation.3 | async-start | bytes 2097152 | tf_op jit(solution)/shard_map/all_to_all | solution.py:376
  196.9 1.2 copy-start.2
  198.1 1.2 copy-start.4
  (10 other events, 9.6 us)

commit v5 on v4

--- a/solution.py
+++ b/solution.py
@@ -17,20 +17,14 @@
 WIDE = 256
 PANEL = 512
 TOP = 4
-HIGHEST = lax.Precision.HIGHEST
 
 VMEM = pl.BlockSpec(memory_space=pltpu.VMEM)
 SMEM = pl.BlockSpec(memory_space=pltpu.SMEM)
+HBM = pl.BlockSpec(memory_space=pl.ANY)
 
 
 def params(mib):
     return pltpu.CompilerParams(vmem_limit_bytes=mib << 20)
-
-
-def contract(a, b, dims):
-    return lax.dot_general(
-        a, b, ((dims[:1], dims[1:]), ((), ())), precision=HIGHEST, preferred_element_type=jnp.float32
-    )
 
 
 def split(a):
@@ -47,19 +41,7 @@
     return product(a[0], b[1]) + product(a[1], b[0]) + product(a[0], b[0])
 
 
-def dot(a, b):
-    return contract(a, b, (1, 0))
-
-
-def dot_t(a, b):
-    return contract(a, b, (1, 1))
-
-
-def t_dot(a, b):
-    return contract(a, b, (0, 0))
-
-
-def spread_kernel(where_ref, map_ref, child_ref, out_ref, low_ref):
+def spread_kernel(where_ref, map_ref, child_ref, out_ref):
     child = where_ref[0]
     out_ref[...] = jnp.zeros_like(out_ref)
     lane_block = lax.broadcasted_iota(jnp.int32, (BLK, TILE), 1) // BLK
@@ -76,22 +58,32 @@
         return carry
 
     lax.fori_loop(0, child_ref.shape[1] // TILE, body, 0)
-    for sub in range(SUBS):
-        low_ref[sub] = out_ref[: 2 * ROWS]
-
-
-def spread_rows(where, index_map, child):
-    return pl.pallas_call(
-        spread_kernel,
-        out_shape=(
-            jax.ShapeDtypeStruct((2 * SHARDS, BLK, TILE), jnp.float32),
-            jax.ShapeDtypeStruct((SUBS, 2 * ROWS, BLK, TILE), jnp.float32),
-        ),
-        in_specs=[SMEM, SMEM, VMEM],
-        out_specs=(VMEM, VMEM),
-        compiler_params=params(4),
-        name="spread_rows",
-    )(where, index_map, child)
+
+
+def spread_low_kernel(where_ref, map_ref, child_ref, out_ref):
+    child = where_ref[0]
+    count = 2 * ROWS
+    out_ref[0] = jnp.zeros_like(out_ref[0])
+    lane_block = lax.broadcasted_iota(jnp.int32, (BLK, TILE), 1) // BLK
+
+    def body(tile, carry):
+        for part in range(TILE // BLK):
+            block = map_ref[child, tile * (TILE // BLK) + part]
+            target = block // (TILE // BLK)
+
+            @pl.when(target < count)
+            def _():
+                place = block % (TILE // BLK)
+                rows = child_ref[:, pl.ds(pl.multiple_of(tile * TILE, TILE), TILE)]
+                shift = (place - part + TILE // BLK) % (TILE // BLK) * BLK
+                moved = pltpu.roll(rows, shift, 1)
+                out_ref[0, target] = jnp.where(lane_block == place, moved, out_ref[0, target])
+
+        return carry
+
+    lax.fori_loop(0, child_ref.shape[1] // TILE, body, 0)
+    for sub in range(1, SUBS):
+        out_ref[sub] = out_ref[0]
 
 
 def each_source(where_ref, map_ref, use):
@@ -132,14 +124,17 @@
         top_ref[q] = out_ref[...]
 
 
-def place_rest_kernel(where_ref, map_ref, received_ref, parent_ref, top_ref, out_ref):
+def place_rest_kernel(where_ref, map_ref, received_ref, parent_ref, top_ref, pivots_ref, out_ref):
     def use(source, slot):
         @pl.when(slot >= TOP)
         def _():
-            add_block(out_ref, slot, parent_ref[slot - TOP], received_ref, source)
+            add_block(out_ref, SHARDS + slot, parent_ref[slot - TOP], received_ref, source)
 
     each_source(where_ref, map_ref, use)
-    out_ref[:TOP] = top_ref[0]
+    for q in range(COLS):
+        for half in range(2):
+            out_ref[2 * q + half] = pivots_ref[q, 2 + half]
+    out_ref[SHARDS : SHARDS + TOP] = top_ref[0]
 
 
 FRONT = jax.ShapeDtypeStruct((SHARDS, BLK, WIDE), jnp.float32)
@@ -220,6 +215,10 @@
             e[h] = e[h] - de
 
 
+def multiply(a, b, dims):
+    return contract_split(split(a), split(b), dims)
+
+
 def invert_factor(m_ref, w_ref, t_ref):
     tiles = m_ref.shape[0] // TILE
     w_ref[...] = jnp.zeros_like(w_ref)
@@ -236,45 +235,55 @@
                 lo, hi = c * TILE, (c + 1) * TILE
                 t = t_ref[...]
                 if c:
-                    w_ref[lo:hi, :lo] = dot(t, w_ref[lo:hi, :lo])
+                    w_ref[lo:hi, :lo] = multiply(t, w_ref[lo:hi, :lo], (1, 0))
                 w_ref[lo:hi, lo:hi] = t
                 if c + 1 < tiles:
-                    x = dot(t, m_ref[lo:hi, hi:])
-                    m_ref[hi:, hi:] = m_ref[hi:, hi:] - t_dot(x, x)
-                    w_ref[hi:, :hi] = w_ref[hi:, :hi] - t_dot(x, w_ref[lo:hi, :hi])
+                    x = multiply(t, m_ref[lo:hi, hi:], (1, 0))
+                    m_ref[hi:, hi:] = m_ref[hi:, hi:] - multiply(x, x, (0, 0))
+                    w_ref[hi:, :hi] = w_ref[hi:, :hi] - multiply(x, w_ref[lo:hi, :hi], (0, 0))
 
         return carry
 
     lax.fori_loop(0, tiles, body, 0)
 
 
-def fill(row, refs, into, first, last):
+def chunk_of(row, number):
+    return (row // 2 ^ number // 2) * 2 + (row % 2 ^ number % 2)
+
+
+def each_chunk(row, refs, use, first=0, last=ROWS):
     for number, ref in enumerate(refs):
-        chunk = (row // 2 ^ number // 2) * 2 + (row % 2 ^ number % 2)
+        chunk = chunk_of(row, number)
 
         @pl.when((chunk >= first) & (chunk < last))
         def _():
-            low = pl.multiple_of((chunk - first) * WIDE, WIDE)
-            for q in range(COLS):
-                for half in range(2):
-                    at = (2 * q + half) * BLK
-                    into[at : at + BLK, pl.ds(low, WIDE)] = ref[q, half]
-
-
-def first_kernel(where_ref, own, core, across, both, w_ref, m_ref, t_ref):
-    fill(where_ref[2], (own, core, across, both), m_ref, 0, 2)
+            use(number, ref, pl.ds(pl.multiple_of((chunk - first) * WIDE, WIDE), WIDE))
+
+
+def first_kernel(where_ref, own, core, across, both, w_ref, m_ref, t_ref, sems):
+    def copy(number, ref, lanes):
+        return pltpu.make_async_copy(ref, m_ref.at[:, lanes], sems.at[number])
+
+    row, refs = where_ref[2], (own, core, across, both)
+    each_chunk(row, refs, lambda *at: copy(*at).start(), 0, 2)
+    each_chunk(row, refs, lambda *at: copy(*at).wait(), 0, 2)
     invert_factor(m_ref, w_ref, t_ref)
+
+
+def square():
+    return pltpu.VMEM((PANEL, PANEL), jnp.float32)
 
 
 def first_factor(where, pieces):
     return pl.pallas_call(
         first_kernel,
         out_shape=jax.ShapeDtypeStruct((PANEL, PANEL), jnp.float32),
-        in_specs=[SMEM] + [VMEM] * 4,
+        in_specs=[SMEM] + [HBM] * 4,
         out_specs=VMEM,
         scratch_shapes=[
-            pltpu.VMEM((PANEL, PANEL), jnp.float32),
+            square(),
             pltpu.VMEM((TILE, TILE), jnp.float32),
+            pltpu.SemaphoreType.DMA((4,)),
         ],
         compiler_params=params(10),
         cost_estimate=pl.CostEstimate(flops=60_000_000_000, bytes_accessed=4 << 20, transcendentals=0),
@@ -282,13 +291,35 @@
     )(where, *pieces)
 
 
-def second_kernel(where_ref, inv_ref, *refs):
-    upper, lower, (w_ref, x_ref, a_ref, m_ref, t_ref) = refs[:4], refs[4:8], refs[8:]
-    fill(where_ref[2], upper, a_ref, 2, 4)
-    x_ref[...] = dot(inv_ref[...], a_ref[...])
-    fill(where_ref[2], lower, a_ref, 2, 4)
-    m_ref[...] = a_ref[...] - t_dot(x_ref[...], x_ref[...])
+def second_kernel(where_ref, inv_hbm, *refs):
+    upper, lower, refs = refs[:4], refs[4:8], refs[8:]
+    w_hbm, x_hbm, inv_ref, a_ref, m_ref, w_ref, x_ref, t_ref, sems = refs
+
+    def copy_upper(number, ref, lanes):
+        return pltpu.make_async_copy(ref, a_ref.at[:, lanes], sems.at[number])
+
+    def copy_lower(number, ref, lanes):
+        rows = ref.at[pl.ds(0, PANEL), :]
+        return pltpu.make_async_copy(rows, m_ref.at[:, lanes], sems.at[4 + number])
+
+    row = where_ref[2]
+    inv = pltpu.make_async_copy(inv_hbm, inv_ref, sems.at[8])
+    inv.start()
+    each_chunk(row, upper, lambda *at: copy_upper(*at).start(), 2, 4)
+    each_chunk(row, lower, lambda *at: copy_lower(*at).start(), 2, 4)
+    inv.wait()
+    each_chunk(row, upper, lambda *at: copy_upper(*at).wait(), 2, 4)
+    x_ref[...] = multiply(inv_ref[...], a_ref[...], (1, 0))
+    out = pltpu.make_async_copy(x_ref, x_hbm, sems.at[9])
+    out.start()
+    x = x_ref[...]
+    each_chunk(row, lower, lambda *at: copy_lower(*at).wait(), 2, 4)
+    m_ref[...] = m_ref[...] - multiply(x, x, (0, 0))
     invert_factor(m_ref, w_ref, t_ref)
+    last = pltpu.make_async_copy(w_ref, w_hbm, sems.at[10])
+    last.start()
+    out.wait()
+    last.wait()
 
 
 def second_factor(where, inv, upper, lower):
@@ -296,68 +327,86 @@
     return pl.pallas_call(
         second_kernel,
         out_shape=(shape, shape),
-        in_specs=[SMEM] + [VMEM] * 9,
-        out_specs=(VMEM, VMEM),
+        in_specs=[SMEM] + [HBM] * 9,
+        out_specs=(HBM, HBM),
         scratch_shapes=[
-            pltpu.VMEM((PANEL, PANEL), jnp.float32),
-            pltpu.VMEM((PANEL, PANEL), jnp.float32),
+            square(), square(), square(), square(), square(),
             pltpu.VMEM((TILE, TILE), jnp.float32),
+            pltpu.SemaphoreType.DMA((11,)),
         ],
-        compiler_params=params(16),
+        compiler_params=params(20),
         cost_estimate=pl.CostEstimate(flops=60_000_000_000, bytes_accessed=8 << 20, transcendentals=0),
         name="second_factor",
     )(where, inv, *upper, *lower)
 
 
 def finish_kernel(
-    where_ref, inv0_ref, inv1_ref, x01_ref, cols_ref, row0, row1, row2, row3, front_ref, out_ref,
-    rows_ref, cols0_ref, cols1_ref,
+    where_ref, inv0_hbm, inv1_hbm, x01_hbm, cols_hbm, row0, row1, row2, row3, front_hbm, out_ref,
+    inv0_ref, inv1_ref, x01_ref, rows_ref, cols0_ref, cols1_ref, front_ref, sems,
 ):
     col, row, shard = where_ref[1], where_ref[2], where_ref[3]
-    for number, ref in enumerate((row0, row1, row2, row3)):
-        chunk = (row // 2 ^ number // 2) * 2 + (row % 2 ^ number % 2)
-        low = pl.multiple_of(chunk * WIDE, WIDE)
-        for slot in range(SHARDS):
-            rows_ref[slot * BLK : (slot + 1) * BLK, pl.ds(low, WIDE)] = ref[slot]
-    for q in range(COLS):
-        for half in range(2):
-            at = slice(q * 2 * BLK + half * BLK, q * 2 * BLK + (half + 1) * BLK)
-            cols0_ref[at, :] = cols_ref[q, half]
-            cols1_ref[at, :] = cols_ref[q, 2 + half]
+    refs = (row0, row1, row2, row3)
+
+    def copy_rows(number, ref, lanes):
+        return pltpu.make_async_copy(
+            ref.at[pl.ds(PANEL, PANEL), :], rows_ref.at[:, lanes], sems.at[number]
+        )
+
+    copies = [
+        (inv0_hbm, inv0_ref),
+        (cols_hbm.at[:, pl.ds(0, 2 * BLK), :], cols0_ref),
+        (cols_hbm.at[:, pl.ds(2 * BLK, 2 * BLK), :], cols1_ref),
+        (x01_hbm, x01_ref),
+        (inv1_hbm, inv1_ref),
+        (front_hbm, front_ref),
+    ]
+    copies = [
+        pltpu.make_async_copy(source, target, sems.at[4 + i])
+        for i, (source, target) in enumerate(copies)
+    ]
+    each_chunk(row, refs, lambda *at: copy_rows(*at).start())
+    for copy in copies:
+        copy.start()
+    each_chunk(row, refs, lambda *at: copy_rows(*at).wait())
+    for copy in copies:
+        copy.wait()
     inv0, inv1, x01 = split(inv0_ref[...]), split(inv1_ref[...]), split(x01_ref[...])
     r0 = split(contract_split(split(rows_ref[:, :PANEL]), inv0, (1, 1)))
-    c0 = contract_split(inv0, split(cols0_ref[...]), (1, 0))
-    cols0_ref[...] = c0
+    c0 = contract_split(inv0, split(cols0_ref[...].reshape(PANEL, WIDE)), (1, 0))
+    cols0_ref[...] = c0.reshape(cols0_ref.shape)
     c0 = split(c0)
     r1 = split(rows_ref[:, PANEL:] - contract_split(r0, x01, (1, 0)))
     r1 = split(contract_split(r1, inv1, (1, 1)))
-    c1 = split(cols1_ref[...] - contract_split(x01, c0, (0, 0)))
+    c1 = split(cols1_ref[...].reshape(PANEL, WIDE) - contract_split(x01, c0, (0, 0)))
     c1 = contract_split(inv1, c1, (1, 0))
-    cols1_ref[...] = c1
+    cols1_ref[...] = c1.reshape(cols1_ref.shape)
     update = contract_split(r0, c0, (1, 0)) + contract_split(r1, split(c1), (1, 0))
     live = (shard >= ROWS).astype(jnp.float32)
-    for slot in range(4, SHARDS):
+    for slot in range(TOP, SHARDS):
         rows = slice(slot * BLK, (slot + 1) * BLK)
         out_ref[slot] = (front_ref[slot] - update[rows]) * live
-    mine = pl.multiple_of(col * 2 * BLK, 2 * BLK)
     past = (shard >= ROWS // 2).astype(jnp.float32)
     for half in range(2):
-        out_ref[half] = cols0_ref[pl.ds(mine + half * BLK, BLK), :]
-        out_ref[2 + half] = cols1_ref[pl.ds(mine + half * BLK, BLK), :] * past
+        rows = slice(half * BLK, (half + 1) * BLK)
+        out_ref[half] = cols0_ref[col, rows, :]
+        out_ref[2 + half] = cols1_ref[col, rows, :] * past
 
 
 def finish(where, inv0, inv1, x01, cols, rows, front):
     return pl.pallas_call(
         finish_kernel,
-        out_shape=jax.ShapeDtypeStruct((SHARDS, BLK, WIDE), jnp.float32),
-        in_specs=[SMEM] + [VMEM] * 9,
+        out_shape=FRONT,
+        in_specs=[SMEM] + [HBM] * 9,
         out_specs=VMEM,
         scratch_shapes=[
+            square(), square(), square(),
             pltpu.VMEM((PANEL, 2 * PANEL), jnp.float32),
-            pltpu.VMEM((PANEL, WIDE), jnp.float32),
-            pltpu.VMEM((PANEL, WIDE), jnp.float32),
+            pltpu.VMEM((COLS, 2 * BLK, WIDE), jnp.float32),
+            pltpu.VMEM((COLS, 2 * BLK, WIDE), jnp.float32),
+            pltpu.VMEM((SHARDS, BLK, WIDE), jnp.float32),
+            pltpu.SemaphoreType.DMA((10,)),
         ],
-        compiler_params=params(24),
+        compiler_params=params(28),
         name="finish",
     )(where, inv0, inv1, x01, cols, *rows, front)
 
@@ -397,7 +446,12 @@
     parent_top = from_first(parent[:TOP], sub)
     parent_rest = from_first(parent[TOP:], sub)
 
-    spread, low = spread_rows(where, index_map, child_schur)
+    low = call(
+        spread_low_kernel,
+        jax.ShapeDtypeStruct((SUBS, 2 * ROWS, BLK, TILE), jnp.float32),
+        (where, index_map, child_schur),
+        4,
+    )
     low = exchange(low.reshape(SHARDS, 2, BLK, TILE), ("sub", "row"))
     tops, _ = call(
         place_top_kernel,
@@ -405,19 +459,34 @@
         (where, index_map, low, parent_top),
         6,
     )
+    spread = call(
+        spread_kernel,
+        jax.ShapeDtypeStruct((2 * SHARDS, BLK, TILE), jnp.float32),
+        (where, index_map, child_schur),
+        4,
+    )
+    tops, spread = lax.optimization_barrier((tops, spread))
     pivots = exchange(tops, "col")
-    rows = call(place_rest_kernel, FRONT, (where, index_map, low, parent_rest, tops), 6)
-    rows = over_rows(rows)
-    upper = over_rows(pivots[:, :2])
-    lower = over_rows(pivots[:, 2:])
+    tail = call(
+        place_rest_kernel,
+        jax.ShapeDtypeStruct((2 * SHARDS, BLK, WIDE), jnp.float32),
+        (where, index_map, low, parent_rest, tops, pivots),
+        8,
+    )
+    upper = over_rows(pivots[:, :2].reshape(PANEL, WIDE))
     inv0 = first_factor(where, upper)
 
+
     spread, _ = lax.optimization_barrier((spread.reshape(SHARDS, 2, BLK, TILE), pivots))
-    received, _ = lax.optimization_barrier((exchange(spread, ("sub", "row")), inv0))
+    tail = tail.reshape(2 * PANEL, WIDE)
+    received, across, _ = lax.optimization_barrier(
+        (exchange(spread, ("sub", "row")), swap(tail, "row", 2), inv0)
+    )
+    tail = tail, swap(tail, "row", 1), across, swap(across, "row", 1)
     front, tops = call(place_kernel, (FRONT, TOPS), (where, index_map, received, parent), 6)
-    inv1, x01 = second_factor(where, inv0, upper, lower)
-    cols = exchange(tops, "col")
-    out = finish(where, inv0, inv1, x01, cols, rows, front)
+    inv1, x01 = second_factor(where, inv0, upper, tail)
+    cols = exchange(tops, "col").reshape(COLS, TOP * BLK, WIDE)
+    out = finish(where, inv0, inv1, x01, cols, tail, front)
     return out.reshape(parent_front.shape)
 
 

time: 210 us -> 197 us (0.938)
  starting transfers between devices: 96.5 us -> 84.3 us
  waiting for transfers between devices: 25.2 us -> 21.8 us
    ppermute x6, waiting for transfers between devices: 25.2 us -> 13.5 us  [from_first(): got = lax.ppermute(x, 'sub', pairs)]
    pallas_call x3 -> x5, Pallas kernels: 7.27 us -> 17 us  [call(): pl.pallas_call(kernel, out_shape=out_shape, in_specs=[SMEM, SMEM] + [VMEM...]
    ppermute x9 -> x6, starting transfers between devices: 32.4 us -> 23.2 us  [swap(): return lax.ppermute(x, axis, [(i, i ^ bit) for i in range(ROWS)])]
    all_to_all x4, waiting for transfers between devices: 0.01 us -> 7.74 us  [exchange(): return lax.all_to_all(x, axis, split_axis=0, concat_axis=0, tiled=True)]
    pallas_call x2 -> x1, Pallas kernels: 13.9 us -> 9.08 us  [finish(): pl.pallas_call(finish_kernel, out_shape=FRONT, in_specs=[SMEM] + [HBM] *...]
    all_to_all x4, starting transfers between devices: 42.7 us -> 39.6 us  [exchange(): return lax.all_to_all(x, axis, split_axis=0, concat_axis=0, tiled=True)]
    pallas_call x1, Pallas kernels: 28.3 us -> 25.5 us  [second_factor(): pl.pallas_call(second_kernel, out_shape=(shape, shape), in_specs=[SMEM] +...]
  transfers between devices with their start and end apart: 19 -> 16, of which waited for: 6 -> 5; matrix products, arithmetic and copies ran while one was open for 1% -> 1% of each run, Pallas kernels for 27% -> 29%
where the time goes in v5:
time: 197 us; the launch traced here: 195 us
  starting transfers between devices  84.3 us (43%)
  Pallas kernels  74.9 us (38%)
  waiting for transfers between devices  21.8 us (11%)
  local copies, waits for them, and re-layouts  12.9 us (7%)
    all_to_all x4, starting transfers between devices, exchange(): return lax.all_to_all(x, axis, split_axis=0, concat_axis=0, tiled=True)  39.6 us
    pallas_call x1, Pallas kernels, second_factor(): pl.pallas_call(second_kernel, out_shape=(shape, shape), in_specs=[SMEM] +...  25.5 us
    pallas_call x1, Pallas kernels, first_factor(): pl.pallas_call(first_kernel, out_shape=jax.ShapeDtypeStruct((PANEL, PANEL...  23.2 us
    ppermute x6, starting transfers between devices, swap(): return lax.ppermute(x, axis, [(i, i ^ bit) for i in range(ROWS)])  23.2 us
    ppermute x6, starting transfers between devices, from_first(): got = lax.ppermute(x, 'sub', pairs)  21.5 us
    pallas_call x5, Pallas kernels, call(): pl.pallas_call(kernel, out_shape=out_shape, in_specs=[SMEM, SMEM] + [VMEM...  17 us
    ppermute x6, waiting for transfers between devices, from_first(): got = lax.ppermute(x, 'sub', pairs)  13.5 us
    unnamed x30, local copies, waits for them, and re-layouts  12 us
  transfers between devices with their start and end apart: 16, of which 5 were waited for; matrix products, arithmetic and copies ran while one was open for 1% of the time, Pallas kernels for 29%

profile of v5, /device:TPU:1, one launch (start us, length us, event | category | flops | bytes accessed | tf_op | source)
XLA Modules:
  0.0 194.8 jit_solution(9058738506970338253)
XLA Ops:
  1.6 6.3 %spread_low.1 = f32[8,8,16,128]{3,2,1,0:T(8,128)} custom-call(s32[4]{0:T(128)S(1)} %pad_add_fusion.where_ref, s32[2,256]{1,0:T(2,128)S(1)} %copy-done.14, f32[16,4096]{1,0:T(8,128)S(1)} %copy-done.10), custom_call_target="tpu_custom_call" | custom-call | tf_op jit(solution)/shard_map/spread_low/pallas_call | solution.py:146
  7.9 13.4 %all-to-all-start = ((f32[32,2,16,128]{3,2,1,0:T(8,128)}), f32[32,2,16,128]{3,2,1,0:T(8,128)S(1)}, u32[]{:S(2)}, u32[]{:S(2)}) async-start(f32[32,2,16,128]{3,2,1,0:T(8,128)} %bitcast.4), calls=%async_computation | async-start | bytes 1048576 | tf_op jit(solution)/shard_map/all_to_all | solution.py:425
  21.4 7.3 %collective-permute-start = (f32[4,16,256]{2,1,0:T(8,128)S(1)}, f32[4,16,256]{2,1,0:T(8,128)S(1)}, u32[]{:S(2)}, u32[]{:S(2)}) collective-permute-start(f32[4,16,256]{2,1,0:T(8,128)S(1)} %bitcast.24), channel_id=1, source_target_pairs={{0,256},{1,257},{2,258},{3,259},{4,260},{5,261},{6,262},{7,263},{8... | collective-permute-start | bytes 196616 | tf_op jit(solution)/shard_map/ppermute | solution.py:436
  28.8 4.4 %collective-permute-done = f32[4,16,256]{2,1,0:T(8,128)S(1)} collective-permute-done((f32[4,16,256]{2,1,0:T(8,128)S(1)}, f32[4,16,256]{2,1,0:T(8,128)S(1)}, u32[]{:S(2)}, u32[]{:S(2)}) %collective-permute-start) | collective-permute-done | bytes 65568 | tf_op jit(solution)/shard_map/ppermute | solution.py:436
  37.1 4.4 %spread.1 = f32[64,16,128]{2,1,0:T(8,128)S(1)} custom-call(s32[4]{0:T(128)S(1)} %pad_add_fusion.where_ref, s32[2,256]{1,0:T(2,128)S(1)} %copy-done.14, f32[16,4096]{1,0:T(8,128)S(1)} %copy-done.11), custom_call_target="tpu_custom_call" | custom-call | tf_op jit(solution)/shard_map/spread/pallas_call | solution.py:146
  42.4 2.6 %place_top.1 = (f32[16,4,16,256]{3,2,1,0:T(8,128)}, f32[4,16,256]{2,1,0:T(8,128)}) custom-call(s32[4]{0:T(128)S(1)} %pad_add_fusion.where_ref, s32[2,256]{1,0:T(2,128)S(1)} %copy-done.14, f32[32,2,16,128]{3,2,1,0:T(8,128)S(1)} %all-to-all-done.received_ref, f32[4,16,256]{2,1,0:T(8,128)S(1)} %broadcast_select_fusion.5.parent_ref), custom_call_target="tpu_custom_call" | custom-call | tf_op jit(solution)/shard_map/place_top/pallas_call | solution.py:146
  45.0 9.1 %all-to-all-start.1 = ((f32[16,4,16,256]{3,2,1,0:T(8,128)}), f32[16,4,16,256]{3,2,1,0:T(8,128)S(1)}, u32[]{:S(2)}, u32[]{:S(2)}) async-start(f32[16,4,16,256]{3,2,1,0:T(8,128)} %get-tuple-element.16.top_ref), calls=%async_computation.1 | async-start | bytes 2097152 | tf_op jit(solution)/shard_map/all_to_all | solution.py:425
  54.1 8.2 %collective-permute-start.6 = (f32[28,16,256]{2,1,0:T(8,128)S(1)}, f32[28,16,256]{2,1,0:T(8,128)S(1)}, u32[]{:S(2)}, u32[]{:S(2)}) collective-permute-start(f32[28,16,256]{2,1,0:T(8,128)S(1)} %bitcast.22), channel_id=1, source_target_pairs={{0,256},{1,257},{2,258},{3,259},{4,260},{5,261},{6,262},{7,263},{8... | collective-permute-start | bytes 1376264 | tf_op jit(solution)/shard_map/ppermute | solution.py:436
  62.3 7.9 %collective-permute-done.6 = f32[28,16,256]{2,1,0:T(8,128)S(1)} collective-permute-done((f32[28,16,256]{2,1,0:T(8,128)S(1)}, f32[28,16,256]{2,1,0:T(8,128)S(1)}, u32[]{:S(2)}, u32[]{:S(2)}) %collective-permute-start.6) | collective-permute-done | bytes 458784 | tf_op jit(solution)/shard_map/ppermute | solution.py:436
  70.2 2.1 %collective-permute-start.7 = (f32[28,16,256]{2,1,0:T(8,128)S(1)}, f32[28,16,256]{2,1,0:T(8,128)}, u32[]{:S(2)}, u32[]{:S(2)}) collective-permute-start(f32[28,16,256]{2,1,0:T(8,128)S(1)} %broadcast_select_fusion), channel_id=1, source_target_pairs={{0,128},{256,384},{1,129},{257,385},{2,130},{258,386},{3,131},{259... | collective-permute-start | bytes 1376264 | tf_op jit(solution)/shard_map/ppermute | solution.py:436
  72.3 7.7 %all-to-all-done.1.pivots_ref = f32[16,4,16,256]{3,2,1,0:T(8,128)S(1)} async-done(((f32[16,4,16,256]{3,2,1,0:T(8,128)}), f32[16,4,16,256]{3,2,1,0:T(8,128)S(1)}, u32[]{:S(2)}, u32[]{:S(2)}) %all-to-all-start.1) | async-done | bytes 1048608 | tf_op jit(solution)/shard_map/all_to_all | solution.py:425
  80.9 2.4 %collective-permute-start.4 = (f32[512,256]{1,0:T(8,128)}, f32[512,256]{1,0:T(8,128)}, u32[]{:S(2)}, u32[]{:S(2)}) collective-permute-start(f32[512,256]{1,0:T(8,128)} %bitcast.6.own.refs_0_), channel_id=1, source_target_pairs={{0,32},{16,48},{32,0},{48,16},{1,33},{17,49},{33,1},{49,17},{2,34}... | collective-permute-start | bytes 1572872 | tf_op jit(solution)/shard_map/ppermute | solution.py:415
  84.7 6.4 %collective-permute-start.3 = (f32[512,256]{1,0:T(8,128)}, f32[512,256]{1,0:T(8,128)}, u32[]{:S(2)}, u32[]{:S(2)}) collective-permute-start(f32[512,256]{1,0:T(8,128)} %bitcast.6.own.refs_0_), channel_id=1, source_target_pairs={{0,16},{16,0},{32,48},{48,32},{1,17},{17,1},{33,49},{49,33},{2,18}... | collective-permute-start | bytes 1572872 | tf_op jit(solution)/shard_map/ppermute | solution.py:415
  91.7 7.6 %collective-permute-start.5 = (f32[512,256]{1,0:T(8,128)}, f32[512,256]{1,0:T(8,128)}, u32[]{:S(2)}, u32[]{:S(2)}) collective-permute-start(f32[512,256]{1,0:T(8,128)} %collective-permute-done.4.across.refs_2_), channel_id=1, source_target_pairs={{0,16},{16,0},{32,48},{48,32},{1,17},{17,1},{33,49},{49,33},{2,18}... | collective-permute-start | bytes 1572872 | tf_op jit(solution)/shard_map/ppermute | solution.py:415
  99.4 2.3 %place_rest.1 = f32[64,16,256]{2,1,0:T(8,128)S(1)} custom-call(s32[4]{0:T(128)S(1)} %pad_add_fusion.where_ref, s32[2,256]{1,0:T(2,128)S(1)} %copy-done.14, f32[32,2,16,128]{3,2,1,0:T(8,128)S(1)} %all-to-all-done.received_ref, f32[28,16,256]{2,1,0:T(8,128)S(1)} %broadcast_select_fusion.2.parent_ref, f32[16,4,16,256]{3,2,1,0:T(8,128)} %get-tuple-element.16.top_ref, ...), custom_call_target="tpu_custom_call" | custom-call | tf_op jit(solution)/shard_map/place_rest/pallas_call | solution.py:146
  101.7 2.4 %collective-permute-start.10 = (f32[1024,256]{1,0:T(8,128)S(1)}, f32[1024,256]{1,0:T(8,128)}, u32[]{:S(2)}, u32[]{:S(2)}) collective-permute-start(f32[1024,256]{1,0:T(8,128)S(1)} %bitcast.16), channel_id=1, source_target_pairs={{0,32},{16,48},{32,0},{48,16},{1,33},{17,49},{33,1},{49,17},{2,34}... | collective-permute-start | bytes 3145736 | tf_op jit(solution)/shard_map/ppermute | solution.py:415
  104.1 2.2 %collective-permute-start.9 = (f32[1024,256]{1,0:T(8,128)S(1)}, f32[1024,256]{1,0:T(8,128)}, u32[]{:S(2)}, u32[]{:S(2)}) collective-permute-start(f32[1024,256]{1,0:T(8,128)S(1)} %bitcast.17), channel_id=1, source_target_pairs={{0,16},{16,0},{32,48},{48,32},{1,17},{17,1},{33,49},{49,33},{2,18}... | collective-permute-start | bytes 3145736 | tf_op jit(solution)/shard_map/ppermute | solution.py:415
  106.3 9.4 %all-to-all-start.2 = ((f32[32,2,16,128]{3,2,1,0:T(8,128)}), f32[32,2,16,128]{3,2,1,0:T(8,128)S(1)}, u32[]{:S(2)}, u32[]{:S(2)}) async-start(f32[32,2,16,128]{3,2,1,0:T(8,128)} %bitcast.21), calls=%async_computation.2 | async-start | bytes 1048576 | tf_op jit(solution)/shard_map/all_to_all | solution.py:425
  115.7 23.2 %first_factor.1.inv_hbm.inv0_hbm = f32[512,512]{1,0:T(8,128)S(1)} custom-call(s32[4]{0:T(128)S(1)} %pad_add_fusion.where_ref, f32[512,256]{1,0:T(8,128)} %bitcast.6.own.refs_0_, f32[512,256]{1,0:T(8,128)} %collective-permute-done.3.core.refs_1_, f32[512,256]{1,0:T(8,128)} %collective-permute-done.4.across.refs_2_, f32[512,256]{1,0:T(8,128)} %collective-permute-done.5.both.refs_3_), custom_call_target="tpu_custom_call" | custom-call | flops 60000002048 | bytes 4194304 | tf_op jit(solution)/shard_map/first_factor/pallas_call | solution.py:278
  140.0 2.1 %collective-permute-start.11 = (f32[1024,256]{1,0:T(8,128)}, f32[1024,256]{1,0:T(8,128)}, u32[]{:S(2)}, u32[]{:S(2)}) collective-permute-start(f32[1024,256]{1,0:T(8,128)} %collective-permute-done.10.refs_6_.row2), channel_id=1, source_target_pairs={{0,16},{16,0},{32,48},{48,32},{1,17},{17,1},{33,49},{49,33},{2,18}... | collective-permute-start | bytes 3145736 | tf_op jit(solution)/shard_map/ppermute | solution.py:415
  142.1 1.4 place.1
  145.4 7.7 %all-to-all-start.3 = ((f32[16,4,16,256]{3,2,1,0:T(8,128)}), f32[16,4,16,256]{3,2,1,0:T(8,128)S(1)}, u32[]{:S(2)}, u32[]{:S(2)}) async-start(f32[16,4,16,256]{3,2,1,0:T(8,128)} %copy-done.9), calls=%async_computation.3 | async-start | bytes 2097152 | tf_op jit(solution)/shard_map/all_to_all | solution.py:425
  154.4 25.5 %second_factor.1 = (f32[512,512]{1,0:T(8,128)S(1)}, f32[512,512]{1,0:T(8,128)S(1)}) custom-call(s32[4]{0:T(128)S(1)} %pad_add_fusion.where_ref, f32[512,512]{1,0:T(8,128)S(1)} %copy-done.3, f32[512,256]{1,0:T(8,128)} %bitcast.6.own.refs_0_, f32[512,256]{1,0:T(8,128)} %collective-permute-done.3.core.refs_1_, ...), custom_call_target="tpu_custom_call" | custom-call | flops 60000002048 | bytes 8388608 | tf_op jit(solution)/shard_map/second_factor/pallas_call | solution.py:327
  185.5 9.1 %finish.1 = f32[32,16,256]{2,1,0:T(8,128)} custom-call(s32[4]{0:T(128)S(1)} %pad_add_fusion.where_ref, f32[512,512]{1,0:T(8,128)S(1)} %copy-done.4, f32[512,512]{1,0:T(8,128)S(1)} %copy-done.6, f32[512,512]{1,0:T(8,128)S(1)} %copy-done.8, f32[16,64,256]{2,1,0:T(8,128)S(1)} %bitcast.15, f32[1024,256]{1,0:T(8,128)S(1)} %bitcast.19, ...), custom_call_target="tpu_custom_call" | custom-call | tf_op jit(solution)/shard_map/finish/pallas_call | solution.py:396
  (56 shorter events, 19.0 us)
Async XLA Ops:
  7.9 13.4 %copy-start = (f32[16,1,32,256]{3,2,1,0:T(8,128)S(1)}, f32[16,1,32,256]{3,2,1,0:T(8,128)}, u32[]{:S(2)}) copy-start(f32[16,1,32,256]{3,2,1,0:T(8,128)} %param.3) | copy-start | bytes 1572868
  7.9 34.4 %all-to-all-start = ((f32[32,2,16,128]{3,2,1,0:T(8,128)}), f32[32,2,16,128]{3,2,1,0:T(8,128)S(1)}, u32[]{:S(2)}, u32[]{:S(2)}) async-start(f32[32,2,16,128]{3,2,1,0:T(8,128)} %bitcast.4), calls=%async_computation | async-start | bytes 1048576 | tf_op jit(solution)/shard_map/all_to_all | solution.py:425
  21.4 15.7 %copy-start.11 = (f32[16,4096]{1,0:T(8,128)S(1)}, f32[16,4096]{1,0:T(8,128)}, u32[]{:S(2)}) copy-start(f32[16,4096]{1,0:T(8,128)} %child_ref.3) | copy-start | bytes 786436
  21.4 11.7 %collective-permute-start = (f32[4,16,256]{2,1,0:T(8,128)S(1)}, f32[4,16,256]{2,1,0:T(8,128)S(1)}, u32[]{:S(2)}, u32[]{:S(2)}) collective-permute-start(f32[4,16,256]{2,1,0:T(8,128)S(1)} %bitcast.24), channel_id=1, source_target_pairs={{0,256},{1,257},{2,258},{3,259},{4,260},{5,261},{6,262},{7,263},{8... | collective-permute-start | bytes 196616 | tf_op jit(solution)/shard_map/ppermute | solution.py:436
  33.1 2.6 %collective-permute-start.1 = (f32[4,16,256]{2,1,0:T(8,128)S(1)}, f32[4,16,256]{2,1,0:T(8,128)S(1)}, u32[]{:S(2)}, u32[]{:S(2)}) collective-permute-start(f32[4,16,256]{2,1,0:T(8,128)S(1)} %broadcast_select_fusion.3), channel_id=1, source_target_pairs={{0,128},{256,384},{1,129},{257,385},{2,130},{258,386},{3,131},{259... | collective-permute-start | bytes 196616 | tf_op jit(solution)/shard_map/ppermute | solution.py:436
  35.8 6.6 %collective-permute-start.2 = (f32[4,16,256]{2,1,0:T(8,128)S(1)}, f32[4,16,256]{2,1,0:T(8,128)S(1)}, u32[]{:S(2)}, u32[]{:S(2)}) collective-permute-start(f32[4,16,256]{2,1,0:T(8,128)S(1)} %broadcast_select_fusion.4), channel_id=1, source_target_pairs={{0,64},{128,192},{256,320},{384,448},{1,65},{129,193},{257,321},{3... | collective-permute-start | bytes 196616 | tf_op jit(solution)/shard_map/ppermute | solution.py:436
  45.0 35.1 %all-to-all-start.1 = ((f32[16,4,16,256]{3,2,1,0:T(8,128)}), f32[16,4,16,256]{3,2,1,0:T(8,128)S(1)}, u32[]{:S(2)}, u32[]{:S(2)}) async-start(f32[16,4,16,256]{3,2,1,0:T(8,128)} %get-tuple-element.16.top_ref), calls=%async_computation.1 | async-start | bytes 2097152 | tf_op jit(solution)/shard_map/all_to_all | solution.py:425
  54.1 16.1 %collective-permute-start.6 = (f32[28,16,256]{2,1,0:T(8,128)S(1)}, f32[28,16,256]{2,1,0:T(8,128)S(1)}, u32[]{:S(2)}, u32[]{:S(2)}) collective-permute-start(f32[28,16,256]{2,1,0:T(8,128)S(1)} %bitcast.22), channel_id=1, source_target_pairs={{0,256},{1,257},{2,258},{3,259},{4,260},{5,261},{6,262},{7,263},{8... | collective-permute-start | bytes 1376264 | tf_op jit(solution)/shard_map/ppermute | solution.py:436
  70.2 13.1 %collective-permute-start.7 = (f32[28,16,256]{2,1,0:T(8,128)S(1)}, f32[28,16,256]{2,1,0:T(8,128)}, u32[]{:S(2)}, u32[]{:S(2)}) collective-permute-start(f32[28,16,256]{2,1,0:T(8,128)S(1)} %broadcast_select_fusion), channel_id=1, source_target_pairs={{0,128},{256,384},{1,129},{257,385},{2,130},{258,386},{3,131},{259... | collective-permute-start | bytes 1376264 | tf_op jit(solution)/shard_map/ppermute | solution.py:436
  80.9 10.8 %collective-permute-start.4 = (f32[512,256]{1,0:T(8,128)}, f32[512,256]{1,0:T(8,128)}, u32[]{:S(2)}, u32[]{:S(2)}) collective-permute-start(f32[512,256]{1,0:T(8,128)} %bitcast.6.own.refs_0_), channel_id=1, source_target_pairs={{0,32},{16,48},{32,0},{48,16},{1,33},{17,49},{33,1},{49,17},{2,34}... | collective-permute-start | bytes 1572872 | tf_op jit(solution)/shard_map/ppermute | solution.py:415
  83.4 15.9 %collective-permute-start.8 = (f32[28,16,256]{2,1,0:T(8,128)S(1)}, f32[28,16,256]{2,1,0:T(8,128)S(1)}, u32[]{:S(2)}, u32[]{:S(2)}) collective-permute-start(f32[28,16,256]{2,1,0:T(8,128)S(1)} %broadcast_select_fusion.1), channel_id=1, source_target_pairs={{0,64},{128,192},{256,320},{384,448},{1,65},{129,193},{257,321},{3... | collective-permute-start | bytes 1376264 | tf_op jit(solution)/shard_map/ppermute | solution.py:436
  84.7 31.0 %collective-permute-start.3 = (f32[512,256]{1,0:T(8,128)}, f32[512,256]{1,0:T(8,128)}, u32[]{:S(2)}, u32[]{:S(2)}) collective-permute-start(f32[512,256]{1,0:T(8,128)} %bitcast.6.own.refs_0_), channel_id=1, source_target_pairs={{0,16},{16,0},{32,48},{48,32},{1,17},{17,1},{33,49},{49,33},{2,18}... | collective-permute-start | bytes 1572872 | tf_op jit(solution)/shard_map/ppermute | solution.py:415
  91.7 24.1 %collective-permute-start.5 = (f32[512,256]{1,0:T(8,128)}, f32[512,256]{1,0:T(8,128)}, u32[]{:S(2)}, u32[]{:S(2)}) collective-permute-start(f32[512,256]{1,0:T(8,128)} %collective-permute-done.4.across.refs_2_), channel_id=1, source_target_pairs={{0,16},{16,0},{32,48},{48,32},{1,17},{17,1},{33,49},{49,33},{2,18}... | collective-permute-start | bytes 1572872 | tf_op jit(solution)/shard_map/ppermute | solution.py:415
  101.7 38.3 %collective-permute-start.10 = (f32[1024,256]{1,0:T(8,128)S(1)}, f32[1024,256]{1,0:T(8,128)}, u32[]{:S(2)}, u32[]{:S(2)}) collective-permute-start(f32[1024,256]{1,0:T(8,128)S(1)} %bitcast.16), channel_id=1, source_target_pairs={{0,32},{16,48},{32,0},{48,16},{1,33},{17,49},{33,1},{49,17},{2,34}... | collective-permute-start | bytes 3145736 | tf_op jit(solution)/shard_map/ppermute | solution.py:415
  104.1 49.0 %collective-permute-start.9 = (f32[1024,256]{1,0:T(8,128)S(1)}, f32[1024,256]{1,0:T(8,128)}, u32[]{:S(2)}, u32[]{:S(2)}) collective-permute-start(f32[1024,256]{1,0:T(8,128)S(1)} %bitcast.17), channel_id=1, source_target_pairs={{0,16},{16,0},{32,48},{48,32},{1,17},{17,1},{33,49},{49,33},{2,18}... | collective-permute-start | bytes 3145736 | tf_op jit(solution)/shard_map/ppermute | solution.py:415
  106.3 33.6 %all-to-all-start.2 = ((f32[32,2,16,128]{3,2,1,0:T(8,128)}), f32[32,2,16,128]{3,2,1,0:T(8,128)S(1)}, u32[]{:S(2)}, u32[]{:S(2)}) async-start(f32[32,2,16,128]{3,2,1,0:T(8,128)} %bitcast.21), calls=%async_computation.2 | async-start | bytes 1048576 | tf_op jit(solution)/shard_map/all_to_all | solution.py:425
  140.0 13.1 %collective-permute-start.11 = (f32[1024,256]{1,0:T(8,128)}, f32[1024,256]{1,0:T(8,128)}, u32[]{:S(2)}, u32[]{:S(2)}) collective-permute-start(f32[1024,256]{1,0:T(8,128)} %collective-permute-done.10.refs_6_.row2), channel_id=1, source_target_pairs={{0,16},{16,0},{32,48},{48,32},{1,17},{17,1},{33,49},{49,33},{2,18}... | collective-permute-start | bytes 3145736 | tf_op jit(solution)/shard_map/ppermute | solution.py:415
  143.5 1.0 copy-start.9
  145.4 36.5 %copy-start.13 = (f32[32,16,256]{2,1,0:T(8,128)S(1)}, f32[32,16,256]{2,1,0:T(8,128)}, u32[]{:S(2)}) copy-start(f32[32,16,256]{2,1,0:T(8,128)} %copy-done.12) | copy-start | bytes 1572868
  145.4 36.5 %all-to-all-start.3 = ((f32[16,4,16,256]{3,2,1,0:T(8,128)}), f32[16,4,16,256]{3,2,1,0:T(8,128)S(1)}, u32[]{:S(2)}, u32[]{:S(2)}) async-start(f32[16,4,16,256]{3,2,1,0:T(8,128)} %copy-done.9), calls=%async_computation.3 | async-start | bytes 2097152 | tf_op jit(solution)/shard_map/all_to_all | solution.py:425
  153.1 1.2 copy-start.3
  181.9 1.2 copy-start.4
  183.1 1.2 copy-start.6
  184.3 1.2 copy-start.8
  (7 other events, 6.2 us)

commit v6 on v5

--- a/solution.py
+++ b/solution.py
@@ -60,30 +60,32 @@
     lax.fori_loop(0, child_ref.shape[1] // TILE, body, 0)
 
 
-def spread_low_kernel(where_ref, map_ref, child_ref, out_ref):
+def spread_low_kernel(where_ref, map_ref, child_ref, out_ref, from_ref):
     child = where_ref[0]
+    part = TILE // BLK
     count = 2 * ROWS
-    out_ref[0] = jnp.zeros_like(out_ref[0])
     lane_block = lax.broadcasted_iota(jnp.int32, (BLK, TILE), 1) // BLK
 
-    def body(tile, carry):
-        for part in range(TILE // BLK):
-            block = map_ref[child, tile * (TILE // BLK) + part]
-            target = block // (TILE // BLK)
-
-            @pl.when(target < count)
-            def _():
-                place = block % (TILE // BLK)
-                rows = child_ref[:, pl.ds(pl.multiple_of(tile * TILE, TILE), TILE)]
-                shift = (place - part + TILE // BLK) % (TILE // BLK) * BLK
-                moved = pltpu.roll(rows, shift, 1)
-                out_ref[0, target] = jnp.where(lane_block == place, moved, out_ref[0, target])
-
+    def clear(block, carry):
+        from_ref[block] = -1
         return carry
 
-    lax.fori_loop(0, child_ref.shape[1] // TILE, body, 0)
-    for sub in range(1, SUBS):
-        out_ref[sub] = out_ref[0]
+    def note(block, carry):
+        from_ref[map_ref[child, block]] = block
+        return carry
+
+    lax.fori_loop(0, count * part, clear, 0, unroll=8)
+    lax.fori_loop(0, map_ref.shape[1], note, 0, unroll=8)
+    for target in range(count):
+        tile = jnp.zeros((BLK, TILE), jnp.float32)
+        for place in range(part):
+            block = from_ref[target * part + place]
+            source = jnp.maximum(block, 0)
+            rows = child_ref[:, pl.ds(pl.multiple_of(source // part * TILE, TILE), TILE)]
+            moved = pltpu.roll(rows, (place - source % part + part) % part * BLK, 1)
+            tile = jnp.where((lane_block == place) & (block >= 0), moved, tile)
+        for sub in range(SUBS):
+            out_ref[sub, target] = tile
 
 
 def each_source(where_ref, map_ref, use):
@@ -285,7 +287,7 @@
             pltpu.VMEM((TILE, TILE), jnp.float32),
             pltpu.SemaphoreType.DMA((4,)),
         ],
-        compiler_params=params(10),
+        compiler_params=params(60),
         cost_estimate=pl.CostEstimate(flops=60_000_000_000, bytes_accessed=4 << 20, transcendentals=0),
         name="first_factor",
     )(where, *pieces)
@@ -334,7 +336,7 @@
             pltpu.VMEM((TILE, TILE), jnp.float32),
             pltpu.SemaphoreType.DMA((11,)),
         ],
-        compiler_params=params(20),
+        compiler_params=params(60),
         cost_estimate=pl.CostEstimate(flops=60_000_000_000, bytes_accessed=8 << 20, transcendentals=0),
         name="second_factor",
     )(where, inv, *upper, *lower)
@@ -406,7 +408,7 @@
             pltpu.VMEM((SHARDS, BLK, WIDE), jnp.float32),
             pltpu.SemaphoreType.DMA((10,)),
         ],
-        compiler_params=params(28),
+        compiler_params=params(60),
         name="finish",
     )(where, inv0, inv1, x01, cols, *rows, front)
 
@@ -430,10 +432,12 @@
     return x, swap(x, "row", 1), across, swap(across, "row", 1)
 
 
-def from_first(x, sub):
+def from_first(x, sub, beside=None):
     for step in (4, 2, 1):
         pairs = [(i, i + step) for i in range(0, SUBS, 2 * step)]
         got = lax.ppermute(x, "sub", pairs)
+        if beside is not None and step == 4:
+            got, _ = lax.optimization_barrier((got, beside))
         x = jnp.where(sub % (2 * step) == step, got, x)
     return x
 
@@ -444,13 +448,13 @@
     where = jnp.stack([shard // (SHARDS // 2), col, row, shard]).astype(jnp.int32)
     parent = parent_front.reshape(SHARDS, BLK, WIDE)
     parent_top = from_first(parent[:TOP], sub)
-    parent_rest = from_first(parent[TOP:], sub)
 
     low = call(
         spread_low_kernel,
         jax.ShapeDtypeStruct((SUBS, 2 * ROWS, BLK, TILE), jnp.float32),
         (where, index_map, child_schur),
         4,
+        [pltpu.SMEM((2 * SHARDS * TILE // BLK,), jnp.int32)],
     )
     low = exchange(low.reshape(SHARDS, 2, BLK, TILE), ("sub", "row"))
     tops, _ = call(
@@ -459,14 +463,15 @@
         (where, index_map, low, parent_top),
         6,
     )
+    tops, child_late = lax.optimization_barrier((tops, child_schur))
+    pivots = exchange(tops, "col")
     spread = call(
         spread_kernel,
         jax.ShapeDtypeStruct((2 * SHARDS, BLK, TILE), jnp.float32),
-        (where, index_map, child_schur),
+        (where, index_map, child_late),
         4,
     )
-    tops, spread = lax.optimization_barrier((tops, spread))
-    pivots = exchange(tops, "col")
+    parent_rest = from_first(parent[TOP:], sub, spread)
     tail = call(
         place_rest_kernel,
         jax.ShapeDtypeStruct((2 * SHARDS, BLK, WIDE), jnp.float32),

time: 197 us -> 188 us (0.954)
  local copies, waits for them, and re-layouts: 12.9 us -> 5.16 us
  waiting for transfers between devices: 21.8 us -> 17.8 us
    unnamed x30 -> x20, local copies, waits for them, and re-layouts: 12 us -> 4.28 us
    ppermute x6, waiting for transfers between devices: 13.5 us -> 9.14 us  [from_first(): got = lax.ppermute(x, 'sub', pairs)]
    pallas_call x5, Pallas kernels: 17 us -> 14.6 us  [call(): pl.pallas_call(kernel, out_shape=out_shape, in_specs=[SMEM, SMEM] + [VMEM...]
    ppermute x6, starting transfers between devices: 21.5 us -> 23.7 us  [from_first(): got = lax.ppermute(x, 'sub', pairs)]
  transfers between devices with their start and end apart: 16 -> 16, of which waited for: 5 -> 6; matrix products, arithmetic and copies ran while one was open for 1% -> 1% of each run, Pallas kernels for 29% -> 33%
where the time goes in v6:
time: 188 us; the launch traced here: 184 us
  starting transfers between devices  84.1 us (45%)
  Pallas kernels  76.3 us (41%)
  waiting for transfers between devices  17.8 us (9%)
  local copies, waits for them, and re-layouts  5.16 us (3%)
    all_to_all x4, starting transfers between devices, exchange(): return lax.all_to_all(x, axis, split_axis=0, concat_axis=0, tiled=True)  38.8 us
    pallas_call x1, Pallas kernels, second_factor(): pl.pallas_call(second_kernel, out_shape=(shape, shape), in_specs=[SMEM] +...  26.7 us
    pallas_call x1, Pallas kernels, first_factor(): pl.pallas_call(first_kernel, out_shape=jax.ShapeDtypeStruct((PANEL, PANEL...  24.3 us
    ppermute x6, starting transfers between devices, from_first(): got = lax.ppermute(x, 'sub', pairs)  23.7 us
    ppermute x6, starting transfers between devices, swap(): return lax.ppermute(x, axis, [(i, i ^ bit) for i in range(ROWS)])  21.7 us
    pallas_call x5, Pallas kernels, call(): pl.pallas_call(kernel, out_shape=out_shape, in_specs=[SMEM, SMEM] + [VMEM...  14.6 us
    pallas_call x1, Pallas kernels, finish(): pl.pallas_call(finish_kernel, out_shape=FRONT, in_specs=[SMEM] + [HBM] *...  10.7 us
    ppermute x6, waiting for transfers between devices, from_first(): got = lax.ppermute(x, 'sub', pairs)  9.14 us
  transfers between devices with their start and end apart: 16, of which 6 were waited for; matrix products, arithmetic and copies ran while one was open for 1% of the time, Pallas kernels for 33%

profile of v6, /device:TPU:1, one launch (start us, length us, event | category | flops | bytes accessed | tf_op | source)
XLA Modules:
  0.0 184.2 jit_solution(17180058560849970328)
XLA Ops:
  1.6 2.8 %spread_low.1 = f32[8,8,16,128]{3,2,1,0:T(8,128)} custom-call(s32[4]{0:T(128)S(1)} %pad_add_fusion.where_ref, s32[2,256]{1,0:T(2,128)S(1)} %copy-done.6, f32[16,4096]{1,0:T(8,128)S(1)} %copy-done.3), custom_call_target="tpu_custom_call" | custom-call | tf_op jit(solution)/shard_map/spread_low/pallas_call | solution.py:148
  4.4 13.0 %all-to-all-start = ((f32[32,2,16,128]{3,2,1,0:T(8,128)}), f32[32,2,16,128]{3,2,1,0:T(8,128)S(1)}, u32[]{:S(2)}, u32[]{:S(2)}) async-start(f32[32,2,16,128]{3,2,1,0:T(8,128)} %bitcast.4), calls=%async_computation | async-start | bytes 1048576 | tf_op jit(solution)/shard_map/all_to_all | solution.py:427
  17.5 7.2 %collective-permute-start = (f32[4,16,256]{2,1,0:T(8,128)S(1)}, f32[4,16,256]{2,1,0:T(8,128)S(1)}, u32[]{:S(2)}, u32[]{:S(2)}) collective-permute-start(f32[4,16,256]{2,1,0:T(8,128)S(1)} %bitcast.24), channel_id=1, source_target_pairs={{0,256},{1,257},{2,258},{3,259},{4,260},{5,261},{6,262},{7,263},{8... | collective-permute-start | bytes 196616 | tf_op jit(solution)/shard_map/ppermute | solution.py:438
  24.7 4.5 %collective-permute-done = f32[4,16,256]{2,1,0:T(8,128)S(1)} collective-permute-done((f32[4,16,256]{2,1,0:T(8,128)S(1)}, f32[4,16,256]{2,1,0:T(8,128)S(1)}, u32[]{:S(2)}, u32[]{:S(2)}) %collective-permute-start) | collective-permute-done | bytes 65568 | tf_op jit(solution)/shard_map/ppermute | solution.py:438
  34.5 2.6 %place_top.1 = (f32[16,4,16,256]{3,2,1,0:T(8,128)}, f32[4,16,256]{2,1,0:T(8,128)}) custom-call(s32[4]{0:T(128)S(1)} %pad_add_fusion.where_ref, s32[2,256]{1,0:T(2,128)S(1)} %copy-done.6, f32[32,2,16,128]{3,2,1,0:T(8,128)S(1)} %all-to-all-done.received_ref, f32[4,16,256]{2,1,0:T(8,128)S(1)} %broadcast_select_fusion.5.parent_ref), custom_call_target="tpu_custom_call" | custom-call | tf_op jit(solution)/shard_map/place_top/pallas_call | solution.py:148
  37.1 9.1 %all-to-all-start.1 = ((f32[16,4,16,256]{3,2,1,0:T(8,128)}), f32[16,4,16,256]{3,2,1,0:T(8,128)S(1)}, u32[]{:S(2)}, u32[]{:S(2)}) async-start(f32[16,4,16,256]{3,2,1,0:T(8,128)} %get-tuple-element.17.top_ref), calls=%async_computation.1 | async-start | bytes 2097152 | tf_op jit(solution)/shard_map/all_to_all | solution.py:427
  46.3 8.3 %collective-permute-start.6 = (f32[28,16,256]{2,1,0:T(8,128)S(1)}, f32[28,16,256]{2,1,0:T(8,128)S(1)}, u32[]{:S(2)}, u32[]{:S(2)}) collective-permute-start(f32[28,16,256]{2,1,0:T(8,128)S(1)} %bitcast.22), channel_id=1, source_target_pairs={{0,256},{1,257},{2,258},{3,259},{4,260},{5,261},{6,262},{7,263},{8... | collective-permute-start | bytes 1376264 | tf_op jit(solution)/shard_map/ppermute | solution.py:438
  54.6 4.4 %spread.1 = f32[64,16,128]{2,1,0:T(8,128)S(1)} custom-call(s32[4]{0:T(128)S(1)} %pad_add_fusion.where_ref, s32[2,256]{1,0:T(2,128)S(1)} %copy-done.6, f32[16,4096]{1,0:T(8,128)S(1)} %copy-done.4), custom_call_target="tpu_custom_call" | custom-call | tf_op jit(solution)/shard_map/spread/pallas_call | solution.py:148
  62.0 2.1 %collective-permute-start.7 = (f32[28,16,256]{2,1,0:T(8,128)S(1)}, f32[28,16,256]{2,1,0:T(8,128)}, u32[]{:S(2)}, u32[]{:S(2)}) collective-permute-start(f32[28,16,256]{2,1,0:T(8,128)S(1)} %broadcast_select_fusion), channel_id=1, source_target_pairs={{0,128},{256,384},{1,129},{257,385},{2,130},{258,386},{3,131},{259... | collective-permute-start | bytes 1376264 | tf_op jit(solution)/shard_map/ppermute | solution.py:438
  64.0 8.1 %all-to-all-done.1.pivots_ref = f32[16,4,16,256]{3,2,1,0:T(8,128)S(1)} async-done(((f32[16,4,16,256]{3,2,1,0:T(8,128)}), f32[16,4,16,256]{3,2,1,0:T(8,128)S(1)}, u32[]{:S(2)}, u32[]{:S(2)}) %all-to-all-start.1) | async-done | bytes 1048608 | tf_op jit(solution)/shard_map/all_to_all | solution.py:427
  73.0 2.5 %collective-permute-start.4 = (f32[512,256]{1,0:T(8,128)}, f32[512,256]{1,0:T(8,128)}, u32[]{:S(2)}, u32[]{:S(2)}) collective-permute-start(f32[512,256]{1,0:T(8,128)} %bitcast.6.own.refs_0_), channel_id=1, source_target_pairs={{0,32},{16,48},{32,0},{48,16},{1,33},{17,49},{33,1},{49,17},{2,34}... | collective-permute-start | bytes 1572872 | tf_op jit(solution)/shard_map/ppermute | solution.py:417
  75.6 3.5 %collective-permute-start.8 = (f32[28,16,256]{2,1,0:T(8,128)S(1)}, f32[28,16,256]{2,1,0:T(8,128)S(1)}, u32[]{:S(2)}, u32[]{:S(2)}) collective-permute-start(f32[28,16,256]{2,1,0:T(8,128)S(1)} %broadcast_select_fusion.1), channel_id=1, source_target_pairs={{0,64},{128,192},{256,320},{384,448},{1,65},{129,193},{257,321},{3... | collective-permute-start | bytes 1376264 | tf_op jit(solution)/shard_map/ppermute | solution.py:438
  79.1 7.4 %collective-permute-start.3 = (f32[512,256]{1,0:T(8,128)}, f32[512,256]{1,0:T(8,128)}, u32[]{:S(2)}, u32[]{:S(2)}) collective-permute-start(f32[512,256]{1,0:T(8,128)} %bitcast.6.own.refs_0_), channel_id=1, source_target_pairs={{0,16},{16,0},{32,48},{48,32},{1,17},{17,1},{33,49},{49,33},{2,18}... | collective-permute-start | bytes 1572872 | tf_op jit(solution)/shard_map/ppermute | solution.py:417
  86.5 4.9 %collective-permute-start.5 = (f32[512,256]{1,0:T(8,128)}, f32[512,256]{1,0:T(8,128)}, u32[]{:S(2)}, u32[]{:S(2)}) collective-permute-start(f32[512,256]{1,0:T(8,128)} %collective-permute-done.4.across.refs_2_), channel_id=1, source_target_pairs={{0,16},{16,0},{32,48},{48,32},{1,17},{17,1},{33,49},{49,33},{2,18}... | collective-permute-start | bytes 1572872 | tf_op jit(solution)/shard_map/ppermute | solution.py:417
  91.5 2.3 %place_rest.1 = f32[64,16,256]{2,1,0:T(8,128)S(1)} custom-call(s32[4]{0:T(128)S(1)} %pad_add_fusion.where_ref, s32[2,256]{1,0:T(2,128)S(1)} %copy-done.6, f32[32,2,16,128]{3,2,1,0:T(8,128)S(1)} %all-to-all-done.received_ref, f32[28,16,256]{2,1,0:T(8,128)S(1)} %broadcast_select_fusion.2.parent_ref, f32[16,4,16,256]{3,2,1,0:T(8,128)} %get-tuple-element.17.top_ref, ...), custom_call_target="tpu_custom_call" | custom-call | tf_op jit(solution)/shard_map/place_rest/pallas_call | solution.py:148
  93.8 2.5 %collective-permute-start.10 = (f32[1024,256]{1,0:T(8,128)S(1)}, f32[1024,256]{1,0:T(8,128)}, u32[]{:S(2)}, u32[]{:S(2)}) collective-permute-start(f32[1024,256]{1,0:T(8,128)S(1)} %bitcast.15), channel_id=1, source_target_pairs={{0,32},{16,48},{32,0},{48,16},{1,33},{17,49},{33,1},{49,17},{2,34}... | collective-permute-start | bytes 3145736 | tf_op jit(solution)/shard_map/ppermute | solution.py:417
  96.4 2.2 %collective-permute-start.9 = (f32[1024,256]{1,0:T(8,128)S(1)}, f32[1024,256]{1,0:T(8,128)}, u32[]{:S(2)}, u32[]{:S(2)}) collective-permute-start(f32[1024,256]{1,0:T(8,128)S(1)} %bitcast.16), channel_id=1, source_target_pairs={{0,16},{16,0},{32,48},{48,32},{1,17},{17,1},{33,49},{49,33},{2,18}... | collective-permute-start | bytes 3145736 | tf_op jit(solution)/shard_map/ppermute | solution.py:417
  98.6 10.0 %all-to-all-start.2 = ((f32[32,2,16,128]{3,2,1,0:T(8,128)}), f32[32,2,16,128]{3,2,1,0:T(8,128)S(1)}, u32[]{:S(2)}, u32[]{:S(2)}) async-start(f32[32,2,16,128]{3,2,1,0:T(8,128)} %bitcast.20), calls=%async_computation.2 | async-start | bytes 1048576 | tf_op jit(solution)/shard_map/all_to_all | solution.py:427
  108.6 24.3 %first_factor.1.inv_hbm.inv0_hbm = f32[512,512]{1,0:T(8,128)} custom-call(s32[4]{0:T(128)} %copy-done.7, f32[512,256]{1,0:T(8,128)} %bitcast.6.own.refs_0_, f32[512,256]{1,0:T(8,128)} %collective-permute-done.3.core.refs_1_, f32[512,256]{1,0:T(8,128)} %collective-permute-done.4.across.refs_2_, f32[512,256]{1,0:T(8,128)} %collective-permute-done.5.both.refs_3_), custom_call_target="tpu_custom_call" | custom-call | flops 60000002048 | bytes 4194304 | tf_op jit(solution)/shard_map/first_factor/pallas_call | solution.py:280
  133.0 2.1 %collective-permute-start.11 = (f32[1024,256]{1,0:T(8,128)}, f32[1024,256]{1,0:T(8,128)}, u32[]{:S(2)}, u32[]{:S(2)}) collective-permute-start(f32[1024,256]{1,0:T(8,128)} %collective-permute-done.10.refs_6_.row2), channel_id=1, source_target_pairs={{0,16},{16,0},{32,48},{48,32},{1,17},{17,1},{33,49},{49,33},{2,18}... | collective-permute-start | bytes 3145736 | tf_op jit(solution)/shard_map/ppermute | solution.py:417
  135.1 2.5 %place.1 = (f32[32,16,256]{2,1,0:T(8,128)S(1)}, f32[16,4,16,256]{3,2,1,0:T(8,128)}) custom-call(s32[4]{0:T(128)S(1)} %copy-done.8, s32[2,256]{1,0:T(2,128)S(1)} %copy-done.6, f32[32,2,16,128]{3,2,1,0:T(8,128)S(1)} %all-to-all-done.2.received_ref, f32[32,16,256]{2,1,0:T(8,128)S(1)} %bitcast.19), custom_call_target="tpu_custom_call" | custom-call | tf_op jit(solution)/shard_map/place/pallas_call | solution.py:148
  138.4 6.6 %all-to-all-start.3 = ((f32[16,4,16,256]{3,2,1,0:T(8,128)}), f32[16,4,16,256]{3,2,1,0:T(8,128)S(1)}, u32[]{:S(2)}, u32[]{:S(2)}) async-start(f32[16,4,16,256]{3,2,1,0:T(8,128)} %get-tuple-element.25), calls=%async_computation.3 | async-start | bytes 2097152 | tf_op jit(solution)/shard_map/all_to_all | solution.py:427
  145.1 26.7 %second_factor.1 = (f32[512,512]{1,0:T(8,128)}, f32[512,512]{1,0:T(8,128)}) custom-call(s32[4]{0:T(128)} %copy-done.7, f32[512,512]{1,0:T(8,128)} %first_factor.1.inv_hbm.inv0_hbm, f32[512,256]{1,0:T(8,128)} %bitcast.6.own.refs_0_, f32[512,256]{1,0:T(8,128)} %collective-permute-done.3.core.refs_1_, f32[512,256]{1,0:T(8,128)} %collective-permute-done.4.across.refs_2_, ...), custom_call_target="tpu_custom_call" | custom-call | flops 60000002048 | bytes 8388608 | tf_op jit(solution)/shard_map/second_factor/pallas_call | solution.py:329
  173.4 10.7 %finish.1 = f32[32,16,256]{2,1,0:T(8,128)} custom-call(s32[4]{0:T(128)} %copy-done.7, f32[512,512]{1,0:T(8,128)} %first_factor.1.inv_hbm.inv0_hbm, f32[512,512]{1,0:T(8,128)} %get-tuple-element.22.inv1_hbm, f32[512,512]{1,0:T(8,128)} %get-tuple-element.23.x01_hbm, f32[16,64,256]{2,1,0:T(8,128)} %bitcast.21, f32[1024,256]{1,0:T(8,128)} %bitcast.18, ...), custom_call_target="tpu_custom_call" | custom-call | tf_op jit(solution)/shard_map/finish/pallas_call | solution.py:398
  (46 shorter events, 13.3 us)
Async XLA Ops:
  0.7 0.9 copy-start.3
  1.6 89.9 %copy-start.7 = (s32[4]{0:T(128)}, s32[4]{0:T(128)S(1)}, u32[]{:S(2)}) copy-start(s32[4]{0:T(128)S(1)} %pad_add_fusion.where_ref) | copy-start | bytes 52
  4.4 13.0 %copy-start.1 = (f32[16,1,32,256]{3,2,1,0:T(8,128)S(1)}, f32[16,1,32,256]{3,2,1,0:T(8,128)}, u32[]{:S(2)}) copy-start(f32[16,1,32,256]{3,2,1,0:T(8,128)} %param.3) | copy-start | bytes 1572868
  4.4 30.1 %all-to-all-start = ((f32[32,2,16,128]{3,2,1,0:T(8,128)}), f32[32,2,16,128]{3,2,1,0:T(8,128)S(1)}, u32[]{:S(2)}, u32[]{:S(2)}) async-start(f32[32,2,16,128]{3,2,1,0:T(8,128)} %bitcast.4), calls=%async_computation | async-start | bytes 1048576 | tf_op jit(solution)/shard_map/all_to_all | solution.py:427
  17.5 11.7 %collective-permute-start = (f32[4,16,256]{2,1,0:T(8,128)S(1)}, f32[4,16,256]{2,1,0:T(8,128)S(1)}, u32[]{:S(2)}, u32[]{:S(2)}) collective-permute-start(f32[4,16,256]{2,1,0:T(8,128)S(1)} %bitcast.24), channel_id=1, source_target_pairs={{0,256},{1,257},{2,258},{3,259},{4,260},{5,261},{6,262},{7,263},{8... | collective-permute-start | bytes 196616 | tf_op jit(solution)/shard_map/ppermute | solution.py:438
  29.3 2.6 %collective-permute-start.1 = (f32[4,16,256]{2,1,0:T(8,128)S(1)}, f32[4,16,256]{2,1,0:T(8,128)S(1)}, u32[]{:S(2)}, u32[]{:S(2)}) collective-permute-start(f32[4,16,256]{2,1,0:T(8,128)S(1)} %broadcast_select_fusion.3), channel_id=1, source_target_pairs={{0,128},{256,384},{1,129},{257,385},{2,130},{258,386},{3,131},{259... | collective-permute-start | bytes 196616 | tf_op jit(solution)/shard_map/ppermute | solution.py:438
  31.9 2.6 %collective-permute-start.2 = (f32[4,16,256]{2,1,0:T(8,128)S(1)}, f32[4,16,256]{2,1,0:T(8,128)S(1)}, u32[]{:S(2)}, u32[]{:S(2)}) collective-permute-start(f32[4,16,256]{2,1,0:T(8,128)S(1)} %broadcast_select_fusion.4), channel_id=1, source_target_pairs={{0,64},{128,192},{256,320},{384,448},{1,65},{129,193},{257,321},{3... | collective-permute-start | bytes 196616 | tf_op jit(solution)/shard_map/ppermute | solution.py:438
  37.1 35.0 %all-to-all-start.1 = ((f32[16,4,16,256]{3,2,1,0:T(8,128)}), f32[16,4,16,256]{3,2,1,0:T(8,128)S(1)}, u32[]{:S(2)}, u32[]{:S(2)}) async-start(f32[16,4,16,256]{3,2,1,0:T(8,128)} %get-tuple-element.17.top_ref), calls=%async_computation.1 | async-start | bytes 2097152 | tf_op jit(solution)/shard_map/all_to_all | solution.py:427
  46.2 8.4 %copy-start.4 = (f32[16,4096]{1,0:T(8,128)S(1)}, f32[16,4096]{1,0:T(8,128)}, u32[]{:S(2)}) copy-start(f32[16,4096]{1,0:T(8,128)} %child_ref.2) | copy-start | bytes 786436
  46.3 15.6 %collective-permute-start.6 = (f32[28,16,256]{2,1,0:T(8,128)S(1)}, f32[28,16,256]{2,1,0:T(8,128)S(1)}, u32[]{:S(2)}, u32[]{:S(2)}) collective-permute-start(f32[28,16,256]{2,1,0:T(8,128)S(1)} %bitcast.22), channel_id=1, source_target_pairs={{0,256},{1,257},{2,258},{3,259},{4,260},{5,261},{6,262},{7,263},{8... | collective-permute-start | bytes 1376264 | tf_op jit(solution)/shard_map/ppermute | solution.py:438
  62.0 13.5 %collective-permute-start.7 = (f32[28,16,256]{2,1,0:T(8,128)S(1)}, f32[28,16,256]{2,1,0:T(8,128)}, u32[]{:S(2)}, u32[]{:S(2)}) collective-permute-start(f32[28,16,256]{2,1,0:T(8,128)S(1)} %broadcast_select_fusion), channel_id=1, source_target_pairs={{0,128},{256,384},{1,129},{257,385},{2,130},{258,386},{3,131},{259... | collective-permute-start | bytes 1376264 | tf_op jit(solution)/shard_map/ppermute | solution.py:438
  73.0 13.5 %collective-permute-start.4 = (f32[512,256]{1,0:T(8,128)}, f32[512,256]{1,0:T(8,128)}, u32[]{:S(2)}, u32[]{:S(2)}) collective-permute-start(f32[512,256]{1,0:T(8,128)} %bitcast.6.own.refs_0_), channel_id=1, source_target_pairs={{0,32},{16,48},{32,0},{48,16},{1,33},{17,49},{33,1},{49,17},{2,34}... | collective-permute-start | bytes 1572872 | tf_op jit(solution)/shard_map/ppermute | solution.py:417
  75.6 15.8 %collective-permute-start.8 = (f32[28,16,256]{2,1,0:T(8,128)S(1)}, f32[28,16,256]{2,1,0:T(8,128)S(1)}, u32[]{:S(2)}, u32[]{:S(2)}) collective-permute-start(f32[28,16,256]{2,1,0:T(8,128)S(1)} %broadcast_select_fusion.1), channel_id=1, source_target_pairs={{0,64},{128,192},{256,320},{384,448},{1,65},{129,193},{257,321},{3... | collective-permute-start | bytes 1376264 | tf_op jit(solution)/shard_map/ppermute | solution.py:438
  79.1 29.5 %collective-permute-start.3 = (f32[512,256]{1,0:T(8,128)}, f32[512,256]{1,0:T(8,128)}, u32[]{:S(2)}, u32[]{:S(2)}) collective-permute-start(f32[512,256]{1,0:T(8,128)} %bitcast.6.own.refs_0_), channel_id=1, source_target_pairs={{0,16},{16,0},{32,48},{48,32},{1,17},{17,1},{33,49},{49,33},{2,18}... | collective-permute-start | bytes 1572872 | tf_op jit(solution)/shard_map/ppermute | solution.py:417
  86.5 22.1 %collective-permute-start.5 = (f32[512,256]{1,0:T(8,128)}, f32[512,256]{1,0:T(8,128)}, u32[]{:S(2)}, u32[]{:S(2)}) collective-permute-start(f32[512,256]{1,0:T(8,128)} %collective-permute-done.4.across.refs_2_), channel_id=1, source_target_pairs={{0,16},{16,0},{32,48},{48,32},{1,17},{17,1},{33,49},{49,33},{2,18}... | collective-permute-start | bytes 1572872 | tf_op jit(solution)/shard_map/ppermute | solution.py:417
  93.8 39.1 %copy-start = (f32[64,16,256]{2,1,0:T(8,128)}, f32[64,16,256]{2,1,0:T(8,128)S(1)}, u32[]{:S(2)}) copy-start(f32[64,16,256]{2,1,0:T(8,128)S(1)} %place_rest.1) | copy-start | bytes 3145732
  93.8 39.2 %collective-permute-start.10 = (f32[1024,256]{1,0:T(8,128)S(1)}, f32[1024,256]{1,0:T(8,128)}, u32[]{:S(2)}, u32[]{:S(2)}) collective-permute-start(f32[1024,256]{1,0:T(8,128)S(1)} %bitcast.15), channel_id=1, source_target_pairs={{0,32},{16,48},{32,0},{48,16},{1,33},{17,49},{33,1},{49,17},{2,34}... | collective-permute-start | bytes 3145736 | tf_op jit(solution)/shard_map/ppermute | solution.py:417
  96.4 48.7 %collective-permute-start.9 = (f32[1024,256]{1,0:T(8,128)S(1)}, f32[1024,256]{1,0:T(8,128)}, u32[]{:S(2)}, u32[]{:S(2)}) collective-permute-start(f32[1024,256]{1,0:T(8,128)S(1)} %bitcast.16), channel_id=1, source_target_pairs={{0,16},{16,0},{32,48},{48,32},{1,17},{17,1},{33,49},{49,33},{2,18}... | collective-permute-start | bytes 3145736 | tf_op jit(solution)/shard_map/ppermute | solution.py:417
  98.6 34.4 %all-to-all-start.2 = ((f32[32,2,16,128]{3,2,1,0:T(8,128)}), f32[32,2,16,128]{3,2,1,0:T(8,128)S(1)}, u32[]{:S(2)}, u32[]{:S(2)}) async-start(f32[32,2,16,128]{3,2,1,0:T(8,128)} %bitcast.20), calls=%async_computation.2 | async-start | bytes 1048576 | tf_op jit(solution)/shard_map/all_to_all | solution.py:427
  132.9 2.2 %copy-start.8 = (s32[4]{0:T(128)S(1)}, s32[4]{0:T(128)}, u32[]{:S(2)}) copy-start(s32[4]{0:T(128)} %copy-done.7) | copy-start | bytes 52
  133.0 12.1 %collective-permute-start.11 = (f32[1024,256]{1,0:T(8,128)}, f32[1024,256]{1,0:T(8,128)}, u32[]{:S(2)}, u32[]{:S(2)}) collective-permute-start(f32[1024,256]{1,0:T(8,128)} %collective-permute-done.10.refs_6_.row2), channel_id=1, source_target_pairs={{0,16},{16,0},{32,48},{48,32},{1,17},{17,1},{33,49},{49,33},{2,18}... | collective-permute-start | bytes 3145736 | tf_op jit(solution)/shard_map/ppermute | solution.py:417
  137.6 0.8 copy-start.5
  138.4 33.9 %all-to-all-start.3 = ((f32[16,4,16,256]{3,2,1,0:T(8,128)}), f32[16,4,16,256]{3,2,1,0:T(8,128)S(1)}, u32[]{:S(2)}, u32[]{:S(2)}) async-start(f32[16,4,16,256]{3,2,1,0:T(8,128)} %get-tuple-element.25), calls=%async_computation.3 | async-start | bytes 2097152 | tf_op jit(solution)/shard_map/all_to_all | solution.py:427
  172.3 1.1 copy-start.9
  (2 other events, 1.5 us)

commit v7 on v6

--- a/solution.py
+++ b/solution.py
@@ -88,57 +88,51 @@
             out_ref[sub, target] = tile
 
 
-def each_source(where_ref, map_ref, use):
+def find_sources(where_ref, map_ref, from_ref):
     col = where_ref[1]
-
-    def body(source, carry):
-        child = source // (SHARDS // 2)
-        block = map_ref[child, source % (SHARDS // 2) * COLS + col]
-        use(source, block // (2 * COLS) * 2 + block % 2)
-        return carry
-
-    lax.fori_loop(0, SHARDS, body, 0)
-
-
-def add_block(out_ref, slot, parent, received_ref, source):
+    for source in range(SHARDS):
+        child, number = divmod(source, SHARDS // 2)
+        block = map_ref[child, number * COLS + col]
+        from_ref[block // (2 * COLS) * 2 + block % 2] = source
+
+
+def add_block(out_ref, at, parent, received_ref, source):
     for half in range(2):
         lanes = slice(half * TILE, (half + 1) * TILE)
-        out_ref[slot, :, lanes] = parent[:, lanes] + received_ref[source, half]
-
-
-def place_kernel(where_ref, map_ref, received_ref, parent_ref, out_ref, top_ref):
-    def use(source, slot):
-        add_block(out_ref, slot, parent_ref[slot], received_ref, source)
-
-    each_source(where_ref, map_ref, use)
+        out_ref[at, :, lanes] = parent[:, lanes] + received_ref[source, half]
+
+
+def place_kernel(where_ref, map_ref, received_ref, parent_ref, out_ref, top_ref, from_ref):
+    find_sources(where_ref, map_ref, from_ref)
+    for slot in range(SHARDS):
+        add_block(out_ref, slot, parent_ref[slot], received_ref, from_ref[slot])
     for q in range(COLS):
         top_ref[q] = out_ref[:TOP]
 
 
-def place_top_kernel(where_ref, map_ref, received_ref, parent_ref, top_ref, out_ref):
-    def use(source, slot):
-        @pl.when(slot < TOP)
-        def _():
-            add_block(out_ref, slot, parent_ref[slot], received_ref, source)
-
-    each_source(where_ref, map_ref, use)
-    for q in range(COLS):
-        top_ref[q] = out_ref[...]
-
-
-def place_rest_kernel(where_ref, map_ref, received_ref, parent_ref, top_ref, pivots_ref, out_ref):
-    def use(source, slot):
-        @pl.when(slot >= TOP)
-        def _():
-            add_block(out_ref, SHARDS + slot, parent_ref[slot - TOP], received_ref, source)
-
-    each_source(where_ref, map_ref, use)
+def place_top_kernel(where_ref, map_ref, received_ref, parent_ref, top_ref, from_ref):
+    find_sources(where_ref, map_ref, from_ref)
+    for slot in range(TOP):
+        for half in range(2):
+            lanes = slice(half * TILE, (half + 1) * TILE)
+            block = parent_ref[slot, :, lanes] + received_ref[from_ref[slot], half]
+            for q in range(COLS):
+                top_ref[q, slot, :, lanes] = block
+
+
+def place_rest_kernel(
+    where_ref, map_ref, received_ref, parent_ref, top_ref, pivots_ref, out_ref, from_ref
+):
+    find_sources(where_ref, map_ref, from_ref)
+    for slot in range(TOP, SHARDS):
+        add_block(out_ref, SHARDS + slot, parent_ref[slot - TOP], received_ref, from_ref[slot])
     for q in range(COLS):
         for half in range(2):
             out_ref[2 * q + half] = pivots_ref[q, 2 + half]
     out_ref[SHARDS : SHARDS + TOP] = top_ref[0]
 
 
+SOURCES = [pltpu.SMEM((SHARDS,), jnp.int32)]
 FRONT = jax.ShapeDtypeStruct((SHARDS, BLK, WIDE), jnp.float32)
 TOPS = jax.ShapeDtypeStruct((COLS, TOP, BLK, WIDE), jnp.float32)
 
@@ -366,22 +360,29 @@
         pltpu.make_async_copy(source, target, sems.at[4 + i])
         for i, (source, target) in enumerate(copies)
     ]
-    each_chunk(row, refs, lambda *at: copy_rows(*at).start())
     for copy in copies:
         copy.start()
-    each_chunk(row, refs, lambda *at: copy_rows(*at).wait())
-    for copy in copies:
-        copy.wait()
-    inv0, inv1, x01 = split(inv0_ref[...]), split(inv1_ref[...]), split(x01_ref[...])
-    r0 = split(contract_split(split(rows_ref[:, :PANEL]), inv0, (1, 1)))
+    each_chunk(row, refs, lambda *at: copy_rows(*at).start())
+    inv0_copy, cols0_copy, cols1_copy, x01_copy, inv1_copy, front_copy = copies
+    inv0_copy.wait()
+    cols0_copy.wait()
+    inv0 = split(inv0_ref[...])
     c0 = contract_split(inv0, split(cols0_ref[...].reshape(PANEL, WIDE)), (1, 0))
     cols0_ref[...] = c0.reshape(cols0_ref.shape)
     c0 = split(c0)
+    cols1_copy.wait()
+    x01_copy.wait()
+    x01 = split(x01_ref[...])
+    c1 = split(cols1_ref[...].reshape(PANEL, WIDE) - contract_split(x01, c0, (0, 0)))
+    inv1_copy.wait()
+    inv1 = split(inv1_ref[...])
+    c1 = contract_split(inv1, c1, (1, 0))
+    cols1_ref[...] = c1.reshape(cols1_ref.shape)
+    each_chunk(row, refs, lambda *at: copy_rows(*at).wait())
+    r0 = split(contract_split(split(rows_ref[:, :PANEL]), inv0, (1, 1)))
     r1 = split(rows_ref[:, PANEL:] - contract_split(r0, x01, (1, 0)))
     r1 = split(contract_split(r1, inv1, (1, 1)))
-    c1 = split(cols1_ref[...].reshape(PANEL, WIDE) - contract_split(x01, c0, (0, 0)))
-    c1 = contract_split(inv1, c1, (1, 0))
-    cols1_ref[...] = c1.reshape(cols1_ref.shape)
+    front_copy.wait()
     update = contract_split(r0, c0, (1, 0)) + contract_split(r1, split(c1), (1, 0))
     live = (shard >= ROWS).astype(jnp.float32)
     for slot in range(TOP, SHARDS):
@@ -408,7 +409,7 @@
             pltpu.VMEM((SHARDS, BLK, WIDE), jnp.float32),
             pltpu.SemaphoreType.DMA((10,)),
         ],
-        compiler_params=params(60),
+        compiler_params=params(59),
         name="finish",
     )(where, inv0, inv1, x01, cols, *rows, front)
 
@@ -436,10 +437,10 @@
     for step in (4, 2, 1):
         pairs = [(i, i + step) for i in range(0, SUBS, 2 * step)]
         got = lax.ppermute(x, "sub", pairs)
-        if beside is not None and step == 4:
-            got, _ = lax.optimization_barrier((got, beside))
+        if step == 4:
+            got, beside = lax.optimization_barrier((got, beside))
         x = jnp.where(sub % (2 * step) == step, got, x)
-    return x
+    return x, beside
 
 
 def local(parent_front, child_schur, index_map):
@@ -447,7 +448,6 @@
     shard = sub * ROWS + row
     where = jnp.stack([shard // (SHARDS // 2), col, row, shard]).astype(jnp.int32)
     parent = parent_front.reshape(SHARDS, BLK, WIDE)
-    parent_top = from_first(parent[:TOP], sub)
 
     low = call(
         spread_low_kernel,
@@ -456,13 +456,9 @@
         4,
         [pltpu.SMEM((2 * SHARDS * TILE // BLK,), jnp.int32)],
     )
+    parent_top, low = from_first(parent[:TOP], sub, low)
     low = exchange(low.reshape(SHARDS, 2, BLK, TILE), ("sub", "row"))
-    tops, _ = call(
-        place_top_kernel,
-        (TOPS, jax.ShapeDtypeStruct((TOP, BLK, WIDE), jnp.float32)),
-        (where, index_map, low, parent_top),
-        6,
-    )
+    tops = call(place_top_kernel, TOPS, (where, index_map, low, parent_top), 6, SOURCES)
     tops, child_late = lax.optimization_barrier((tops, child_schur))
     pivots = exchange(tops, "col")
     spread = call(
@@ -471,12 +467,13 @@
         (where, index_map, child_late),
         4,
     )
-    parent_rest = from_first(parent[TOP:], sub, spread)
+    parent_rest, spread = from_first(parent[TOP:], sub, spread)
     tail = call(
         place_rest_kernel,
         jax.ShapeDtypeStruct((2 * SHARDS, BLK, WIDE), jnp.float32),
         (where, index_map, low, parent_rest, tops, pivots),
         8,
+        SOURCES,
     )
     upper = over_rows(pivots[:, :2].reshape(PANEL, WIDE))
     inv0 = first_factor(where, upper)
@@ -488,7 +485,7 @@
         (exchange(spread, ("sub", "row")), swap(tail, "row", 2), inv0)
     )
     tail = tail, swap(tail, "row", 1), across, swap(across, "row", 1)
-    front, tops = call(place_kernel, (FRONT, TOPS), (where, index_map, received, parent), 6)
+    front, tops = call(place_kernel, (FRONT, TOPS), (where, index_map, received, parent), 6, SOURCES)
     inv1, x01 = second_factor(where, inv0, upper, tail)
     cols = exchange(tops, "col").reshape(COLS, TOP * BLK, WIDE)
     out = finish(where, inv0, inv1, x01, cols, tail, front)

time: 188 us -> 193 us (1.027)
  waiting for transfers between devices: 17.8 us -> 24.7 us
  starting transfers between devices: 84.1 us -> 81.5 us
    all_to_all x4, starting transfers between devices: 38.8 us -> 31.4 us  [exchange(): return lax.all_to_all(x, axis, split_axis=0, concat_axis=0, tiled=True)]
    all_to_all x4, waiting for transfers between devices: 8.65 us -> 12.8 us  [exchange(): return lax.all_to_all(x, axis, split_axis=0, concat_axis=0, tiled=True)]
    ppermute x6, starting transfers between devices: 23.7 us -> 27.6 us  [from_first(): got = lax.ppermute(x, 'sub', pairs)]
    ppermute x6, waiting for transfers between devices: 9.14 us -> 11.9 us  [from_first(): got = lax.ppermute(x, 'sub', pairs)]
where the time goes in v7:
time: 193 us; the launch traced here: 189 us
  starting transfers between devices  81.5 us (42%)
  Pallas kernels  75.8 us (39%)
  waiting for transfers between devices  24.7 us (13%)
  local copies, waits for them, and re-layouts  6 us (3%)
    all_to_all x4, starting transfers between devices, exchange(): return lax.all_to_all(x, axis, split_axis=0, concat_axis=0, tiled=True)  31.4 us
    ppermute x6, starting transfers between devices, from_first(): got = lax.ppermute(x, 'sub', pairs)  27.6 us
    pallas_call x1, Pallas kernels, second_factor(): pl.pallas_call(second_kernel, out_shape=(shape, shape), in_specs=[SMEM] +...  26.7 us
    pallas_call x1, Pallas kernels, first_factor(): pl.pallas_call(first_kernel, out_shape=jax.ShapeDtypeStruct((PANEL, PANEL...  24.4 us
    ppermute x6, starting transfers between devices, swap(): return lax.ppermute(x, axis, [(i, i ^ bit) for i in range(ROWS)])  22.6 us
    pallas_call x5, Pallas kernels, call(): pl.pallas_call(kernel, out_shape=out_shape, in_specs=[SMEM, SMEM] + [VMEM...  12.8 us
    all_to_all x4, waiting for transfers between devices, exchange(): return lax.all_to_all(x, axis, split_axis=0, concat_axis=0, tiled=True)  12.8 us
    pallas_call x1, Pallas kernels, finish(): pl.pallas_call(finish_kernel, out_shape=FRONT, in_specs=[SMEM] + [HBM] *...  12 us
  transfers between devices with their start and end apart: 16, of which 6 were waited for; matrix products, arithmetic and copies ran while one was open for 1% of the time, Pallas kernels for 33%

profile of v7, /device:TPU:1, one launch (start us, length us, event | category | flops | bytes accessed | tf_op | source)
XLA Modules:
  0.0 189.0 jit_solution(13436333777613417592)
XLA Ops:
  0.8 11.5 %collective-permute-start = (f32[4,16,256]{2,1,0:T(8,128)S(1)}, f32[4,16,256]{2,1,0:T(8,128)S(1)}, u32[]{:S(2)}, u32[]{:S(2)}) collective-permute-start(f32[4,16,256]{2,1,0:T(8,128)S(1)} %bitcast.24), channel_id=1, source_target_pairs={{0,256},{1,257},{2,258},{3,259},{4,260},{5,261},{6,262},{7,263},{8... | collective-permute-start | bytes 196616 | tf_op jit(solution)/shard_map/ppermute | solution.py:439
  14.0 2.8 %spread_low.1 = f32[8,8,16,128]{3,2,1,0:T(8,128)} custom-call(s32[4]{0:T(128)S(1)} %pad_add_fusion.where_ref, s32[2,256]{1,0:T(2,128)S(1)} %copy-done.6, f32[16,4096]{1,0:T(8,128)S(1)} %copy-done.3), custom_call_target="tpu_custom_call" | custom-call | tf_op jit(solution)/shard_map/spread_low/pallas_call | solution.py:142
  16.8 7.0 %all-to-all-start = ((f32[32,2,16,128]{3,2,1,0:T(8,128)}), f32[32,2,16,128]{3,2,1,0:T(8,128)S(1)}, u32[]{:S(2)}, u32[]{:S(2)}) async-start(f32[32,2,16,128]{3,2,1,0:T(8,128)} %bitcast.5), calls=%async_computation | async-start | bytes 1048576 | tf_op jit(solution)/shard_map/all_to_all | solution.py:428
  23.8 4.2 %collective-permute-start.1 = (f32[4,16,256]{2,1,0:T(8,128)S(1)}, f32[4,16,256]{2,1,0:T(8,128)S(1)}, u32[]{:S(2)}, u32[]{:S(2)}) collective-permute-start(f32[4,16,256]{2,1,0:T(8,128)S(1)} %broadcast_select_fusion.3), channel_id=1, source_target_pairs={{0,128},{256,384},{1,129},{257,385},{2,130},{258,386},{3,131},{259... | collective-permute-start | bytes 196616 | tf_op jit(solution)/shard_map/ppermute | solution.py:439
  28.0 7.5 %collective-permute-done.1 = f32[4,16,256]{2,1,0:T(8,128)S(1)} collective-permute-done((f32[4,16,256]{2,1,0:T(8,128)S(1)}, f32[4,16,256]{2,1,0:T(8,128)S(1)}, u32[]{:S(2)}, u32[]{:S(2)}) %collective-permute-start.1) | collective-permute-done | bytes 65568 | tf_op jit(solution)/shard_map/ppermute | solution.py:439
  38.2 2.7 %all-to-all-done.received_ref = f32[32,2,16,128]{3,2,1,0:T(8,128)S(1)} async-done(((f32[32,2,16,128]{3,2,1,0:T(8,128)}), f32[32,2,16,128]{3,2,1,0:T(8,128)S(1)}, u32[]{:S(2)}, u32[]{:S(2)}) %all-to-all-start) | async-done | bytes 524320 | tf_op jit(solution)/shard_map/all_to_all | solution.py:428
  42.9 9.2 %all-to-all-start.1 = ((f32[16,4,16,256]{3,2,1,0:T(8,128)}), f32[16,4,16,256]{3,2,1,0:T(8,128)S(1)}, u32[]{:S(2)}, u32[]{:S(2)}) async-start(f32[16,4,16,256]{3,2,1,0:T(8,128)} %place_top.1.top_ref), calls=%async_computation.1 | async-start | bytes 2097152 | tf_op jit(solution)/shard_map/all_to_all | solution.py:428
  52.2 5.9 %collective-permute-start.6 = (f32[28,16,256]{2,1,0:T(8,128)S(1)}, f32[28,16,256]{2,1,0:T(8,128)S(1)}, u32[]{:S(2)}, u32[]{:S(2)}) collective-permute-start(f32[28,16,256]{2,1,0:T(8,128)S(1)} %bitcast.22), channel_id=1, source_target_pairs={{0,256},{1,257},{2,258},{3,259},{4,260},{5,261},{6,262},{7,263},{8... | collective-permute-start | bytes 1376264 | tf_op jit(solution)/shard_map/ppermute | solution.py:439
  58.1 4.4 %spread.1 = f32[64,16,128]{2,1,0:T(8,128)S(1)} custom-call(s32[4]{0:T(128)S(1)} %pad_add_fusion.where_ref, s32[2,256]{1,0:T(2,128)S(1)} %copy-done.6, f32[16,4096]{1,0:T(8,128)S(1)} %copy-done.4), custom_call_target="tpu_custom_call" | custom-call | tf_op jit(solution)/shard_map/spread/pallas_call | solution.py:142
  63.4 3.1 %collective-permute-done.6 = f32[28,16,256]{2,1,0:T(8,128)S(1)} collective-permute-done((f32[28,16,256]{2,1,0:T(8,128)S(1)}, f32[28,16,256]{2,1,0:T(8,128)S(1)}, u32[]{:S(2)}, u32[]{:S(2)}) %collective-permute-start.6) | collective-permute-done | bytes 458784 | tf_op jit(solution)/shard_map/ppermute | solution.py:439
  66.5 2.1 %collective-permute-start.7 = (f32[28,16,256]{2,1,0:T(8,128)S(1)}, f32[28,16,256]{2,1,0:T(8,128)}, u32[]{:S(2)}, u32[]{:S(2)}) collective-permute-start(f32[28,16,256]{2,1,0:T(8,128)S(1)} %broadcast_select_fusion), channel_id=1, source_target_pairs={{0,128},{256,384},{1,129},{257,385},{2,130},{258,386},{3,131},{259... | collective-permute-start | bytes 1376264 | tf_op jit(solution)/shard_map/ppermute | solution.py:439
  68.6 9.5 %all-to-all-done.1.pivots_ref = f32[16,4,16,256]{3,2,1,0:T(8,128)S(1)} async-done(((f32[16,4,16,256]{3,2,1,0:T(8,128)}), f32[16,4,16,256]{3,2,1,0:T(8,128)S(1)}, u32[]{:S(2)}, u32[]{:S(2)}) %all-to-all-start.1) | async-done | bytes 1048608 | tf_op jit(solution)/shard_map/all_to_all | solution.py:428
  78.9 2.5 %collective-permute-start.4 = (f32[512,256]{1,0:T(8,128)}, f32[512,256]{1,0:T(8,128)}, u32[]{:S(2)}, u32[]{:S(2)}) collective-permute-start(f32[512,256]{1,0:T(8,128)} %bitcast.6.own.refs_0_), channel_id=1, source_target_pairs={{0,32},{16,48},{32,0},{48,16},{1,33},{17,49},{33,1},{49,17},{2,34}... | collective-permute-start | bytes 1572872 | tf_op jit(solution)/shard_map/ppermute | solution.py:418
  81.5 2.6 %collective-permute-start.8 = (f32[28,16,256]{2,1,0:T(8,128)S(1)}, f32[28,16,256]{2,1,0:T(8,128)S(1)}, u32[]{:S(2)}, u32[]{:S(2)}) collective-permute-start(f32[28,16,256]{2,1,0:T(8,128)S(1)} %broadcast_select_fusion.1), channel_id=1, source_target_pairs={{0,64},{128,192},{256,320},{384,448},{1,65},{129,193},{257,321},{3... | collective-permute-start | bytes 1376264 | tf_op jit(solution)/shard_map/ppermute | solution.py:439
  84.1 6.6 %collective-permute-start.3 = (f32[512,256]{1,0:T(8,128)}, f32[512,256]{1,0:T(8,128)}, u32[]{:S(2)}, u32[]{:S(2)}) collective-permute-start(f32[512,256]{1,0:T(8,128)} %bitcast.6.own.refs_0_), channel_id=1, source_target_pairs={{0,16},{16,0},{32,48},{48,32},{1,17},{17,1},{33,49},{49,33},{2,18}... | collective-permute-start | bytes 1572872 | tf_op jit(solution)/shard_map/ppermute | solution.py:418
  90.8 6.5 %collective-permute-start.5 = (f32[512,256]{1,0:T(8,128)}, f32[512,256]{1,0:T(8,128)}, u32[]{:S(2)}, u32[]{:S(2)}) collective-permute-start(f32[512,256]{1,0:T(8,128)} %collective-permute-done.4.across.refs_2_), channel_id=1, source_target_pairs={{0,16},{16,0},{32,48},{48,32},{1,17},{17,1},{33,49},{49,33},{2,18}... | collective-permute-start | bytes 1572872 | tf_op jit(solution)/shard_map/ppermute | solution.py:418
  99.0 2.5 %collective-permute-start.10 = (f32[1024,256]{1,0:T(8,128)S(1)}, f32[1024,256]{1,0:T(8,128)}, u32[]{:S(2)}, u32[]{:S(2)}) collective-permute-start(f32[1024,256]{1,0:T(8,128)S(1)} %bitcast.15), channel_id=1, source_target_pairs={{0,32},{16,48},{32,0},{48,16},{1,33},{17,49},{33,1},{49,17},{2,34}... | collective-permute-start | bytes 3145736 | tf_op jit(solution)/shard_map/ppermute | solution.py:418
  101.6 2.2 %collective-permute-start.9 = (f32[1024,256]{1,0:T(8,128)S(1)}, f32[1024,256]{1,0:T(8,128)}, u32[]{:S(2)}, u32[]{:S(2)}) collective-permute-start(f32[1024,256]{1,0:T(8,128)S(1)} %bitcast.16), channel_id=1, source_target_pairs={{0,16},{16,0},{32,48},{48,32},{1,17},{17,1},{33,49},{49,33},{2,18}... | collective-permute-start | bytes 3145736 | tf_op jit(solution)/shard_map/ppermute | solution.py:418
  103.8 8.0 %all-to-all-start.2 = ((f32[32,2,16,128]{3,2,1,0:T(8,128)}), f32[32,2,16,128]{3,2,1,0:T(8,128)S(1)}, u32[]{:S(2)}, u32[]{:S(2)}) async-start(f32[32,2,16,128]{3,2,1,0:T(8,128)} %bitcast.20), calls=%async_computation.2 | async-start | bytes 1048576 | tf_op jit(solution)/shard_map/all_to_all | solution.py:428
  111.8 24.4 %first_factor.1.inv_hbm.inv0_hbm = f32[512,512]{1,0:T(8,128)} custom-call(s32[4]{0:T(128)} %copy-done.7, f32[512,256]{1,0:T(8,128)} %bitcast.6.own.refs_0_, f32[512,256]{1,0:T(8,128)} %collective-permute-done.3.core.refs_1_, f32[512,256]{1,0:T(8,128)} %collective-permute-done.4.across.refs_2_, f32[512,256]{1,0:T(8,128)} %collective-permute-done.5.both.refs_3_), custom_call_target="tpu_custom_call" | custom-call | flops 60000002048 | bytes 4194304 | tf_op jit(solution)/shard_map/first_factor/pallas_call | solution.py:274
  136.2 2.1 %collective-permute-start.11 = (f32[1024,256]{1,0:T(8,128)}, f32[1024,256]{1,0:T(8,128)}, u32[]{:S(2)}, u32[]{:S(2)}) collective-permute-start(f32[1024,256]{1,0:T(8,128)} %collective-permute-done.10.refs_6_.row2), channel_id=1, source_target_pairs={{0,16},{16,0},{32,48},{48,32},{1,17},{17,1},{33,49},{49,33},{2,18}... | collective-permute-start | bytes 3145736 | tf_op jit(solution)/shard_map/ppermute | solution.py:418
  141.2 7.2 %all-to-all-start.3 = ((f32[16,4,16,256]{3,2,1,0:T(8,128)}), f32[16,4,16,256]{3,2,1,0:T(8,128)S(1)}, u32[]{:S(2)}, u32[]{:S(2)}) async-start(f32[16,4,16,256]{3,2,1,0:T(8,128)} %get-tuple-element.29), calls=%async_computation.3 | async-start | bytes 2097152 | tf_op jit(solution)/shard_map/all_to_all | solution.py:428
  148.5 26.7 %second_factor.1 = (f32[512,512]{1,0:T(8,128)}, f32[512,512]{1,0:T(8,128)}) custom-call(s32[4]{0:T(128)} %copy-done.7, f32[512,512]{1,0:T(8,128)} %first_factor.1.inv_hbm.inv0_hbm, f32[512,256]{1,0:T(8,128)} %bitcast.6.own.refs_0_, f32[512,256]{1,0:T(8,128)} %collective-permute-done.3.core.refs_1_, f32[512,256]{1,0:T(8,128)} %collective-permute-done.4.across.refs_2_, ...), custom_call_target="tpu_custom_call" | custom-call | flops 60000002048 | bytes 8388608 | tf_op jit(solution)/shard_map/second_factor/pallas_call | solution.py:323
  176.8 12.0 %finish.1 = f32[32,16,256]{2,1,0:T(8,128)} custom-call(s32[4]{0:T(128)} %copy-done.7, f32[512,512]{1,0:T(8,128)} %first_factor.1.inv_hbm.inv0_hbm, f32[512,512]{1,0:T(8,128)} %get-tuple-element.26.inv1_hbm, f32[512,512]{1,0:T(8,128)} %get-tuple-element.27.x01_hbm, f32[16,64,256]{2,1,0:T(8,128)} %bitcast.21, f32[1024,256]{1,0:T(8,128)} %bitcast.18, ...), custom_call_target="tpu_custom_call" | custom-call | tf_op jit(solution)/shard_map/finish/pallas_call | solution.py:399
  (46 shorter events, 15.1 us)
Async XLA Ops:
  0.8 15.9 %collective-permute-start = (f32[4,16,256]{2,1,0:T(8,128)S(1)}, f32[4,16,256]{2,1,0:T(8,128)S(1)}, u32[]{:S(2)}, u32[]{:S(2)}) collective-permute-start(f32[4,16,256]{2,1,0:T(8,128)S(1)} %bitcast.24), channel_id=1, source_target_pairs={{0,256},{1,257},{2,258},{3,259},{4,260},{5,261},{6,262},{7,263},{8... | collective-permute-start | bytes 196616 | tf_op jit(solution)/shard_map/ppermute | solution.py:439
  13.0 0.9 copy-start.3
  14.0 83.5 %copy-start.7 = (s32[4]{0:T(128)}, s32[4]{0:T(128)S(1)}, u32[]{:S(2)}) copy-start(s32[4]{0:T(128)S(1)} %pad_add_fusion.where_ref) | copy-start | bytes 52
  16.8 24.1 %all-to-all-start = ((f32[32,2,16,128]{3,2,1,0:T(8,128)}), f32[32,2,16,128]{3,2,1,0:T(8,128)S(1)}, u32[]{:S(2)}, u32[]{:S(2)}) async-start(f32[32,2,16,128]{3,2,1,0:T(8,128)} %bitcast.5), calls=%async_computation | async-start | bytes 1048576 | tf_op jit(solution)/shard_map/all_to_all | solution.py:428
  23.8 11.7 %collective-permute-start.1 = (f32[4,16,256]{2,1,0:T(8,128)S(1)}, f32[4,16,256]{2,1,0:T(8,128)S(1)}, u32[]{:S(2)}, u32[]{:S(2)}) collective-permute-start(f32[4,16,256]{2,1,0:T(8,128)S(1)} %broadcast_select_fusion.3), channel_id=1, source_target_pairs={{0,128},{256,384},{1,129},{257,385},{2,130},{258,386},{3,131},{259... | collective-permute-start | bytes 196616 | tf_op jit(solution)/shard_map/ppermute | solution.py:439
  35.5 2.6 %collective-permute-start.2 = (f32[4,16,256]{2,1,0:T(8,128)S(1)}, f32[4,16,256]{2,1,0:T(8,128)S(1)}, u32[]{:S(2)}, u32[]{:S(2)}) collective-permute-start(f32[4,16,256]{2,1,0:T(8,128)S(1)} %broadcast_select_fusion.4), channel_id=1, source_target_pairs={{0,64},{128,192},{256,320},{384,448},{1,65},{129,193},{257,321},{3... | collective-permute-start | bytes 196616 | tf_op jit(solution)/shard_map/ppermute | solution.py:439
  42.9 9.2 %copy-start.1 = (f32[16,1,32,256]{3,2,1,0:T(8,128)S(1)}, f32[16,1,32,256]{3,2,1,0:T(8,128)}, u32[]{:S(2)}) copy-start(f32[16,1,32,256]{3,2,1,0:T(8,128)} %param.3) | copy-start | bytes 1572868
  42.9 35.2 %all-to-all-start.1 = ((f32[16,4,16,256]{3,2,1,0:T(8,128)}), f32[16,4,16,256]{3,2,1,0:T(8,128)S(1)}, u32[]{:S(2)}, u32[]{:S(2)}) async-start(f32[16,4,16,256]{3,2,1,0:T(8,128)} %place_top.1.top_ref), calls=%async_computation.1 | async-start | bytes 2097152 | tf_op jit(solution)/shard_map/all_to_all | solution.py:428
  52.1 6.0 %copy-start.4 = (f32[16,4096]{1,0:T(8,128)S(1)}, f32[16,4096]{1,0:T(8,128)}, u32[]{:S(2)}) copy-start(f32[16,4096]{1,0:T(8,128)} %child_ref.2) | copy-start | bytes 786436
  52.2 14.3 %collective-permute-start.6 = (f32[28,16,256]{2,1,0:T(8,128)S(1)}, f32[28,16,256]{2,1,0:T(8,128)S(1)}, u32[]{:S(2)}, u32[]{:S(2)}) collective-permute-start(f32[28,16,256]{2,1,0:T(8,128)S(1)} %bitcast.22), channel_id=1, source_target_pairs={{0,256},{1,257},{2,258},{3,259},{4,260},{5,261},{6,262},{7,263},{8... | collective-permute-start | bytes 1376264 | tf_op jit(solution)/shard_map/ppermute | solution.py:439
  66.5 14.9 %collective-permute-start.7 = (f32[28,16,256]{2,1,0:T(8,128)S(1)}, f32[28,16,256]{2,1,0:T(8,128)}, u32[]{:S(2)}, u32[]{:S(2)}) collective-permute-start(f32[28,16,256]{2,1,0:T(8,128)S(1)} %broadcast_select_fusion), channel_id=1, source_target_pairs={{0,128},{256,384},{1,129},{257,385},{2,130},{258,386},{3,131},{259... | collective-permute-start | bytes 1376264 | tf_op jit(solution)/shard_map/ppermute | solution.py:439
  78.9 11.9 %collective-permute-start.4 = (f32[512,256]{1,0:T(8,128)}, f32[512,256]{1,0:T(8,128)}, u32[]{:S(2)}, u32[]{:S(2)}) collective-permute-start(f32[512,256]{1,0:T(8,128)} %bitcast.6.own.refs_0_), channel_id=1, source_target_pairs={{0,32},{16,48},{32,0},{48,16},{1,33},{17,49},{33,1},{49,17},{2,34}... | collective-permute-start | bytes 1572872 | tf_op jit(solution)/shard_map/ppermute | solution.py:418
  81.5 15.8 %collective-permute-start.8 = (f32[28,16,256]{2,1,0:T(8,128)S(1)}, f32[28,16,256]{2,1,0:T(8,128)S(1)}, u32[]{:S(2)}, u32[]{:S(2)}) collective-permute-start(f32[28,16,256]{2,1,0:T(8,128)S(1)} %broadcast_select_fusion.1), channel_id=1, source_target_pairs={{0,64},{128,192},{256,320},{384,448},{1,65},{129,193},{257,321},{3... | collective-permute-start | bytes 1376264 | tf_op jit(solution)/shard_map/ppermute | solution.py:439
  84.1 27.7 %collective-permute-start.3 = (f32[512,256]{1,0:T(8,128)}, f32[512,256]{1,0:T(8,128)}, u32[]{:S(2)}, u32[]{:S(2)}) collective-permute-start(f32[512,256]{1,0:T(8,128)} %bitcast.6.own.refs_0_), channel_id=1, source_target_pairs={{0,16},{16,0},{32,48},{48,32},{1,17},{17,1},{33,49},{49,33},{2,18}... | collective-permute-start | bytes 1572872 | tf_op jit(solution)/shard_map/ppermute | solution.py:418
  90.8 21.0 %collective-permute-start.5 = (f32[512,256]{1,0:T(8,128)}, f32[512,256]{1,0:T(8,128)}, u32[]{:S(2)}, u32[]{:S(2)}) collective-permute-start(f32[512,256]{1,0:T(8,128)} %collective-permute-done.4.across.refs_2_), channel_id=1, source_target_pairs={{0,16},{16,0},{32,48},{48,32},{1,17},{17,1},{33,49},{49,33},{2,18}... | collective-permute-start | bytes 1572872 | tf_op jit(solution)/shard_map/ppermute | solution.py:418
  99.0 37.1 %copy-start = (f32[64,16,256]{2,1,0:T(8,128)}, f32[64,16,256]{2,1,0:T(8,128)S(1)}, u32[]{:S(2)}) copy-start(f32[64,16,256]{2,1,0:T(8,128)S(1)} %place_rest.1) | copy-start | bytes 3145732
  99.0 37.2 %collective-permute-start.10 = (f32[1024,256]{1,0:T(8,128)S(1)}, f32[1024,256]{1,0:T(8,128)}, u32[]{:S(2)}, u32[]{:S(2)}) collective-permute-start(f32[1024,256]{1,0:T(8,128)S(1)} %bitcast.15), channel_id=1, source_target_pairs={{0,32},{16,48},{32,0},{48,16},{1,33},{17,49},{33,1},{49,17},{2,34}... | collective-permute-start | bytes 3145736 | tf_op jit(solution)/shard_map/ppermute | solution.py:418
  101.6 46.9 %collective-permute-start.9 = (f32[1024,256]{1,0:T(8,128)S(1)}, f32[1024,256]{1,0:T(8,128)}, u32[]{:S(2)}, u32[]{:S(2)}) collective-permute-start(f32[1024,256]{1,0:T(8,128)S(1)} %bitcast.16), channel_id=1, source_target_pairs={{0,16},{16,0},{32,48},{48,32},{1,17},{17,1},{33,49},{49,33},{2,18}... | collective-permute-start | bytes 3145736 | tf_op jit(solution)/shard_map/ppermute | solution.py:418
  103.8 32.4 %all-to-all-start.2 = ((f32[32,2,16,128]{3,2,1,0:T(8,128)}), f32[32,2,16,128]{3,2,1,0:T(8,128)S(1)}, u32[]{:S(2)}, u32[]{:S(2)}) async-start(f32[32,2,16,128]{3,2,1,0:T(8,128)} %bitcast.20), calls=%async_computation.2 | async-start | bytes 1048576 | tf_op jit(solution)/shard_map/all_to_all | solution.py:428
  136.2 2.2 %copy-start.8 = (s32[4]{0:T(128)S(1)}, s32[4]{0:T(128)}, u32[]{:S(2)}) copy-start(s32[4]{0:T(128)} %copy-done.7) | copy-start | bytes 52
  136.2 12.3 %collective-permute-start.11 = (f32[1024,256]{1,0:T(8,128)}, f32[1024,256]{1,0:T(8,128)}, u32[]{:S(2)}, u32[]{:S(2)}) collective-permute-start(f32[1024,256]{1,0:T(8,128)} %collective-permute-done.10.refs_6_.row2), channel_id=1, source_target_pairs={{0,16},{16,0},{32,48},{48,32},{1,17},{17,1},{33,49},{49,33},{2,18}... | collective-permute-start | bytes 3145736 | tf_op jit(solution)/shard_map/ppermute | solution.py:418
  140.4 0.8 copy-start.5
  141.2 34.5 %all-to-all-start.3 = ((f32[16,4,16,256]{3,2,1,0:T(8,128)}), f32[16,4,16,256]{3,2,1,0:T(8,128)S(1)}, u32[]{:S(2)}, u32[]{:S(2)}) async-start(f32[16,4,16,256]{3,2,1,0:T(8,128)} %get-tuple-element.29), calls=%async_computation.3 | async-start | bytes 2097152 | tf_op jit(solution)/shard_map/all_to_all | solution.py:428
  175.7 1.1 copy-start.9
  (2 other events, 1.5 us)

commit v8 on v7

--- a/solution.py
+++ b/solution.py
@@ -215,7 +215,7 @@
     return contract_split(split(a), split(b), dims)
 
 
-def invert_factor(m_ref, w_ref, t_ref):
+def invert_factor(m_ref, w_ref, t_ref, beside=None):
     tiles = m_ref.shape[0] // TILE
     w_ref[...] = jnp.zeros_like(w_ref)
 
@@ -224,6 +224,8 @@
         factor_tile(
             lambda h: m_ref[pl.ds(pl.multiple_of(low + 8 * h, 8), 8), pl.ds(low, TILE)], t_ref
         )
+        if beside is not None:
+            beside(b)
         for c in range(tiles):
 
             @pl.when(b == c)
@@ -289,7 +291,8 @@
 
 def second_kernel(where_ref, inv_hbm, *refs):
     upper, lower, refs = refs[:4], refs[4:8], refs[8:]
-    w_hbm, x_hbm, inv_ref, a_ref, m_ref, w_ref, x_ref, t_ref, sems = refs
+    w_hbm, x_hbm, r_hbm, inv_ref, a_ref, m_ref, w_ref, x_ref, r_ref, t_ref = refs[:10]
+    inv_parts, x_parts, sems = refs[10:]
 
     def copy_upper(number, ref, lanes):
         return pltpu.make_async_copy(ref, a_ref.at[:, lanes], sems.at[number])
@@ -298,22 +301,46 @@
         rows = ref.at[pl.ds(0, PANEL), :]
         return pltpu.make_async_copy(rows, m_ref.at[:, lanes], sems.at[4 + number])
 
+    def copy_rows(number, ref, lanes):
+        rows = ref.at[pl.ds(PANEL, PANEL), :]
+        return pltpu.make_async_copy(rows, r_ref.at[:, lanes], sems.at[8 + number])
+
     row = where_ref[2]
-    inv = pltpu.make_async_copy(inv_hbm, inv_ref, sems.at[8])
+    inv = pltpu.make_async_copy(inv_hbm, inv_ref, sems.at[12])
     inv.start()
     each_chunk(row, upper, lambda *at: copy_upper(*at).start(), 2, 4)
     each_chunk(row, lower, lambda *at: copy_lower(*at).start(), 2, 4)
+    each_chunk(row, lower, lambda *at: copy_rows(*at).start())
     inv.wait()
+    inv_parts[0], inv_parts[1] = split(inv_ref[...])
     each_chunk(row, upper, lambda *at: copy_upper(*at).wait(), 2, 4)
-    x_ref[...] = multiply(inv_ref[...], a_ref[...], (1, 0))
-    out = pltpu.make_async_copy(x_ref, x_hbm, sems.at[9])
+    inv = inv_parts[0], inv_parts[1]
+    x_ref[...] = contract_split(inv, split(a_ref[...]), (1, 0))
+    out = pltpu.make_async_copy(x_ref, x_hbm, sems.at[13])
     out.start()
-    x = x_ref[...]
+    x_parts[0], x_parts[1] = split(x_ref[...])
+    x = x_parts[0], x_parts[1]
     each_chunk(row, lower, lambda *at: copy_lower(*at).wait(), 2, 4)
-    m_ref[...] = m_ref[...] - multiply(x, x, (0, 0))
-    invert_factor(m_ref, w_ref, t_ref)
-    last = pltpu.make_async_copy(w_ref, w_hbm, sems.at[10])
+    m_ref[...] = m_ref[...] - contract_split(x, x, (0, 0))
+    each_chunk(row, lower, lambda *at: copy_rows(*at).wait())
+
+    def rows_out(b):
+        rows = pl.ds(pl.multiple_of(b * TILE, TILE), TILE)
+        return pltpu.make_async_copy(r_ref.at[rows, :], r_hbm.at[rows, :], sems.at[15 + b])
+
+    def beside(b):
+        rows = pl.ds(pl.multiple_of(b * TILE, TILE), TILE)
+        first = contract_split(split(r_ref[rows, :PANEL]), (inv_parts[0], inv_parts[1]), (1, 1))
+        r_ref[rows, :PANEL] = first
+        left = contract_split(split(first), (x_parts[0], x_parts[1]), (1, 0))
+        r_ref[rows, PANEL:] = r_ref[rows, PANEL:] - left
+        rows_out(b).start()
+
+    invert_factor(m_ref, w_ref, t_ref, beside)
+    last = pltpu.make_async_copy(w_ref, w_hbm, sems.at[14])
     last.start()
+    for b in range(ROWS):
+        rows_out(b).wait()
     out.wait()
     last.wait()
 
@@ -322,13 +349,16 @@
     shape = jax.ShapeDtypeStruct((PANEL, PANEL), jnp.float32)
     return pl.pallas_call(
         second_kernel,
-        out_shape=(shape, shape),
+        out_shape=(shape, shape, jax.ShapeDtypeStruct((PANEL, 2 * PANEL), jnp.float32)),
         in_specs=[SMEM] + [HBM] * 9,
-        out_specs=(HBM, HBM),
+        out_specs=(HBM, HBM, HBM),
         scratch_shapes=[
             square(), square(), square(), square(), square(),
+            pltpu.VMEM((PANEL, 2 * PANEL), jnp.float32),
             pltpu.VMEM((TILE, TILE), jnp.float32),
-            pltpu.SemaphoreType.DMA((11,)),
+            pltpu.VMEM((2, PANEL, PANEL), jnp.bfloat16),
+            pltpu.VMEM((2, PANEL, PANEL), jnp.bfloat16),
+            pltpu.SemaphoreType.DMA((19,)),
         ],
         compiler_params=params(60),
         cost_estimate=pl.CostEstimate(flops=60_000_000_000, bytes_accessed=8 << 20, transcendentals=0),
@@ -337,52 +367,36 @@
 
 
 def finish_kernel(
-    where_ref, inv0_hbm, inv1_hbm, x01_hbm, cols_hbm, row0, row1, row2, row3, front_hbm, out_ref,
+    where_ref, inv0_hbm, inv1_hbm, x01_hbm, cols_hbm, rows_hbm, front_hbm, out_ref,
     inv0_ref, inv1_ref, x01_ref, rows_ref, cols0_ref, cols1_ref, front_ref, sems,
 ):
-    col, row, shard = where_ref[1], where_ref[2], where_ref[3]
-    refs = (row0, row1, row2, row3)
-
-    def copy_rows(number, ref, lanes):
-        return pltpu.make_async_copy(
-            ref.at[pl.ds(PANEL, PANEL), :], rows_ref.at[:, lanes], sems.at[number]
-        )
-
+    col, shard = where_ref[1], where_ref[3]
     copies = [
         (inv0_hbm, inv0_ref),
         (cols_hbm.at[:, pl.ds(0, 2 * BLK), :], cols0_ref),
         (cols_hbm.at[:, pl.ds(2 * BLK, 2 * BLK), :], cols1_ref),
         (x01_hbm, x01_ref),
         (inv1_hbm, inv1_ref),
+        (rows_hbm, rows_ref),
         (front_hbm, front_ref),
     ]
     copies = [
-        pltpu.make_async_copy(source, target, sems.at[4 + i])
+        pltpu.make_async_copy(source, target, sems.at[i])
         for i, (source, target) in enumerate(copies)
     ]
     for copy in copies:
         copy.start()
-    each_chunk(row, refs, lambda *at: copy_rows(*at).start())
-    inv0_copy, cols0_copy, cols1_copy, x01_copy, inv1_copy, front_copy = copies
-    inv0_copy.wait()
-    cols0_copy.wait()
-    inv0 = split(inv0_ref[...])
+    for copy in copies:
+        copy.wait()
+    inv0, inv1, x01 = split(inv0_ref[...]), split(inv1_ref[...]), split(x01_ref[...])
+    r0 = split(rows_ref[:, :PANEL])
     c0 = contract_split(inv0, split(cols0_ref[...].reshape(PANEL, WIDE)), (1, 0))
     cols0_ref[...] = c0.reshape(cols0_ref.shape)
     c0 = split(c0)
-    cols1_copy.wait()
-    x01_copy.wait()
-    x01 = split(x01_ref[...])
+    r1 = split(contract_split(split(rows_ref[:, PANEL:]), inv1, (1, 1)))
     c1 = split(cols1_ref[...].reshape(PANEL, WIDE) - contract_split(x01, c0, (0, 0)))
-    inv1_copy.wait()
-    inv1 = split(inv1_ref[...])
     c1 = contract_split(inv1, c1, (1, 0))
     cols1_ref[...] = c1.reshape(cols1_ref.shape)
-    each_chunk(row, refs, lambda *at: copy_rows(*at).wait())
-    r0 = split(contract_split(split(rows_ref[:, :PANEL]), inv0, (1, 1)))
-    r1 = split(rows_ref[:, PANEL:] - contract_split(r0, x01, (1, 0)))
-    r1 = split(contract_split(r1, inv1, (1, 1)))
-    front_copy.wait()
     update = contract_split(r0, c0, (1, 0)) + contract_split(r1, split(c1), (1, 0))
     live = (shard >= ROWS).astype(jnp.float32)
     for slot in range(TOP, SHARDS):
@@ -399,7 +413,7 @@
     return pl.pallas_call(
         finish_kernel,
         out_shape=FRONT,
-        in_specs=[SMEM] + [HBM] * 9,
+        in_specs=[SMEM] + [HBM] * 6,
         out_specs=VMEM,
         scratch_shapes=[
             square(), square(), square(),
@@ -407,11 +421,11 @@
             pltpu.VMEM((COLS, 2 * BLK, WIDE), jnp.float32),
             pltpu.VMEM((COLS, 2 * BLK, WIDE), jnp.float32),
             pltpu.VMEM((SHARDS, BLK, WIDE), jnp.float32),
-            pltpu.SemaphoreType.DMA((10,)),
+            pltpu.SemaphoreType.DMA((7,)),
         ],
-        compiler_params=params(59),
+        compiler_params=params(60),
         name="finish",
-    )(where, inv0, inv1, x01, cols, *rows, front)
+    )(where, inv0, inv1, x01, cols, rows, front)
 
 
 def swap(x, axis, bit):
@@ -437,10 +451,10 @@
     for step in (4, 2, 1):
         pairs = [(i, i + step) for i in range(0, SUBS, 2 * step)]
         got = lax.ppermute(x, "sub", pairs)
-        if step == 4:
-            got, beside = lax.optimization_barrier((got, beside))
+        if beside is not None and step == 4:
+            got, _ = lax.optimization_barrier((got, beside))
         x = jnp.where(sub % (2 * step) == step, got, x)
-    return x, beside
+    return x
 
 
 def local(parent_front, child_schur, index_map):
@@ -449,6 +463,7 @@
     where = jnp.stack([shard // (SHARDS // 2), col, row, shard]).astype(jnp.int32)
     parent = parent_front.reshape(SHARDS, BLK, WIDE)
 
+    parent_top = from_first(parent[:TOP], sub)
     low = call(
         spread_low_kernel,
         jax.ShapeDtypeStruct((SUBS, 2 * ROWS, BLK, TILE), jnp.float32),
@@ -456,7 +471,6 @@
         4,
         [pltpu.SMEM((2 * SHARDS * TILE // BLK,), jnp.int32)],
     )
-    parent_top, low = from_first(parent[:TOP], sub, low)
     low = exchange(low.reshape(SHARDS, 2, BLK, TILE), ("sub", "row"))
     tops = call(place_top_kernel, TOPS, (where, index_map, low, parent_top), 6, SOURCES)
     tops, child_late = lax.optimization_barrier((tops, child_schur))
@@ -467,7 +481,7 @@
         (where, index_map, child_late),
         4,
     )
-    parent_rest, spread = from_first(parent[TOP:], sub, spread)
+    parent_rest = from_first(parent[TOP:], sub, spread)
     tail = call(
         place_rest_kernel,
         jax.ShapeDtypeStruct((2 * SHARDS, BLK, WIDE), jnp.float32),
@@ -486,9 +500,9 @@
     )
     tail = tail, swap(tail, "row", 1), across, swap(across, "row", 1)
     front, tops = call(place_kernel, (FRONT, TOPS), (where, index_map, received, parent), 6, SOURCES)
-    inv1, x01 = second_factor(where, inv0, upper, tail)
+    inv1, x01, rows = second_factor(where, inv0, upper, tail)
     cols = exchange(tops, "col").reshape(COLS, TOP * BLK, WIDE)
-    out = finish(where, inv0, inv1, x01, cols, tail, front)
+    out = finish(where, inv0, inv1, x01, cols, rows, front)
     return out.reshape(parent_front.shape)
 
 

time: 193 us -> 183 us (0.948)
  waiting for transfers between devices: 24.7 us -> 16.6 us
  Pallas kernels: 75.8 us -> 73.7 us
    all_to_all x4, starting transfers between devices: 31.4 us -> 38.9 us  [exchange(): return lax.all_to_all(x, axis, split_axis=0, concat_axis=0, tiled=True)]
    ppermute x6, starting transfers between devices: 27.6 us -> 22.9 us  [from_first(): got = lax.ppermute(x, 'sub', pairs)]
    all_to_all x4, waiting for transfers between devices: 12.8 us -> 8.23 us  [exchange(): return lax.all_to_all(x, axis, split_axis=0, concat_axis=0, tiled=True)]
    pallas_call x1, Pallas kernels: 12 us -> 8.37 us  [finish(): pl.pallas_call(finish_kernel, out_shape=FRONT, in_specs=[SMEM] + [HBM] *...]
    ppermute x6, waiting for transfers between devices: 11.9 us -> 8.35 us  [from_first(): got = lax.ppermute(x, 'sub', pairs)]
  transfers between devices with their start and end apart: 16 -> 16, of which waited for: 6 -> 5; matrix products, arithmetic and copies ran while one was open for 1% -> 2% of each run, Pallas kernels for 33% -> 34%
where the time goes in v8:
time: 183 us; the launch traced here: 180 us
  starting transfers between devices  82.5 us (45%)
  Pallas kernels  73.7 us (40%)
  waiting for transfers between devices  16.6 us (9%)
  local copies, waits for them, and re-layouts  4.37 us (2%)
  other arithmetic  2.1 us (1%)
    all_to_all x4, starting transfers between devices, exchange(): return lax.all_to_all(x, axis, split_axis=0, concat_axis=0, tiled=True)  38.9 us
    pallas_call x1, Pallas kernels, second_factor(): pl.pallas_call(second_kernel, out_shape=(shape, shape, jax.ShapeDtypeStru...  27.4 us
    pallas_call x1, Pallas kernels, first_factor(): pl.pallas_call(first_kernel, out_shape=jax.ShapeDtypeStruct((PANEL, PANEL...  24.4 us
    ppermute x6, starting transfers between devices, from_first(): got = lax.ppermute(x, 'sub', pairs)  22.9 us
    ppermute x6, starting transfers between devices, swap(): return lax.ppermute(x, axis, [(i, i ^ bit) for i in range(ROWS)])  20.7 us
    pallas_call x5, Pallas kernels, call(): pl.pallas_call(kernel, out_shape=out_shape, in_specs=[SMEM, SMEM] + [VMEM...  13.5 us
    pallas_call x1, Pallas kernels, finish(): pl.pallas_call(finish_kernel, out_shape=FRONT, in_specs=[SMEM] + [HBM] *...  8.37 us
    ppermute x6, waiting for transfers between devices, from_first(): got = lax.ppermute(x, 'sub', pairs)  8.35 us
  transfers between devices with their start and end apart: 16, of which 5 were waited for; matrix products, arithmetic and copies ran while one was open for 2% of the time, Pallas kernels for 34%

profile of v8, /device:TPU:1, one launch (start us, length us, event | category | flops | bytes accessed | tf_op | source)
XLA Modules:
  0.0 179.8 jit_solution(2759640599274762283)
XLA Ops:
  1.7 2.8 %spread_low.1 = f32[8,8,16,128]{3,2,1,0:T(8,128)} custom-call(s32[4]{0:T(128)S(1)} %pad_add_fusion.where_ref, s32[2,256]{1,0:T(2,128)S(1)} %copy-done.5, f32[16,4096]{1,0:T(8,128)S(1)} %copy-done.2), custom_call_target="tpu_custom_call" | custom-call | tf_op jit(solution)/shard_map/spread_low/pallas_call | solution.py:142
  4.5 12.9 %all-to-all-start = ((f32[32,2,16,128]{3,2,1,0:T(8,128)}), f32[32,2,16,128]{3,2,1,0:T(8,128)S(1)}, u32[]{:S(2)}, u32[]{:S(2)}) async-start(f32[32,2,16,128]{3,2,1,0:T(8,128)} %bitcast.4), calls=%async_computation | async-start | bytes 1048576 | tf_op jit(solution)/shard_map/all_to_all | solution.py:442
  18.3 7.2 %collective-permute-start = (f32[4,16,256]{2,1,0:T(8,128)S(1)}, f32[4,16,256]{2,1,0:T(8,128)S(1)}, u32[]{:S(2)}, u32[]{:S(2)}) collective-permute-start(f32[4,16,256]{2,1,0:T(8,128)S(1)} %bitcast.22), channel_id=1, source_target_pairs={{0,256},{1,257},{2,258},{3,259},{4,260},{5,261},{6,262},{7,263},{8... | collective-permute-start | bytes 196616 | tf_op jit(solution)/shard_map/ppermute | solution.py:453
  25.5 3.7 %collective-permute-done = f32[4,16,256]{2,1,0:T(8,128)S(1)} collective-permute-done((f32[4,16,256]{2,1,0:T(8,128)S(1)}, f32[4,16,256]{2,1,0:T(8,128)S(1)}, u32[]{:S(2)}, u32[]{:S(2)}) %collective-permute-start) | collective-permute-done | bytes 65568 | tf_op jit(solution)/shard_map/ppermute | solution.py:453
  34.6 1.9 %place_top.1.top_ref = f32[16,4,16,256]{3,2,1,0:T(8,128)} custom-call(s32[4]{0:T(128)S(1)} %pad_add_fusion.where_ref, s32[2,256]{1,0:T(2,128)S(1)} %copy-done.6, f32[32,2,16,128]{3,2,1,0:T(8,128)S(1)} %all-to-all-done.received_ref, f32[4,16,256]{2,1,0:T(8,128)S(1)} %broadcast_select_fusion.5.parent_ref), custom_call_target="tpu_custom_call" | custom-call | tf_op jit(solution)/shard_map/place_top/pallas_call | solution.py:142
  36.6 9.1 %all-to-all-start.1 = ((f32[16,4,16,256]{3,2,1,0:T(8,128)}), f32[16,4,16,256]{3,2,1,0:T(8,128)S(1)}, u32[]{:S(2)}, u32[]{:S(2)}) async-start(f32[16,4,16,256]{3,2,1,0:T(8,128)} %place_top.1.top_ref), calls=%async_computation.1 | async-start | bytes 2097152 | tf_op jit(solution)/shard_map/all_to_all | solution.py:442
  45.7 8.2 %collective-permute-start.6 = (f32[28,16,256]{2,1,0:T(8,128)S(1)}, f32[28,16,256]{2,1,0:T(8,128)S(1)}, u32[]{:S(2)}, u32[]{:S(2)}) collective-permute-start(f32[28,16,256]{2,1,0:T(8,128)S(1)} %bitcast.20), channel_id=1, source_target_pairs={{0,256},{1,257},{2,258},{3,259},{4,260},{5,261},{6,262},{7,263},{8... | collective-permute-start | bytes 1376264 | tf_op jit(solution)/shard_map/ppermute | solution.py:453
  53.9 5.2 %spread.1 = f32[64,16,128]{2,1,0:T(8,128)} custom-call(s32[4]{0:T(128)S(1)} %pad_add_fusion.where_ref, s32[2,256]{1,0:T(2,128)S(1)} %copy-done.6, f32[16,4096]{1,0:T(8,128)S(1)} %copy-done.3), custom_call_target="tpu_custom_call" | custom-call | tf_op jit(solution)/shard_map/spread/pallas_call | solution.py:142
  59.1 2.1 %collective-permute-done.6 = f32[28,16,256]{2,1,0:T(8,128)S(1)} collective-permute-done((f32[28,16,256]{2,1,0:T(8,128)S(1)}, f32[28,16,256]{2,1,0:T(8,128)S(1)}, u32[]{:S(2)}, u32[]{:S(2)}) %collective-permute-start.6) | collective-permute-done | bytes 458784 | tf_op jit(solution)/shard_map/ppermute | solution.py:453
  63.4 8.2 %all-to-all-done.1.pivots_ref = f32[16,4,16,256]{3,2,1,0:T(8,128)S(1)} async-done(((f32[16,4,16,256]{3,2,1,0:T(8,128)}), f32[16,4,16,256]{3,2,1,0:T(8,128)S(1)}, u32[]{:S(2)}, u32[]{:S(2)}) %all-to-all-start.1) | async-done | bytes 1048608 | tf_op jit(solution)/shard_map/all_to_all | solution.py:442
  72.4 2.5 %collective-permute-start.4 = (f32[512,256]{1,0:T(8,128)}, f32[512,256]{1,0:T(8,128)}, u32[]{:S(2)}, u32[]{:S(2)}) collective-permute-start(f32[512,256]{1,0:T(8,128)} %bitcast.6.own.refs_0_), channel_id=1, source_target_pairs={{0,32},{16,48},{32,0},{48,16},{1,33},{17,49},{33,1},{49,17},{2,34}... | collective-permute-start | bytes 1572872 | tf_op jit(solution)/shard_map/ppermute | solution.py:432
  76.1 3.5 %collective-permute-start.8 = (f32[28,16,256]{2,1,0:T(8,128)S(1)}, f32[28,16,256]{2,1,0:T(8,128)S(1)}, u32[]{:S(2)}, u32[]{:S(2)}) collective-permute-start(f32[28,16,256]{2,1,0:T(8,128)S(1)} %broadcast_select_fusion.1), channel_id=1, source_target_pairs={{0,64},{128,192},{256,320},{384,448},{1,65},{129,193},{257,321},{3... | collective-permute-start | bytes 1376264 | tf_op jit(solution)/shard_map/ppermute | solution.py:453
  79.6 7.4 %collective-permute-start.3 = (f32[512,256]{1,0:T(8,128)}, f32[512,256]{1,0:T(8,128)}, u32[]{:S(2)}, u32[]{:S(2)}) collective-permute-start(f32[512,256]{1,0:T(8,128)} %bitcast.6.own.refs_0_), channel_id=1, source_target_pairs={{0,16},{16,0},{32,48},{48,32},{1,17},{17,1},{33,49},{49,33},{2,18}... | collective-permute-start | bytes 1572872 | tf_op jit(solution)/shard_map/ppermute | solution.py:432
  86.9 3.9 %collective-permute-start.5 = (f32[512,256]{1,0:T(8,128)}, f32[512,256]{1,0:T(8,128)}, u32[]{:S(2)}, u32[]{:S(2)}) collective-permute-start(f32[512,256]{1,0:T(8,128)} %collective-permute-done.4.across.refs_2_), channel_id=1, source_target_pairs={{0,16},{16,0},{32,48},{48,32},{1,17},{17,1},{33,49},{49,33},{2,18}... | collective-permute-start | bytes 1572872 | tf_op jit(solution)/shard_map/ppermute | solution.py:432
  91.0 1.6 place_rest.1
  92.6 2.5 %collective-permute-start.10 = (f32[1024,256]{1,0:T(8,128)S(1)}, f32[1024,256]{1,0:T(8,128)}, u32[]{:S(2)}, u32[]{:S(2)}) collective-permute-start(f32[1024,256]{1,0:T(8,128)S(1)} %bitcast.16), channel_id=1, source_target_pairs={{0,32},{16,48},{32,0},{48,16},{1,33},{17,49},{33,1},{49,17},{2,34}... | collective-permute-start | bytes 3145736 | tf_op jit(solution)/shard_map/ppermute | solution.py:432
  95.1 2.2 %collective-permute-start.9 = (f32[1024,256]{1,0:T(8,128)S(1)}, f32[1024,256]{1,0:T(8,128)}, u32[]{:S(2)}, u32[]{:S(2)}) collective-permute-start(f32[1024,256]{1,0:T(8,128)S(1)} %bitcast.17), channel_id=1, source_target_pairs={{0,16},{16,0},{32,48},{48,32},{1,17},{17,1},{33,49},{49,33},{2,18}... | collective-permute-start | bytes 3145736 | tf_op jit(solution)/shard_map/ppermute | solution.py:432
  97.3 10.7 %all-to-all-start.2 = ((f32[32,2,16,128]{3,2,1,0:T(8,128)}), f32[32,2,16,128]{3,2,1,0:T(8,128)S(1)}, u32[]{:S(2)}, u32[]{:S(2)}) async-start(f32[32,2,16,128]{3,2,1,0:T(8,128)} %bitcast.9), calls=%async_computation.2 | async-start | bytes 1048576 | tf_op jit(solution)/shard_map/all_to_all | solution.py:442
  108.1 24.4 %first_factor.1.inv_hbm.inv0_hbm = f32[512,512]{1,0:T(8,128)} custom-call(s32[4]{0:T(128)} %copy-done.7, f32[512,256]{1,0:T(8,128)} %bitcast.6.own.refs_0_, f32[512,256]{1,0:T(8,128)} %collective-permute-done.3.core.refs_1_, f32[512,256]{1,0:T(8,128)} %collective-permute-done.4.across.refs_2_, f32[512,256]{1,0:T(8,128)} %collective-permute-done.5.both.refs_3_), custom_call_target="tpu_custom_call" | custom-call | flops 60000002048 | bytes 4194304 | tf_op jit(solution)/shard_map/first_factor/pallas_call | solution.py:276
  132.5 2.1 %collective-permute-start.11 = (f32[1024,256]{1,0:T(8,128)}, f32[1024,256]{1,0:T(8,128)}, u32[]{:S(2)}, u32[]{:S(2)}) collective-permute-start(f32[1024,256]{1,0:T(8,128)} %collective-permute-done.10.refs_6_), channel_id=1, source_target_pairs={{0,16},{16,0},{32,48},{48,32},{1,17},{17,1},{33,49},{49,33},{2,18}... | collective-permute-start | bytes 3145736 | tf_op jit(solution)/shard_map/ppermute | solution.py:432
  134.7 2.0 %place.1 = (f32[32,16,256]{2,1,0:T(8,128)S(1)}, f32[16,4,16,256]{3,2,1,0:T(8,128)}) custom-call(s32[4]{0:T(128)S(1)} %copy-done.8, s32[2,256]{1,0:T(2,128)S(1)} %copy-done.6, f32[32,2,16,128]{3,2,1,0:T(8,128)S(1)} %all-to-all-done.2.received_ref, f32[32,16,256]{2,1,0:T(8,128)S(1)} %bitcast.15), custom_call_target="tpu_custom_call" | custom-call | tf_op jit(solution)/shard_map/place/pallas_call | solution.py:142
  136.7 6.2 %all-to-all-start.3 = ((f32[16,4,16,256]{3,2,1,0:T(8,128)}), f32[16,4,16,256]{3,2,1,0:T(8,128)S(1)}, u32[]{:S(2)}, u32[]{:S(2)}) async-start(f32[16,4,16,256]{3,2,1,0:T(8,128)} %get-tuple-element.24), calls=%async_computation.3 | async-start | bytes 2097152 | tf_op jit(solution)/shard_map/all_to_all | solution.py:442
  142.9 27.4 %second_factor.1 = (f32[512,512]{1,0:T(8,128)}, f32[512,512]{1,0:T(8,128)}, f32[512,1024]{1,0:T(8,128)}) custom-call(s32[4]{0:T(128)} %copy-done.7, f32[512,512]{1,0:T(8,128)} %first_factor.1.inv_hbm.inv0_hbm, f32[512,256]{1,0:T(8,128)} %bitcast.6.own.refs_0_, f32[512,256]{1,0:T(8,128)} %collective-permute-done.3.core.refs_1_, ...), custom_call_target="tpu_custom_call" | custom-call | flops 60000002048 | bytes 8388608 | tf_op jit(solution)/shard_map/second_factor/pallas_call | solution.py:350
  171.3 8.4 %finish.1 = f32[32,16,256]{2,1,0:T(8,128)} custom-call(s32[4]{0:T(128)} %copy-done.7, f32[512,512]{1,0:T(8,128)} %first_factor.1.inv_hbm.inv0_hbm, f32[512,512]{1,0:T(8,128)} %get-tuple-element.21.inv1_hbm, f32[512,512]{1,0:T(8,128)} %get-tuple-element.22.x01_hbm, f32[16,64,256]{2,1,0:T(8,128)} %bitcast.19, f32[512,1024]{1,0:T(8,128)} %get-tuple-element.25.rows_hbm, ...), custom_call_target="tpu_custom_call" | custom-call | tf_op jit(solution)/shard_map/finish/pallas_call | solution.py:413
  (46 shorter events, 13.1 us)
Async XLA Ops:
  0.0 34.6 %copy-start.6 = (s32[2,256]{1,0:T(2,128)S(1)}, s32[2,256]{1,0:T(2,128)}, u32[]{:S(2)}) copy-start(s32[2,256]{1,0:T(2,128)} %map_ref.9) | copy-start | bytes 6148
  1.7 89.2 %copy-start.7 = (s32[4]{0:T(128)}, s32[4]{0:T(128)S(1)}, u32[]{:S(2)}) copy-start(s32[4]{0:T(128)S(1)} %pad_add_fusion.where_ref) | copy-start | bytes 52
  4.5 30.1 %all-to-all-start = ((f32[32,2,16,128]{3,2,1,0:T(8,128)}), f32[32,2,16,128]{3,2,1,0:T(8,128)S(1)}, u32[]{:S(2)}, u32[]{:S(2)}) async-start(f32[32,2,16,128]{3,2,1,0:T(8,128)} %bitcast.4), calls=%async_computation | async-start | bytes 1048576 | tf_op jit(solution)/shard_map/all_to_all | solution.py:442
  18.3 10.9 %collective-permute-start = (f32[4,16,256]{2,1,0:T(8,128)S(1)}, f32[4,16,256]{2,1,0:T(8,128)S(1)}, u32[]{:S(2)}, u32[]{:S(2)}) collective-permute-start(f32[4,16,256]{2,1,0:T(8,128)S(1)} %bitcast.22), channel_id=1, source_target_pairs={{0,256},{1,257},{2,258},{3,259},{4,260},{5,261},{6,262},{7,263},{8... | collective-permute-start | bytes 196616 | tf_op jit(solution)/shard_map/ppermute | solution.py:453
  29.2 16.5 %copy-start = (f32[16,1,32,256]{3,2,1,0:T(8,128)S(1)}, f32[16,1,32,256]{3,2,1,0:T(8,128)}, u32[]{:S(2)}) copy-start(f32[16,1,32,256]{3,2,1,0:T(8,128)} %param.3) | copy-start | bytes 1572868
  29.2 2.7 %collective-permute-start.1 = (f32[4,16,256]{2,1,0:T(8,128)S(1)}, f32[4,16,256]{2,1,0:T(8,128)S(1)}, u32[]{:S(2)}, u32[]{:S(2)}) collective-permute-start(f32[4,16,256]{2,1,0:T(8,128)S(1)} %broadcast_select_fusion.3), channel_id=1, source_target_pairs={{0,128},{256,384},{1,129},{257,385},{2,130},{258,386},{3,131},{259... | collective-permute-start | bytes 196616 | tf_op jit(solution)/shard_map/ppermute | solution.py:453
  32.0 2.6 %collective-permute-start.2 = (f32[4,16,256]{2,1,0:T(8,128)S(1)}, f32[4,16,256]{2,1,0:T(8,128)S(1)}, u32[]{:S(2)}, u32[]{:S(2)}) collective-permute-start(f32[4,16,256]{2,1,0:T(8,128)S(1)} %broadcast_select_fusion.4), channel_id=1, source_target_pairs={{0,64},{128,192},{256,320},{384,448},{1,65},{129,193},{257,321},{3... | collective-permute-start | bytes 196616 | tf_op jit(solution)/shard_map/ppermute | solution.py:453
  34.6 19.3 %copy-start.3 = (f32[16,4096]{1,0:T(8,128)S(1)}, f32[16,4096]{1,0:T(8,128)}, u32[]{:S(2)}) copy-start(f32[16,4096]{1,0:T(8,128)} %child_ref.2) | copy-start | bytes 786436
  36.6 35.0 %all-to-all-start.1 = ((f32[16,4,16,256]{3,2,1,0:T(8,128)}), f32[16,4,16,256]{3,2,1,0:T(8,128)S(1)}, u32[]{:S(2)}, u32[]{:S(2)}) async-start(f32[16,4,16,256]{3,2,1,0:T(8,128)} %place_top.1.top_ref), calls=%async_computation.1 | async-start | bytes 2097152 | tf_op jit(solution)/shard_map/all_to_all | solution.py:442
  45.7 15.5 %collective-permute-start.6 = (f32[28,16,256]{2,1,0:T(8,128)S(1)}, f32[28,16,256]{2,1,0:T(8,128)S(1)}, u32[]{:S(2)}, u32[]{:S(2)}) collective-permute-start(f32[28,16,256]{2,1,0:T(8,128)S(1)} %bitcast.20), channel_id=1, source_target_pairs={{0,256},{1,257},{2,258},{3,259},{4,260},{5,261},{6,262},{7,263},{8... | collective-permute-start | bytes 1376264 | tf_op jit(solution)/shard_map/ppermute | solution.py:453
  62.0 12.9 %collective-permute-start.7 = (f32[28,16,256]{2,1,0:T(8,128)}, f32[28,16,256]{2,1,0:T(8,128)S(1)}, u32[]{:S(2)}, u32[]{:S(2)}) collective-permute-start(f32[28,16,256]{2,1,0:T(8,128)} %broadcast_select_fusion), channel_id=1, source_target_pairs={{0,128},{256,384},{1,129},{257,385},{2,130},{258,386},{3,131},{259... | collective-permute-start | bytes 1376264 | tf_op jit(solution)/shard_map/ppermute | solution.py:453
  72.4 14.5 %collective-permute-start.4 = (f32[512,256]{1,0:T(8,128)}, f32[512,256]{1,0:T(8,128)}, u32[]{:S(2)}, u32[]{:S(2)}) collective-permute-start(f32[512,256]{1,0:T(8,128)} %bitcast.6.own.refs_0_), channel_id=1, source_target_pairs={{0,32},{16,48},{32,0},{48,16},{1,33},{17,49},{33,1},{49,17},{2,34}... | collective-permute-start | bytes 1572872 | tf_op jit(solution)/shard_map/ppermute | solution.py:432
  76.1 14.8 %collective-permute-start.8 = (f32[28,16,256]{2,1,0:T(8,128)S(1)}, f32[28,16,256]{2,1,0:T(8,128)S(1)}, u32[]{:S(2)}, u32[]{:S(2)}) collective-permute-start(f32[28,16,256]{2,1,0:T(8,128)S(1)} %broadcast_select_fusion.1), channel_id=1, source_target_pairs={{0,64},{128,192},{256,320},{384,448},{1,65},{129,193},{257,321},{3... | collective-permute-start | bytes 1376264 | tf_op jit(solution)/shard_map/ppermute | solution.py:453
  79.6 28.5 %collective-permute-start.3 = (f32[512,256]{1,0:T(8,128)}, f32[512,256]{1,0:T(8,128)}, u32[]{:S(2)}, u32[]{:S(2)}) collective-permute-start(f32[512,256]{1,0:T(8,128)} %bitcast.6.own.refs_0_), channel_id=1, source_target_pairs={{0,16},{16,0},{32,48},{48,32},{1,17},{17,1},{33,49},{49,33},{2,18}... | collective-permute-start | bytes 1572872 | tf_op jit(solution)/shard_map/ppermute | solution.py:432
  86.9 21.1 %collective-permute-start.5 = (f32[512,256]{1,0:T(8,128)}, f32[512,256]{1,0:T(8,128)}, u32[]{:S(2)}, u32[]{:S(2)}) collective-permute-start(f32[512,256]{1,0:T(8,128)} %collective-permute-done.4.across.refs_2_), channel_id=1, source_target_pairs={{0,16},{16,0},{32,48},{48,32},{1,17},{17,1},{33,49},{49,33},{2,18}... | collective-permute-start | bytes 1572872 | tf_op jit(solution)/shard_map/ppermute | solution.py:432
  92.6 39.9 %copy-start.1 = (f32[64,16,256]{2,1,0:T(8,128)}, f32[64,16,256]{2,1,0:T(8,128)S(1)}, u32[]{:S(2)}) copy-start(f32[64,16,256]{2,1,0:T(8,128)S(1)} %place_rest.1) | copy-start | bytes 3145732
  92.6 40.0 %collective-permute-start.10 = (f32[1024,256]{1,0:T(8,128)S(1)}, f32[1024,256]{1,0:T(8,128)}, u32[]{:S(2)}, u32[]{:S(2)}) collective-permute-start(f32[1024,256]{1,0:T(8,128)S(1)} %bitcast.16), channel_id=1, source_target_pairs={{0,32},{16,48},{32,0},{48,16},{1,33},{17,49},{33,1},{49,17},{2,34}... | collective-permute-start | bytes 3145736 | tf_op jit(solution)/shard_map/ppermute | solution.py:432
  95.1 47.8 %collective-permute-start.9 = (f32[1024,256]{1,0:T(8,128)S(1)}, f32[1024,256]{1,0:T(8,128)}, u32[]{:S(2)}, u32[]{:S(2)}) collective-permute-start(f32[1024,256]{1,0:T(8,128)S(1)} %bitcast.17), channel_id=1, source_target_pairs={{0,16},{16,0},{32,48},{48,32},{1,17},{17,1},{33,49},{49,33},{2,18}... | collective-permute-start | bytes 3145736 | tf_op jit(solution)/shard_map/ppermute | solution.py:432
  97.3 35.2 %all-to-all-start.2 = ((f32[32,2,16,128]{3,2,1,0:T(8,128)}), f32[32,2,16,128]{3,2,1,0:T(8,128)S(1)}, u32[]{:S(2)}, u32[]{:S(2)}) async-start(f32[32,2,16,128]{3,2,1,0:T(8,128)} %bitcast.9), calls=%async_computation.2 | async-start | bytes 1048576 | tf_op jit(solution)/shard_map/all_to_all | solution.py:442
  108.0 26.6 %copy-start.8 = (s32[4]{0:T(128)S(1)}, s32[4]{0:T(128)}, u32[]{:S(2)}) copy-start(s32[4]{0:T(128)} %copy-done.7) | copy-start | bytes 52
  132.5 10.4 %collective-permute-start.11 = (f32[1024,256]{1,0:T(8,128)}, f32[1024,256]{1,0:T(8,128)}, u32[]{:S(2)}, u32[]{:S(2)}) collective-permute-start(f32[1024,256]{1,0:T(8,128)} %collective-permute-done.10.refs_6_), channel_id=1, source_target_pairs={{0,16},{16,0},{32,48},{48,32},{1,17},{17,1},{33,49},{49,33},{2,18}... | collective-permute-start | bytes 3145736 | tf_op jit(solution)/shard_map/ppermute | solution.py:432
  136.7 33.6 %copy-start.4 = (f32[32,16,256]{2,1,0:T(8,128)}, f32[32,16,256]{2,1,0:T(8,128)S(1)}, u32[]{:S(2)}) copy-start(f32[32,16,256]{2,1,0:T(8,128)S(1)} %get-tuple-element.26.front_hbm) | copy-start | bytes 1572868
  136.7 33.6 %all-to-all-start.3 = ((f32[16,4,16,256]{3,2,1,0:T(8,128)}), f32[16,4,16,256]{3,2,1,0:T(8,128)S(1)}, u32[]{:S(2)}, u32[]{:S(2)}) async-start(f32[16,4,16,256]{3,2,1,0:T(8,128)} %get-tuple-element.24), calls=%async_computation.3 | async-start | bytes 2097152 | tf_op jit(solution)/shard_map/all_to_all | solution.py:442
  170.3 1.0 copy-start.9
  (2 other events, 1.6 us)

commit v9 on v8

--- a/solution.py
+++ b/solution.py
@@ -60,7 +60,9 @@
     lax.fori_loop(0, child_ref.shape[1] // TILE, body, 0)
 
 
-def spread_low_kernel(where_ref, map_ref, child_ref, out_ref, from_ref):
+def spread_low_kernel(where_ref, map_ref, child_hbm, out_ref, from_ref, child_ref, sems):
+    copy = pltpu.make_async_copy(child_hbm, child_ref, sems.at[0])
+    copy.start()
     child = where_ref[0]
     part = TILE // BLK
     count = 2 * ROWS
@@ -76,6 +78,7 @@
 
     lax.fori_loop(0, count * part, clear, 0, unroll=8)
     lax.fori_loop(0, map_ref.shape[1], note, 0, unroll=8)
+    copy.wait()
     for target in range(count):
         tile = jnp.zeros((BLK, TILE), jnp.float32)
         for place in range(part):
@@ -137,16 +140,14 @@
 TOPS = jax.ShapeDtypeStruct((COLS, TOP, BLK, WIDE), jnp.float32)
 
 
-def call(kernel, out_shape, operands, mib, scratch=(), flops=None):
-    cost = flops and pl.CostEstimate(flops=flops, bytes_accessed=4 << 20, transcendentals=0)
+def call(kernel, out_shape, operands, mib, scratch=(), big=VMEM):
     return pl.pallas_call(
         kernel,
         out_shape=out_shape,
-        in_specs=[SMEM, SMEM] + [VMEM] * (len(operands) - 2),
+        in_specs=[SMEM, SMEM] + [big] * (len(operands) - 2),
         out_specs=jax.tree.map(lambda _: VMEM, out_shape),
         scratch_shapes=list(scratch),
         compiler_params=params(mib),
-        cost_estimate=cost,
         name=kernel.__name__.removesuffix("_kernel"),
     )(*operands)
 
@@ -468,8 +469,13 @@
         spread_low_kernel,
         jax.ShapeDtypeStruct((SUBS, 2 * ROWS, BLK, TILE), jnp.float32),
         (where, index_map, child_schur),
-        4,
-        [pltpu.SMEM((2 * SHARDS * TILE // BLK,), jnp.int32)],
+        60,
+        [
+            pltpu.SMEM((2 * SHARDS * TILE // BLK,), jnp.int32),
+            pltpu.VMEM(child_schur.shape, child_schur.dtype),
+            pltpu.SemaphoreType.DMA((1,)),
+        ],
+        big=HBM,
     )
     low = exchange(low.reshape(SHARDS, 2, BLK, TILE), ("sub", "row"))
     tops = call(place_top_kernel, TOPS, (where, index_map, low, parent_top), 6, SOURCES)

time: 183 us -> 182 us (level)
  transfers between devices with their start and end apart: 16 -> 16, of which waited for: 5 -> 5; matrix products, arithmetic and copies ran while one was open for 2% -> 1% of each run, Pallas kernels for 34% -> 34%
where the time goes in v9:
time: 182 us; the launch traced here: 179 us
  starting transfers between devices  83.2 us (46%)
  Pallas kernels  74 us (41%)
  waiting for transfers between devices  17.4 us (10%)
  local copies, waits for them, and re-layouts  2.72 us (1%)
    all_to_all x4, starting transfers between devices, exchange(): return lax.all_to_all(x, axis, split_axis=0, concat_axis=0, tiled=True)  38.6 us
    pallas_call x1, Pallas kernels, second_factor(): pl.pallas_call(second_kernel, out_shape=(shape, shape, jax.ShapeDtypeStru...  27.4 us
    pallas_call x1, Pallas kernels, first_factor(): pl.pallas_call(first_kernel, out_shape=jax.ShapeDtypeStruct((PANEL, PANEL...  24.4 us
    ppermute x6, starting transfers between devices, from_first(): got = lax.ppermute(x, 'sub', pairs)  22.9 us
    ppermute x6, starting transfers between devices, swap(): return lax.ppermute(x, axis, [(i, i ^ bit) for i in range(ROWS)])  21.7 us
    pallas_call x5, Pallas kernels, call(): pl.pallas_call(kernel, out_shape=out_shape, in_specs=[SMEM, SMEM] + [big]...  13.8 us
    all_to_all x4, waiting for transfers between devices, exchange(): return lax.all_to_all(x, axis, split_axis=0, concat_axis=0, tiled=True)  8.99 us
    pallas_call x1, Pallas kernels, finish(): pl.pallas_call(finish_kernel, out_shape=FRONT, in_specs=[SMEM] + [HBM] *...  8.37 us
  transfers between devices with their start and end apart: 16, of which 5 were waited for; matrix products, arithmetic and copies ran while one was open for 1% of the time, Pallas kernels for 34%

profile of v9, /device:TPU:1, one launch (start us, length us, event | category | flops | bytes accessed | tf_op | source)
XLA Modules:
  0.0 178.7 jit_solution(7296619826384760927)
XLA Ops:
  0.6 3.1 %spread_low.1 = f32[8,8,16,128]{3,2,1,0:T(8,128)} custom-call(s32[4]{0:T(128)} %pad_add_fusion.where_ref, s32[2,256]{1,0:T(2,128)} %map_ref.9, f32[16,4096]{1,0:T(8,128)} %child_ref), custom_call_target="tpu_custom_call" | custom-call | tf_op jit(solution)/shard_map/spread_low/pallas_call | solution.py:144
  3.7 12.9 %all-to-all-start = ((f32[32,2,16,128]{3,2,1,0:T(8,128)}), f32[32,2,16,128]{3,2,1,0:T(8,128)S(1)}, u32[]{:S(2)}, u32[]{:S(2)}) async-start(f32[32,2,16,128]{3,2,1,0:T(8,128)} %bitcast.20), calls=%async_computation | async-start | bytes 1048576 | tf_op jit(solution)/shard_map/all_to_all | solution.py:443
  17.4 7.2 %collective-permute-start = (f32[4,16,256]{2,1,0:T(8,128)S(1)}, f32[4,16,256]{2,1,0:T(8,128)S(1)}, u32[]{:S(2)}, u32[]{:S(2)}) collective-permute-start(f32[4,16,256]{2,1,0:T(8,128)S(1)} %bitcast.23), channel_id=1, source_target_pairs={{0,256},{1,257},{2,258},{3,259},{4,260},{5,261},{6,262},{7,263},{8... | collective-permute-start | bytes 196616 | tf_op jit(solution)/shard_map/ppermute | solution.py:454
  24.6 3.7 %collective-permute-done = f32[4,16,256]{2,1,0:T(8,128)S(1)} collective-permute-done((f32[4,16,256]{2,1,0:T(8,128)S(1)}, f32[4,16,256]{2,1,0:T(8,128)S(1)}, u32[]{:S(2)}, u32[]{:S(2)}) %collective-permute-start) | collective-permute-done | bytes 65568 | tf_op jit(solution)/shard_map/ppermute | solution.py:454
  33.8 2.0 %place_top.1.top_ref = f32[16,4,16,256]{3,2,1,0:T(8,128)} custom-call(s32[4]{0:T(128)S(1)} %copy-done.5, s32[2,256]{1,0:T(2,128)S(1)} %copy-done.4, f32[32,2,16,128]{3,2,1,0:T(8,128)S(1)} %all-to-all-done.received_ref, f32[4,16,256]{2,1,0:T(8,128)S(1)} %broadcast_select_fusion.5.parent_ref), custom_call_target="tpu_custom_call" | custom-call | tf_op jit(solution)/shard_map/place_top/pallas_call | solution.py:144
  35.7 9.1 %all-to-all-start.1 = ((f32[16,4,16,256]{3,2,1,0:T(8,128)}), f32[16,4,16,256]{3,2,1,0:T(8,128)S(1)}, u32[]{:S(2)}, u32[]{:S(2)}) async-start(f32[16,4,16,256]{3,2,1,0:T(8,128)} %place_top.1.top_ref), calls=%async_computation.1 | async-start | bytes 2097152 | tf_op jit(solution)/shard_map/all_to_all | solution.py:443
  44.9 8.2 %collective-permute-start.6 = (f32[28,16,256]{2,1,0:T(8,128)S(1)}, f32[28,16,256]{2,1,0:T(8,128)S(1)}, u32[]{:S(2)}, u32[]{:S(2)}) collective-permute-start(f32[28,16,256]{2,1,0:T(8,128)S(1)} %bitcast.21), channel_id=1, source_target_pairs={{0,256},{1,257},{2,258},{3,259},{4,260},{5,261},{6,262},{7,263},{8... | collective-permute-start | bytes 1376264 | tf_op jit(solution)/shard_map/ppermute | solution.py:454
  53.1 5.2 %spread.1 = f32[64,16,128]{2,1,0:T(8,128)} custom-call(s32[4]{0:T(128)S(1)} %copy-done.5, s32[2,256]{1,0:T(2,128)S(1)} %copy-done.4, f32[16,4096]{1,0:T(8,128)S(1)} %copy-done.2), custom_call_target="tpu_custom_call" | custom-call | tf_op jit(solution)/shard_map/spread/pallas_call | solution.py:144
  58.3 2.1 %collective-permute-done.6 = f32[28,16,256]{2,1,0:T(8,128)S(1)} collective-permute-done((f32[28,16,256]{2,1,0:T(8,128)S(1)}, f32[28,16,256]{2,1,0:T(8,128)S(1)}, u32[]{:S(2)}, u32[]{:S(2)}) %collective-permute-start.6) | collective-permute-done | bytes 458784 | tf_op jit(solution)/shard_map/ppermute | solution.py:454
  61.8 9.0 %all-to-all-done.1.pivots_ref = f32[16,4,16,256]{3,2,1,0:T(8,128)S(1)} async-done(((f32[16,4,16,256]{3,2,1,0:T(8,128)}), f32[16,4,16,256]{3,2,1,0:T(8,128)S(1)}, u32[]{:S(2)}, u32[]{:S(2)}) %all-to-all-start.1) | async-done | bytes 1048608 | tf_op jit(solution)/shard_map/all_to_all | solution.py:443
  71.6 2.5 %collective-permute-start.4 = (f32[512,256]{1,0:T(8,128)}, f32[512,256]{1,0:T(8,128)}, u32[]{:S(2)}, u32[]{:S(2)}) collective-permute-start(f32[512,256]{1,0:T(8,128)} %bitcast.6.own.refs_0_), channel_id=1, source_target_pairs={{0,32},{16,48},{32,0},{48,16},{1,33},{17,49},{33,1},{49,17},{2,34}... | collective-permute-start | bytes 1572872 | tf_op jit(solution)/shard_map/ppermute | solution.py:433
  74.2 3.5 %collective-permute-start.8 = (f32[28,16,256]{2,1,0:T(8,128)S(1)}, f32[28,16,256]{2,1,0:T(8,128)S(1)}, u32[]{:S(2)}, u32[]{:S(2)}) collective-permute-start(f32[28,16,256]{2,1,0:T(8,128)S(1)} %broadcast_select_fusion.1), channel_id=1, source_target_pairs={{0,64},{128,192},{256,320},{384,448},{1,65},{129,193},{257,321},{3... | collective-permute-start | bytes 1376264 | tf_op jit(solution)/shard_map/ppermute | solution.py:454
  77.7 7.4 %collective-permute-start.3 = (f32[512,256]{1,0:T(8,128)}, f32[512,256]{1,0:T(8,128)}, u32[]{:S(2)}, u32[]{:S(2)}) collective-permute-start(f32[512,256]{1,0:T(8,128)} %bitcast.6.own.refs_0_), channel_id=1, source_target_pairs={{0,16},{16,0},{32,48},{48,32},{1,17},{17,1},{33,49},{49,33},{2,18}... | collective-permute-start | bytes 1572872 | tf_op jit(solution)/shard_map/ppermute | solution.py:433
  85.1 4.9 %collective-permute-start.5 = (f32[512,256]{1,0:T(8,128)}, f32[512,256]{1,0:T(8,128)}, u32[]{:S(2)}, u32[]{:S(2)}) collective-permute-start(f32[512,256]{1,0:T(8,128)} %collective-permute-done.4.across.refs_2_), channel_id=1, source_target_pairs={{0,16},{16,0},{32,48},{48,32},{1,17},{17,1},{33,49},{49,33},{2,18}... | collective-permute-start | bytes 1572872 | tf_op jit(solution)/shard_map/ppermute | solution.py:433
  90.1 1.6 place_rest.1
  91.7 2.5 %collective-permute-start.10 = (f32[1024,256]{1,0:T(8,128)S(1)}, f32[1024,256]{1,0:T(8,128)}, u32[]{:S(2)}, u32[]{:S(2)}) collective-permute-start(f32[1024,256]{1,0:T(8,128)S(1)} %bitcast.16), channel_id=1, source_target_pairs={{0,32},{16,48},{32,0},{48,16},{1,33},{17,49},{33,1},{49,17},{2,34}... | collective-permute-start | bytes 3145736 | tf_op jit(solution)/shard_map/ppermute | solution.py:433
  94.2 2.2 %collective-permute-start.9 = (f32[1024,256]{1,0:T(8,128)S(1)}, f32[1024,256]{1,0:T(8,128)}, u32[]{:S(2)}, u32[]{:S(2)}) collective-permute-start(f32[1024,256]{1,0:T(8,128)S(1)} %bitcast.17), channel_id=1, source_target_pairs={{0,16},{16,0},{32,48},{48,32},{1,17},{17,1},{33,49},{49,33},{2,18}... | collective-permute-start | bytes 3145736 | tf_op jit(solution)/shard_map/ppermute | solution.py:433
  96.5 10.0 %all-to-all-start.2 = ((f32[32,2,16,128]{3,2,1,0:T(8,128)}), f32[32,2,16,128]{3,2,1,0:T(8,128)S(1)}, u32[]{:S(2)}, u32[]{:S(2)}) async-start(f32[32,2,16,128]{3,2,1,0:T(8,128)} %bitcast.9), calls=%async_computation.2 | async-start | bytes 1048576 | tf_op jit(solution)/shard_map/all_to_all | solution.py:443
  106.5 24.4 %first_factor.1.inv_hbm.inv0_hbm = f32[512,512]{1,0:T(8,128)} custom-call(s32[4]{0:T(128)} %pad_add_fusion.where_ref, f32[512,256]{1,0:T(8,128)} %bitcast.6.own.refs_0_, f32[512,256]{1,0:T(8,128)} %collective-permute-done.3.core.refs_1_, f32[512,256]{1,0:T(8,128)} %collective-permute-done.4.across.refs_2_, f32[512,256]{1,0:T(8,128)} %collective-permute-done.5.both.refs_3_), custom_call_target="tpu_custom_call" | custom-call | flops 60000002048 | bytes 4194304 | tf_op jit(solution)/shard_map/first_factor/pallas_call | solution.py:277
  130.9 2.1 %collective-permute-start.11 = (f32[1024,256]{1,0:T(8,128)}, f32[1024,256]{1,0:T(8,128)}, u32[]{:S(2)}, u32[]{:S(2)}) collective-permute-start(f32[1024,256]{1,0:T(8,128)} %collective-permute-done.10.refs_6_), channel_id=1, source_target_pairs={{0,16},{16,0},{32,48},{48,32},{1,17},{17,1},{33,49},{49,33},{2,18}... | collective-permute-start | bytes 3145736 | tf_op jit(solution)/shard_map/ppermute | solution.py:433
  133.1 2.0 %place.1 = (f32[32,16,256]{2,1,0:T(8,128)S(1)}, f32[16,4,16,256]{3,2,1,0:T(8,128)}) custom-call(s32[4]{0:T(128)S(1)} %copy-done.6, s32[2,256]{1,0:T(2,128)S(1)} %copy-done.4, f32[32,2,16,128]{3,2,1,0:T(8,128)S(1)} %all-to-all-done.2.received_ref, f32[32,16,256]{2,1,0:T(8,128)S(1)} %bitcast.15), custom_call_target="tpu_custom_call" | custom-call | tf_op jit(solution)/shard_map/place/pallas_call | solution.py:144
  135.1 6.7 %all-to-all-start.3 = ((f32[16,4,16,256]{3,2,1,0:T(8,128)}), f32[16,4,16,256]{3,2,1,0:T(8,128)S(1)}, u32[]{:S(2)}, u32[]{:S(2)}) async-start(f32[16,4,16,256]{3,2,1,0:T(8,128)} %get-tuple-element.24), calls=%async_computation.3 | async-start | bytes 2097152 | tf_op jit(solution)/shard_map/all_to_all | solution.py:443
  141.7 27.4 %second_factor.1 = (f32[512,512]{1,0:T(8,128)}, f32[512,512]{1,0:T(8,128)}, f32[512,1024]{1,0:T(8,128)}) custom-call(s32[4]{0:T(128)} %pad_add_fusion.where_ref, f32[512,512]{1,0:T(8,128)} %first_factor.1.inv_hbm.inv0_hbm, f32[512,256]{1,0:T(8,128)} %bitcast.6.own.refs_0_, f32[512,256]{1,0:T(8,128)} %collective-permute-done.3.core.refs_1_, ...), custom_call_target="tpu_custom_call" | custom-call | flops 60000002048 | bytes 8388608 | tf_op jit(solution)/shard_map/second_factor/pallas_call | solution.py:351
  170.2 8.4 %finish.1 = f32[32,16,256]{2,1,0:T(8,128)} custom-call(s32[4]{0:T(128)} %pad_add_fusion.where_ref, f32[512,512]{1,0:T(8,128)} %first_factor.1.inv_hbm.inv0_hbm, f32[512,512]{1,0:T(8,128)} %get-tuple-element.21.inv1_hbm, f32[512,512]{1,0:T(8,128)} %get-tuple-element.22.x01_hbm, f32[16,64,256]{2,1,0:T(8,128)} %bitcast.19, ...), custom_call_target="tpu_custom_call" | custom-call | tf_op jit(solution)/shard_map/finish/pallas_call | solution.py:414
  (42 shorter events, 10.2 us)
Async XLA Ops:
  0.0 33.8 %copy-start.4 = (s32[2,256]{1,0:T(2,128)S(1)}, s32[2,256]{1,0:T(2,128)}, u32[]{:S(2)}) copy-start(s32[2,256]{1,0:T(2,128)} %map_ref.9) | copy-start | bytes 6148
  0.6 33.2 %copy-start.5 = (s32[4]{0:T(128)S(1)}, s32[4]{0:T(128)}, u32[]{:S(2)}) copy-start(s32[4]{0:T(128)} %pad_add_fusion.where_ref) | copy-start | bytes 52
  3.7 30.1 %all-to-all-start = ((f32[32,2,16,128]{3,2,1,0:T(8,128)}), f32[32,2,16,128]{3,2,1,0:T(8,128)S(1)}, u32[]{:S(2)}, u32[]{:S(2)}) async-start(f32[32,2,16,128]{3,2,1,0:T(8,128)} %bitcast.20), calls=%async_computation | async-start | bytes 1048576 | tf_op jit(solution)/shard_map/all_to_all | solution.py:443
  17.4 10.9 %collective-permute-start = (f32[4,16,256]{2,1,0:T(8,128)S(1)}, f32[4,16,256]{2,1,0:T(8,128)S(1)}, u32[]{:S(2)}, u32[]{:S(2)}) collective-permute-start(f32[4,16,256]{2,1,0:T(8,128)S(1)} %bitcast.23), channel_id=1, source_target_pairs={{0,256},{1,257},{2,258},{3,259},{4,260},{5,261},{6,262},{7,263},{8... | collective-permute-start | bytes 196616 | tf_op jit(solution)/shard_map/ppermute | solution.py:454
  28.3 16.5 %copy-start = (f32[16,1,32,256]{3,2,1,0:T(8,128)S(1)}, f32[16,1,32,256]{3,2,1,0:T(8,128)}, u32[]{:S(2)}) copy-start(f32[16,1,32,256]{3,2,1,0:T(8,128)} %param.3) | copy-start | bytes 1572868
  28.4 2.7 %collective-permute-start.1 = (f32[4,16,256]{2,1,0:T(8,128)S(1)}, f32[4,16,256]{2,1,0:T(8,128)S(1)}, u32[]{:S(2)}, u32[]{:S(2)}) collective-permute-start(f32[4,16,256]{2,1,0:T(8,128)S(1)} %broadcast_select_fusion.3), channel_id=1, source_target_pairs={{0,128},{256,384},{1,129},{257,385},{2,130},{258,386},{3,131},{259... | collective-permute-start | bytes 196616 | tf_op jit(solution)/shard_map/ppermute | solution.py:454
  31.1 2.6 %collective-permute-start.2 = (f32[4,16,256]{2,1,0:T(8,128)S(1)}, f32[4,16,256]{2,1,0:T(8,128)S(1)}, u32[]{:S(2)}, u32[]{:S(2)}) collective-permute-start(f32[4,16,256]{2,1,0:T(8,128)S(1)} %broadcast_select_fusion.4), channel_id=1, source_target_pairs={{0,64},{128,192},{256,320},{384,448},{1,65},{129,193},{257,321},{3... | collective-permute-start | bytes 196616 | tf_op jit(solution)/shard_map/ppermute | solution.py:454
  33.7 19.3 %copy-start.2 = (f32[16,4096]{1,0:T(8,128)S(1)}, f32[16,4096]{1,0:T(8,128)}, u32[]{:S(2)}) copy-start(f32[16,4096]{1,0:T(8,128)} %child_ref) | copy-start | bytes 786436
  35.7 35.0 %all-to-all-start.1 = ((f32[16,4,16,256]{3,2,1,0:T(8,128)}), f32[16,4,16,256]{3,2,1,0:T(8,128)S(1)}, u32[]{:S(2)}, u32[]{:S(2)}) async-start(f32[16,4,16,256]{3,2,1,0:T(8,128)} %place_top.1.top_ref), calls=%async_computation.1 | async-start | bytes 2097152 | tf_op jit(solution)/shard_map/all_to_all | solution.py:443
  44.9 15.5 %collective-permute-start.6 = (f32[28,16,256]{2,1,0:T(8,128)S(1)}, f32[28,16,256]{2,1,0:T(8,128)S(1)}, u32[]{:S(2)}, u32[]{:S(2)}) collective-permute-start(f32[28,16,256]{2,1,0:T(8,128)S(1)} %bitcast.21), channel_id=1, source_target_pairs={{0,256},{1,257},{2,258},{3,259},{4,260},{5,261},{6,262},{7,263},{8... | collective-permute-start | bytes 1376264 | tf_op jit(solution)/shard_map/ppermute | solution.py:454
  60.4 13.7 %collective-permute-start.7 = (f32[28,16,256]{2,1,0:T(8,128)S(1)}, f32[28,16,256]{2,1,0:T(8,128)S(1)}, u32[]{:S(2)}, u32[]{:S(2)}) collective-permute-start(f32[28,16,256]{2,1,0:T(8,128)S(1)} %broadcast_select_fusion), channel_id=1, source_target_pairs={{0,128},{256,384},{1,129},{257,385},{2,130},{258,386},{3,131},{259... | collective-permute-start | bytes 1376264 | tf_op jit(solution)/shard_map/ppermute | solution.py:454
  71.6 13.5 %collective-permute-start.4 = (f32[512,256]{1,0:T(8,128)}, f32[512,256]{1,0:T(8,128)}, u32[]{:S(2)}, u32[]{:S(2)}) collective-permute-start(f32[512,256]{1,0:T(8,128)} %bitcast.6.own.refs_0_), channel_id=1, source_target_pairs={{0,32},{16,48},{32,0},{48,16},{1,33},{17,49},{33,1},{49,17},{2,34}... | collective-permute-start | bytes 1572872 | tf_op jit(solution)/shard_map/ppermute | solution.py:433
  74.2 15.8 %collective-permute-start.8 = (f32[28,16,256]{2,1,0:T(8,128)S(1)}, f32[28,16,256]{2,1,0:T(8,128)S(1)}, u32[]{:S(2)}, u32[]{:S(2)}) collective-permute-start(f32[28,16,256]{2,1,0:T(8,128)S(1)} %broadcast_select_fusion.1), channel_id=1, source_target_pairs={{0,64},{128,192},{256,320},{384,448},{1,65},{129,193},{257,321},{3... | collective-permute-start | bytes 1376264 | tf_op jit(solution)/shard_map/ppermute | solution.py:454
  77.7 28.8 %collective-permute-start.3 = (f32[512,256]{1,0:T(8,128)}, f32[512,256]{1,0:T(8,128)}, u32[]{:S(2)}, u32[]{:S(2)}) collective-permute-start(f32[512,256]{1,0:T(8,128)} %bitcast.6.own.refs_0_), channel_id=1, source_target_pairs={{0,16},{16,0},{32,48},{48,32},{1,17},{17,1},{33,49},{49,33},{2,18}... | collective-permute-start | bytes 1572872 | tf_op jit(solution)/shard_map/ppermute | solution.py:433
  85.1 21.4 %collective-permute-start.5 = (f32[512,256]{1,0:T(8,128)}, f32[512,256]{1,0:T(8,128)}, u32[]{:S(2)}, u32[]{:S(2)}) collective-permute-start(f32[512,256]{1,0:T(8,128)} %collective-permute-done.4.across.refs_2_), channel_id=1, source_target_pairs={{0,16},{16,0},{32,48},{48,32},{1,17},{17,1},{33,49},{49,33},{2,18}... | collective-permute-start | bytes 1572872 | tf_op jit(solution)/shard_map/ppermute | solution.py:433
  91.7 39.2 %copy-start.1 = (f32[64,16,256]{2,1,0:T(8,128)}, f32[64,16,256]{2,1,0:T(8,128)S(1)}, u32[]{:S(2)}) copy-start(f32[64,16,256]{2,1,0:T(8,128)S(1)} %place_rest.1) | copy-start | bytes 3145732
  91.7 39.2 %collective-permute-start.10 = (f32[1024,256]{1,0:T(8,128)S(1)}, f32[1024,256]{1,0:T(8,128)}, u32[]{:S(2)}, u32[]{:S(2)}) collective-permute-start(f32[1024,256]{1,0:T(8,128)S(1)} %bitcast.16), channel_id=1, source_target_pairs={{0,32},{16,48},{32,0},{48,16},{1,33},{17,49},{33,1},{49,17},{2,34}... | collective-permute-start | bytes 3145736 | tf_op jit(solution)/shard_map/ppermute | solution.py:433
  94.2 47.5 %collective-permute-start.9 = (f32[1024,256]{1,0:T(8,128)S(1)}, f32[1024,256]{1,0:T(8,128)}, u32[]{:S(2)}, u32[]{:S(2)}) collective-permute-start(f32[1024,256]{1,0:T(8,128)S(1)} %bitcast.17), channel_id=1, source_target_pairs={{0,16},{16,0},{32,48},{48,32},{1,17},{17,1},{33,49},{49,33},{2,18}... | collective-permute-start | bytes 3145736 | tf_op jit(solution)/shard_map/ppermute | solution.py:433
  96.5 34.4 %all-to-all-start.2 = ((f32[32,2,16,128]{3,2,1,0:T(8,128)}), f32[32,2,16,128]{3,2,1,0:T(8,128)S(1)}, u32[]{:S(2)}, u32[]{:S(2)}) async-start(f32[32,2,16,128]{3,2,1,0:T(8,128)} %bitcast.9), calls=%async_computation.2 | async-start | bytes 1048576 | tf_op jit(solution)/shard_map/all_to_all | solution.py:443
  106.4 26.6 %copy-start.6 = (s32[4]{0:T(128)S(1)}, s32[4]{0:T(128)}, u32[]{:S(2)}) copy-start(s32[4]{0:T(128)} %pad_add_fusion.where_ref) | copy-start | bytes 52
  130.9 10.8 %collective-permute-start.11 = (f32[1024,256]{1,0:T(8,128)}, f32[1024,256]{1,0:T(8,128)}, u32[]{:S(2)}, u32[]{:S(2)}) collective-permute-start(f32[1024,256]{1,0:T(8,128)} %collective-permute-done.10.refs_6_), channel_id=1, source_target_pairs={{0,16},{16,0},{32,48},{48,32},{1,17},{17,1},{33,49},{49,33},{2,18}... | collective-permute-start | bytes 3145736 | tf_op jit(solution)/shard_map/ppermute | solution.py:433
  135.1 34.1 %copy-start.3 = (f32[32,16,256]{2,1,0:T(8,128)}, f32[32,16,256]{2,1,0:T(8,128)S(1)}, u32[]{:S(2)}) copy-start(f32[32,16,256]{2,1,0:T(8,128)S(1)} %get-tuple-element.26.front_hbm) | copy-start | bytes 1572868
  135.1 34.1 %all-to-all-start.3 = ((f32[16,4,16,256]{3,2,1,0:T(8,128)}), f32[16,4,16,256]{3,2,1,0:T(8,128)S(1)}, u32[]{:S(2)}, u32[]{:S(2)}) async-start(f32[16,4,16,256]{3,2,1,0:T(8,128)} %get-tuple-element.24), calls=%async_computation.3 | async-start | bytes 2097152 | tf_op jit(solution)/shard_map/all_to_all | solution.py:443
  169.2 1.0 copy-start.7

commit v10 on v9

--- a/solution.py
+++ b/solution.py
@@ -39,6 +39,22 @@
         )
 
     return product(a[0], b[1]) + product(a[1], b[0]) + product(a[0], b[0])
+
+
+def cut(parts, rows, lanes):
+    return parts[0][rows, lanes], parts[1][rows, lanes]
+
+
+def inverse_times(inv, b):
+    near, far, every = slice(0, WIDE), slice(WIDE, PANEL), slice(None)
+    top = contract_split(cut(inv, near, near), cut(b, near, every), (1, 0))
+    return jnp.concatenate([top, contract_split(cut(inv, far, every), b, (1, 0))], axis=0)
+
+
+def times_inverse_t(a, inv):
+    near, far, every = slice(0, WIDE), slice(WIDE, PANEL), slice(None)
+    left = contract_split(cut(a, every, near), cut(inv, near, near), (1, 1))
+    return jnp.concatenate([left, contract_split(a, cut(inv, far, every), (1, 1))], axis=1)
 
 
 def spread_kernel(where_ref, map_ref, child_ref, out_ref):
@@ -391,12 +407,12 @@
         copy.wait()
     inv0, inv1, x01 = split(inv0_ref[...]), split(inv1_ref[...]), split(x01_ref[...])
     r0 = split(rows_ref[:, :PANEL])
-    c0 = contract_split(inv0, split(cols0_ref[...].reshape(PANEL, WIDE)), (1, 0))
+    c0 = inverse_times(inv0, split(cols0_ref[...].reshape(PANEL, WIDE)))
     cols0_ref[...] = c0.reshape(cols0_ref.shape)
     c0 = split(c0)
-    r1 = split(contract_split(split(rows_ref[:, PANEL:]), inv1, (1, 1)))
+    r1 = split(times_inverse_t(split(rows_ref[:, PANEL:]), inv1))
     c1 = split(cols1_ref[...].reshape(PANEL, WIDE) - contract_split(x01, c0, (0, 0)))
-    c1 = contract_split(inv1, c1, (1, 0))
+    c1 = inverse_times(inv1, c1)
     cols1_ref[...] = c1.reshape(cols1_ref.shape)
     update = contract_split(r0, c0, (1, 0)) + contract_split(r1, split(c1), (1, 0))
     live = (shard >= ROWS).astype(jnp.float32)

time: 182 us -> 182 us (level)
  no operation moved by 1% of the time
where the time goes in v10:
time: 182 us; the launch traced here: 179 us
  starting transfers between devices  83.2 us (46%)
  Pallas kernels  74.2 us (41%)
  waiting for transfers between devices  17.4 us (10%)
  local copies, waits for them, and re-layouts  2.72 us (1%)
    all_to_all x4, starting transfers between devices, exchange(): return lax.all_to_all(x, axis, split_axis=0, concat_axis=0, tiled=True)  38.6 us
    pallas_call x1, Pallas kernels, second_factor(): pl.pallas_call(second_kernel, out_shape=(shape, shape, jax.ShapeDtypeStru...  27.4 us
    pallas_call x1, Pallas kernels, first_factor(): pl.pallas_call(first_kernel, out_shape=jax.ShapeDtypeStruct((PANEL, PANEL...  24.4 us
    ppermute x6, starting transfers between devices, from_first(): got = lax.ppermute(x, 'sub', pairs)  22.9 us
    ppermute x6, starting transfers between devices, swap(): return lax.ppermute(x, axis, [(i, i ^ bit) for i in range(ROWS)])  21.7 us
    pallas_call x5, Pallas kernels, call(): pl.pallas_call(kernel, out_shape=out_shape, in_specs=[SMEM, SMEM] + [big]...  13.8 us
    all_to_all x4, waiting for transfers between devices, exchange(): return lax.all_to_all(x, axis, split_axis=0, concat_axis=0, tiled=True)  8.99 us
    pallas_call x1, Pallas kernels, finish(): pl.pallas_call(finish_kernel, out_shape=FRONT, in_specs=[SMEM] + [HBM] *...  8.55 us
  transfers between devices with their start and end apart: 16, of which 5 were waited for; matrix products, arithmetic and copies ran while one was open for 1% of the time, Pallas kernels for 34%

profile of v10, /device:TPU:1, one launch (start us, length us, event | category | flops | bytes accessed | tf_op | source)
XLA Modules:
  0.0 178.9 jit_solution(17930616863565106402)
XLA Ops:
  0.6 3.1 %spread_low.1 = f32[8,8,16,128]{3,2,1,0:T(8,128)} custom-call(s32[4]{0:T(128)} %pad_add_fusion.where_ref, s32[2,256]{1,0:T(2,128)} %map_ref.9, f32[16,4096]{1,0:T(8,128)} %child_ref), custom_call_target="tpu_custom_call" | custom-call | tf_op jit(solution)/shard_map/spread_low/pallas_call | solution.py:160
  3.7 12.9 %all-to-all-start = ((f32[32,2,16,128]{3,2,1,0:T(8,128)}), f32[32,2,16,128]{3,2,1,0:T(8,128)S(1)}, u32[]{:S(2)}, u32[]{:S(2)}) async-start(f32[32,2,16,128]{3,2,1,0:T(8,128)} %bitcast.20), calls=%async_computation | async-start | bytes 1048576 | tf_op jit(solution)/shard_map/all_to_all | solution.py:459
  17.4 7.2 %collective-permute-start = (f32[4,16,256]{2,1,0:T(8,128)S(1)}, f32[4,16,256]{2,1,0:T(8,128)S(1)}, u32[]{:S(2)}, u32[]{:S(2)}) collective-permute-start(f32[4,16,256]{2,1,0:T(8,128)S(1)} %bitcast.23), channel_id=1, source_target_pairs={{0,256},{1,257},{2,258},{3,259},{4,260},{5,261},{6,262},{7,263},{8... | collective-permute-start | bytes 196616 | tf_op jit(solution)/shard_map/ppermute | solution.py:470
  24.6 3.7 %collective-permute-done = f32[4,16,256]{2,1,0:T(8,128)S(1)} collective-permute-done((f32[4,16,256]{2,1,0:T(8,128)S(1)}, f32[4,16,256]{2,1,0:T(8,128)S(1)}, u32[]{:S(2)}, u32[]{:S(2)}) %collective-permute-start) | collective-permute-done | bytes 65568 | tf_op jit(solution)/shard_map/ppermute | solution.py:470
  33.8 2.0 %place_top.1.top_ref = f32[16,4,16,256]{3,2,1,0:T(8,128)} custom-call(s32[4]{0:T(128)S(1)} %copy-done.5, s32[2,256]{1,0:T(2,128)S(1)} %copy-done.4, f32[32,2,16,128]{3,2,1,0:T(8,128)S(1)} %all-to-all-done.received_ref, f32[4,16,256]{2,1,0:T(8,128)S(1)} %broadcast_select_fusion.5.parent_ref), custom_call_target="tpu_custom_call" | custom-call | tf_op jit(solution)/shard_map/place_top/pallas_call | solution.py:160
  35.7 9.1 %all-to-all-start.1 = ((f32[16,4,16,256]{3,2,1,0:T(8,128)}), f32[16,4,16,256]{3,2,1,0:T(8,128)S(1)}, u32[]{:S(2)}, u32[]{:S(2)}) async-start(f32[16,4,16,256]{3,2,1,0:T(8,128)} %place_top.1.top_ref), calls=%async_computation.1 | async-start | bytes 2097152 | tf_op jit(solution)/shard_map/all_to_all | solution.py:459
  44.9 8.2 %collective-permute-start.6 = (f32[28,16,256]{2,1,0:T(8,128)S(1)}, f32[28,16,256]{2,1,0:T(8,128)S(1)}, u32[]{:S(2)}, u32[]{:S(2)}) collective-permute-start(f32[28,16,256]{2,1,0:T(8,128)S(1)} %bitcast.21), channel_id=1, source_target_pairs={{0,256},{1,257},{2,258},{3,259},{4,260},{5,261},{6,262},{7,263},{8... | collective-permute-start | bytes 1376264 | tf_op jit(solution)/shard_map/ppermute | solution.py:470
  53.1 5.2 %spread.1 = f32[64,16,128]{2,1,0:T(8,128)} custom-call(s32[4]{0:T(128)S(1)} %copy-done.5, s32[2,256]{1,0:T(2,128)S(1)} %copy-done.4, f32[16,4096]{1,0:T(8,128)S(1)} %copy-done.2), custom_call_target="tpu_custom_call" | custom-call | tf_op jit(solution)/shard_map/spread/pallas_call | solution.py:160
  58.3 2.1 %collective-permute-done.6 = f32[28,16,256]{2,1,0:T(8,128)S(1)} collective-permute-done((f32[28,16,256]{2,1,0:T(8,128)S(1)}, f32[28,16,256]{2,1,0:T(8,128)S(1)}, u32[]{:S(2)}, u32[]{:S(2)}) %collective-permute-start.6) | collective-permute-done | bytes 458784 | tf_op jit(solution)/shard_map/ppermute | solution.py:470
  61.8 9.0 %all-to-all-done.1.pivots_ref = f32[16,4,16,256]{3,2,1,0:T(8,128)S(1)} async-done(((f32[16,4,16,256]{3,2,1,0:T(8,128)}), f32[16,4,16,256]{3,2,1,0:T(8,128)S(1)}, u32[]{:S(2)}, u32[]{:S(2)}) %all-to-all-start.1) | async-done | bytes 1048608 | tf_op jit(solution)/shard_map/all_to_all | solution.py:459
  71.6 2.5 %collective-permute-start.4 = (f32[512,256]{1,0:T(8,128)}, f32[512,256]{1,0:T(8,128)}, u32[]{:S(2)}, u32[]{:S(2)}) collective-permute-start(f32[512,256]{1,0:T(8,128)} %bitcast.6.own.refs_0_), channel_id=1, source_target_pairs={{0,32},{16,48},{32,0},{48,16},{1,33},{17,49},{33,1},{49,17},{2,34}... | collective-permute-start | bytes 1572872 | tf_op jit(solution)/shard_map/ppermute | solution.py:449
  74.2 3.5 %collective-permute-start.8 = (f32[28,16,256]{2,1,0:T(8,128)S(1)}, f32[28,16,256]{2,1,0:T(8,128)S(1)}, u32[]{:S(2)}, u32[]{:S(2)}) collective-permute-start(f32[28,16,256]{2,1,0:T(8,128)S(1)} %broadcast_select_fusion.1), channel_id=1, source_target_pairs={{0,64},{128,192},{256,320},{384,448},{1,65},{129,193},{257,321},{3... | collective-permute-start | bytes 1376264 | tf_op jit(solution)/shard_map/ppermute | solution.py:470
  77.7 7.4 %collective-permute-start.3 = (f32[512,256]{1,0:T(8,128)}, f32[512,256]{1,0:T(8,128)}, u32[]{:S(2)}, u32[]{:S(2)}) collective-permute-start(f32[512,256]{1,0:T(8,128)} %bitcast.6.own.refs_0_), channel_id=1, source_target_pairs={{0,16},{16,0},{32,48},{48,32},{1,17},{17,1},{33,49},{49,33},{2,18}... | collective-permute-start | bytes 1572872 | tf_op jit(solution)/shard_map/ppermute | solution.py:449
  85.1 4.9 %collective-permute-start.5 = (f32[512,256]{1,0:T(8,128)}, f32[512,256]{1,0:T(8,128)}, u32[]{:S(2)}, u32[]{:S(2)}) collective-permute-start(f32[512,256]{1,0:T(8,128)} %collective-permute-done.4.across.refs_2_), channel_id=1, source_target_pairs={{0,16},{16,0},{32,48},{48,32},{1,17},{17,1},{33,49},{49,33},{2,18}... | collective-permute-start | bytes 1572872 | tf_op jit(solution)/shard_map/ppermute | solution.py:449
  90.1 1.6 place_rest.1
  91.7 2.5 %collective-permute-start.10 = (f32[1024,256]{1,0:T(8,128)S(1)}, f32[1024,256]{1,0:T(8,128)}, u32[]{:S(2)}, u32[]{:S(2)}) collective-permute-start(f32[1024,256]{1,0:T(8,128)S(1)} %bitcast.16), channel_id=1, source_target_pairs={{0,32},{16,48},{32,0},{48,16},{1,33},{17,49},{33,1},{49,17},{2,34}... | collective-permute-start | bytes 3145736 | tf_op jit(solution)/shard_map/ppermute | solution.py:449
  94.2 2.2 %collective-permute-start.9 = (f32[1024,256]{1,0:T(8,128)S(1)}, f32[1024,256]{1,0:T(8,128)}, u32[]{:S(2)}, u32[]{:S(2)}) collective-permute-start(f32[1024,256]{1,0:T(8,128)S(1)} %bitcast.17), channel_id=1, source_target_pairs={{0,16},{16,0},{32,48},{48,32},{1,17},{17,1},{33,49},{49,33},{2,18}... | collective-permute-start | bytes 3145736 | tf_op jit(solution)/shard_map/ppermute | solution.py:449
  96.5 10.0 %all-to-all-start.2 = ((f32[32,2,16,128]{3,2,1,0:T(8,128)}), f32[32,2,16,128]{3,2,1,0:T(8,128)S(1)}, u32[]{:S(2)}, u32[]{:S(2)}) async-start(f32[32,2,16,128]{3,2,1,0:T(8,128)} %bitcast.9), calls=%async_computation.2 | async-start | bytes 1048576 | tf_op jit(solution)/shard_map/all_to_all | solution.py:459
  106.5 24.4 %first_factor.1.inv_hbm.inv0_hbm = f32[512,512]{1,0:T(8,128)} custom-call(s32[4]{0:T(128)} %pad_add_fusion.where_ref, f32[512,256]{1,0:T(8,128)} %bitcast.6.own.refs_0_, f32[512,256]{1,0:T(8,128)} %collective-permute-done.3.core.refs_1_, f32[512,256]{1,0:T(8,128)} %collective-permute-done.4.across.refs_2_, f32[512,256]{1,0:T(8,128)} %collective-permute-done.5.both.refs_3_), custom_call_target="tpu_custom_call" | custom-call | flops 60000002048 | bytes 4194304 | tf_op jit(solution)/shard_map/first_factor/pallas_call | solution.py:293
  130.9 2.1 %collective-permute-start.11 = (f32[1024,256]{1,0:T(8,128)}, f32[1024,256]{1,0:T(8,128)}, u32[]{:S(2)}, u32[]{:S(2)}) collective-permute-start(f32[1024,256]{1,0:T(8,128)} %collective-permute-done.10.refs_6_), channel_id=1, source_target_pairs={{0,16},{16,0},{32,48},{48,32},{1,17},{17,1},{33,49},{49,33},{2,18}... | collective-permute-start | bytes 3145736 | tf_op jit(solution)/shard_map/ppermute | solution.py:449
  133.1 2.0 %place.1 = (f32[32,16,256]{2,1,0:T(8,128)S(1)}, f32[16,4,16,256]{3,2,1,0:T(8,128)}) custom-call(s32[4]{0:T(128)S(1)} %copy-done.6, s32[2,256]{1,0:T(2,128)S(1)} %copy-done.4, f32[32,2,16,128]{3,2,1,0:T(8,128)S(1)} %all-to-all-done.2.received_ref, f32[32,16,256]{2,1,0:T(8,128)S(1)} %bitcast.15), custom_call_target="tpu_custom_call" | custom-call | tf_op jit(solution)/shard_map/place/pallas_call | solution.py:160
  135.1 6.7 %all-to-all-start.3 = ((f32[16,4,16,256]{3,2,1,0:T(8,128)}), f32[16,4,16,256]{3,2,1,0:T(8,128)S(1)}, u32[]{:S(2)}, u32[]{:S(2)}) async-start(f32[16,4,16,256]{3,2,1,0:T(8,128)} %get-tuple-element.24), calls=%async_computation.3 | async-start | bytes 2097152 | tf_op jit(solution)/shard_map/all_to_all | solution.py:459
  141.7 27.4 %second_factor.1 = (f32[512,512]{1,0:T(8,128)}, f32[512,512]{1,0:T(8,128)}, f32[512,1024]{1,0:T(8,128)}) custom-call(s32[4]{0:T(128)} %pad_add_fusion.where_ref, f32[512,512]{1,0:T(8,128)} %first_factor.1.inv_hbm.inv0_hbm, f32[512,256]{1,0:T(8,128)} %bitcast.6.own.refs_0_, f32[512,256]{1,0:T(8,128)} %collective-permute-done.3.core.refs_1_, ...), custom_call_target="tpu_custom_call" | custom-call | flops 60000002048 | bytes 8388608 | tf_op jit(solution)/shard_map/second_factor/pallas_call | solution.py:367
  170.2 8.6 %finish.1 = f32[32,16,256]{2,1,0:T(8,128)} custom-call(s32[4]{0:T(128)} %pad_add_fusion.where_ref, f32[512,512]{1,0:T(8,128)} %first_factor.1.inv_hbm.inv0_hbm, f32[512,512]{1,0:T(8,128)} %get-tuple-element.21.inv1_hbm, f32[512,512]{1,0:T(8,128)} %get-tuple-element.22.x01_hbm, f32[16,64,256]{2,1,0:T(8,128)} %bitcast.19, ...), custom_call_target="tpu_custom_call" | custom-call | tf_op jit(solution)/shard_map/finish/pallas_call | solution.py:430
  (42 shorter events, 10.2 us)
Async XLA Ops:
  0.0 33.8 %copy-start.4 = (s32[2,256]{1,0:T(2,128)S(1)}, s32[2,256]{1,0:T(2,128)}, u32[]{:S(2)}) copy-start(s32[2,256]{1,0:T(2,128)} %map_ref.9) | copy-start | bytes 6148
  0.6 33.2 %copy-start.5 = (s32[4]{0:T(128)S(1)}, s32[4]{0:T(128)}, u32[]{:S(2)}) copy-start(s32[4]{0:T(128)} %pad_add_fusion.where_ref) | copy-start | bytes 52
  3.7 30.1 %all-to-all-start = ((f32[32,2,16,128]{3,2,1,0:T(8,128)}), f32[32,2,16,128]{3,2,1,0:T(8,128)S(1)}, u32[]{:S(2)}, u32[]{:S(2)}) async-start(f32[32,2,16,128]{3,2,1,0:T(8,128)} %bitcast.20), calls=%async_computation | async-start | bytes 1048576 | tf_op jit(solution)/shard_map/all_to_all | solution.py:459
  17.4 10.9 %collective-permute-start = (f32[4,16,256]{2,1,0:T(8,128)S(1)}, f32[4,16,256]{2,1,0:T(8,128)S(1)}, u32[]{:S(2)}, u32[]{:S(2)}) collective-permute-start(f32[4,16,256]{2,1,0:T(8,128)S(1)} %bitcast.23), channel_id=1, source_target_pairs={{0,256},{1,257},{2,258},{3,259},{4,260},{5,261},{6,262},{7,263},{8... | collective-permute-start | bytes 196616 | tf_op jit(solution)/shard_map/ppermute | solution.py:470
  28.3 16.5 %copy-start = (f32[16,1,32,256]{3,2,1,0:T(8,128)S(1)}, f32[16,1,32,256]{3,2,1,0:T(8,128)}, u32[]{:S(2)}) copy-start(f32[16,1,32,256]{3,2,1,0:T(8,128)} %param.3) | copy-start | bytes 1572868
  28.4 2.7 %collective-permute-start.1 = (f32[4,16,256]{2,1,0:T(8,128)S(1)}, f32[4,16,256]{2,1,0:T(8,128)S(1)}, u32[]{:S(2)}, u32[]{:S(2)}) collective-permute-start(f32[4,16,256]{2,1,0:T(8,128)S(1)} %broadcast_select_fusion.3), channel_id=1, source_target_pairs={{0,128},{256,384},{1,129},{257,385},{2,130},{258,386},{3,131},{259... | collective-permute-start | bytes 196616 | tf_op jit(solution)/shard_map/ppermute | solution.py:470
  31.1 2.6 %collective-permute-start.2 = (f32[4,16,256]{2,1,0:T(8,128)S(1)}, f32[4,16,256]{2,1,0:T(8,128)S(1)}, u32[]{:S(2)}, u32[]{:S(2)}) collective-permute-start(f32[4,16,256]{2,1,0:T(8,128)S(1)} %broadcast_select_fusion.4), channel_id=1, source_target_pairs={{0,64},{128,192},{256,320},{384,448},{1,65},{129,193},{257,321},{3... | collective-permute-start | bytes 196616 | tf_op jit(solution)/shard_map/ppermute | solution.py:470
  33.7 19.3 %copy-start.2 = (f32[16,4096]{1,0:T(8,128)S(1)}, f32[16,4096]{1,0:T(8,128)}, u32[]{:S(2)}) copy-start(f32[16,4096]{1,0:T(8,128)} %child_ref) | copy-start | bytes 786436
  35.7 35.0 %all-to-all-start.1 = ((f32[16,4,16,256]{3,2,1,0:T(8,128)}), f32[16,4,16,256]{3,2,1,0:T(8,128)S(1)}, u32[]{:S(2)}, u32[]{:S(2)}) async-start(f32[16,4,16,256]{3,2,1,0:T(8,128)} %place_top.1.top_ref), calls=%async_computation.1 | async-start | bytes 2097152 | tf_op jit(solution)/shard_map/all_to_all | solution.py:459
  44.9 15.5 %collective-permute-start.6 = (f32[28,16,256]{2,1,0:T(8,128)S(1)}, f32[28,16,256]{2,1,0:T(8,128)S(1)}, u32[]{:S(2)}, u32[]{:S(2)}) collective-permute-start(f32[28,16,256]{2,1,0:T(8,128)S(1)} %bitcast.21), channel_id=1, source_target_pairs={{0,256},{1,257},{2,258},{3,259},{4,260},{5,261},{6,262},{7,263},{8... | collective-permute-start | bytes 1376264 | tf_op jit(solution)/shard_map/ppermute | solution.py:470
  60.4 13.7 %collective-permute-start.7 = (f32[28,16,256]{2,1,0:T(8,128)S(1)}, f32[28,16,256]{2,1,0:T(8,128)S(1)}, u32[]{:S(2)}, u32[]{:S(2)}) collective-permute-start(f32[28,16,256]{2,1,0:T(8,128)S(1)} %broadcast_select_fusion), channel_id=1, source_target_pairs={{0,128},{256,384},{1,129},{257,385},{2,130},{258,386},{3,131},{259... | collective-permute-start | bytes 1376264 | tf_op jit(solution)/shard_map/ppermute | solution.py:470
  71.6 13.5 %collective-permute-start.4 = (f32[512,256]{1,0:T(8,128)}, f32[512,256]{1,0:T(8,128)}, u32[]{:S(2)}, u32[]{:S(2)}) collective-permute-start(f32[512,256]{1,0:T(8,128)} %bitcast.6.own.refs_0_), channel_id=1, source_target_pairs={{0,32},{16,48},{32,0},{48,16},{1,33},{17,49},{33,1},{49,17},{2,34}... | collective-permute-start | bytes 1572872 | tf_op jit(solution)/shard_map/ppermute | solution.py:449
  74.2 15.8 %collective-permute-start.8 = (f32[28,16,256]{2,1,0:T(8,128)S(1)}, f32[28,16,256]{2,1,0:T(8,128)S(1)}, u32[]{:S(2)}, u32[]{:S(2)}) collective-permute-start(f32[28,16,256]{2,1,0:T(8,128)S(1)} %broadcast_select_fusion.1), channel_id=1, source_target_pairs={{0,64},{128,192},{256,320},{384,448},{1,65},{129,193},{257,321},{3... | collective-permute-start | bytes 1376264 | tf_op jit(solution)/shard_map/ppermute | solution.py:470
  77.7 28.8 %collective-permute-start.3 = (f32[512,256]{1,0:T(8,128)}, f32[512,256]{1,0:T(8,128)}, u32[]{:S(2)}, u32[]{:S(2)}) collective-permute-start(f32[512,256]{1,0:T(8,128)} %bitcast.6.own.refs_0_), channel_id=1, source_target_pairs={{0,16},{16,0},{32,48},{48,32},{1,17},{17,1},{33,49},{49,33},{2,18}... | collective-permute-start | bytes 1572872 | tf_op jit(solution)/shard_map/ppermute | solution.py:449
  85.1 21.4 %collective-permute-start.5 = (f32[512,256]{1,0:T(8,128)}, f32[512,256]{1,0:T(8,128)}, u32[]{:S(2)}, u32[]{:S(2)}) collective-permute-start(f32[512,256]{1,0:T(8,128)} %collective-permute-done.4.across.refs_2_), channel_id=1, source_target_pairs={{0,16},{16,0},{32,48},{48,32},{1,17},{17,1},{33,49},{49,33},{2,18}... | collective-permute-start | bytes 1572872 | tf_op jit(solution)/shard_map/ppermute | solution.py:449
  91.7 39.2 %copy-start.1 = (f32[64,16,256]{2,1,0:T(8,128)}, f32[64,16,256]{2,1,0:T(8,128)S(1)}, u32[]{:S(2)}) copy-start(f32[64,16,256]{2,1,0:T(8,128)S(1)} %place_rest.1) | copy-start | bytes 3145732
  91.7 39.2 %collective-permute-start.10 = (f32[1024,256]{1,0:T(8,128)S(1)}, f32[1024,256]{1,0:T(8,128)}, u32[]{:S(2)}, u32[]{:S(2)}) collective-permute-start(f32[1024,256]{1,0:T(8,128)S(1)} %bitcast.16), channel_id=1, source_target_pairs={{0,32},{16,48},{32,0},{48,16},{1,33},{17,49},{33,1},{49,17},{2,34}... | collective-permute-start | bytes 3145736 | tf_op jit(solution)/shard_map/ppermute | solution.py:449
  94.2 47.5 %collective-permute-start.9 = (f32[1024,256]{1,0:T(8,128)S(1)}, f32[1024,256]{1,0:T(8,128)}, u32[]{:S(2)}, u32[]{:S(2)}) collective-permute-start(f32[1024,256]{1,0:T(8,128)S(1)} %bitcast.17), channel_id=1, source_target_pairs={{0,16},{16,0},{32,48},{48,32},{1,17},{17,1},{33,49},{49,33},{2,18}... | collective-permute-start | bytes 3145736 | tf_op jit(solution)/shard_map/ppermute | solution.py:449
  96.5 34.4 %all-to-all-start.2 = ((f32[32,2,16,128]{3,2,1,0:T(8,128)}), f32[32,2,16,128]{3,2,1,0:T(8,128)S(1)}, u32[]{:S(2)}, u32[]{:S(2)}) async-start(f32[32,2,16,128]{3,2,1,0:T(8,128)} %bitcast.9), calls=%async_computation.2 | async-start | bytes 1048576 | tf_op jit(solution)/shard_map/all_to_all | solution.py:459
  106.4 26.6 %copy-start.6 = (s32[4]{0:T(128)S(1)}, s32[4]{0:T(128)}, u32[]{:S(2)}) copy-start(s32[4]{0:T(128)} %pad_add_fusion.where_ref) | copy-start | bytes 52
  130.9 10.8 %collective-permute-start.11 = (f32[1024,256]{1,0:T(8,128)}, f32[1024,256]{1,0:T(8,128)}, u32[]{:S(2)}, u32[]{:S(2)}) collective-permute-start(f32[1024,256]{1,0:T(8,128)} %collective-permute-done.10.refs_6_), channel_id=1, source_target_pairs={{0,16},{16,0},{32,48},{48,32},{1,17},{17,1},{33,49},{49,33},{2,18}... | collective-permute-start | bytes 3145736 | tf_op jit(solution)/shard_map/ppermute | solution.py:449
  135.1 34.1 %copy-start.3 = (f32[32,16,256]{2,1,0:T(8,128)}, f32[32,16,256]{2,1,0:T(8,128)S(1)}, u32[]{:S(2)}) copy-start(f32[32,16,256]{2,1,0:T(8,128)S(1)} %get-tuple-element.26.front_hbm) | copy-start | bytes 1572868
  135.1 34.1 %all-to-all-start.3 = ((f32[16,4,16,256]{3,2,1,0:T(8,128)}), f32[16,4,16,256]{3,2,1,0:T(8,128)S(1)}, u32[]{:S(2)}, u32[]{:S(2)}) async-start(f32[16,4,16,256]{3,2,1,0:T(8,128)} %get-tuple-element.24), calls=%async_computation.3 | async-start | bytes 2097152 | tf_op jit(solution)/shard_map/all_to_all | solution.py:459
  169.2 1.0 copy-start.7
